TPU v7x, 32 devices: a whole 2x2x4 slice. The times are simulated.
32 devices in a mesh: seq: 8 (over y, x, core), exp: 4 (over z).
Axes of the slice: x: 2, y: 2, z: 4, core: 2. Of those that a mesh axis runs over, the one named last changes fastest.
Arguments:
- inputs: bfloat16 [4, 1024, 768], P('exp', 'seq'), may hold values from -6 to 6
- encoder: bfloat16 [512, 768], replicated, may hold values from -6 to 6
- lengths: int32 [4, 8], P('exp'), may hold values from 1 to 960, as said below
- buckets: int32 [128], replicated, may hold values from 0 to 31, as said below
- routes: int32 [4, 1024, 1], P('exp', 'seq'), may hold values from 0 to 3
- norm_gains: float32 [3, 768], replicated, may hold values from 0.25 to 1.75
- self_qkv: bfloat16 [768, 2304], replicated, may hold values from -0.21875 to 0.21875
- self_out: bfloat16 [768, 768], replicated, may hold values from -1.75 to 1.75
- cross_q: bfloat16 [768, 768], replicated, may hold values from -0.21875 to 0.21875
- cross_kv: bfloat16 [768, 1536], replicated, may hold values from -0.21875 to 0.21875
- cross_out: bfloat16 [768, 768], replicated, may hold values from -1.75 to 1.75
- rel_bias: float32 [32, 12], replicated, may hold values from -4 to 4
- router: bfloat16 [768, 4], replicated, may hold values from -0.21875 to 0.21875
- expert_in: bfloat16 [4, 768, 3072], P('exp'), may hold values from -0.21875 to 0.21875
- expert_out: bfloat16 [4, 3072, 768], P('exp'), may hold values from -0.4375 to 0.4375
- cotangent: bfloat16 [4, 1024, 768], P('exp', 'seq'), may hold values from -6 to 6
Outputs:
- layer_out: bfloat16 [4, 1024, 768], P('exp', 'seq')
- grad_input: float32 [4, 1024, 768], P('exp', 'seq')
- grad_encoder: float32 [512, 768], P(('seq', 'exp'))
- grad_gains: float32 [3, 768], replicated
- grad_self_qkv: float32 [768, 2304], replicated
- grad_self_out: float32 [768, 768], replicated
- grad_cross_q: float32 [768, 768], replicated
- grad_cross_kv: float32 [768, 1536], replicated
- grad_cross_out: float32 [768, 768], replicated
- grad_rel_bias: float32 [32, 12], replicated
- grad_router: float32 [768, 4], replicated
- grad_expert_in: float32 [4, 768, 3072], P('exp', 'seq')
- grad_expert_out: float32 [4, 3072, 768], P('exp', 'seq')
Inputs may be any that keep to these rules, and one draw needn't show every extreme that they name: In each group the 8 lengths sum to 1024; one of them, at a place drawn from the seed, is 960, and the others sum to 64. buckets[d] = d for d < 16; never falling in d; 31 at d = 127.
All inputs are finite; a program needn't handle non-finite values.
Results may differ from a plain program's by a relative error of at most 0.03.
Values may be sent and summed in bfloat16 or wider, within the bound.
A program may use at most 256 MiB of HBM per device.

v0:
```python
import math

import jax
import jax.numpy as jnp
from jax import lax
from jax.sharding import PartitionSpec as P

H = 12
HD = 64


epsilon = 1e-06
masked_out = -1e30
highest = lax.Precision.HIGHEST


def rms_norm(value, gain):
    return value * lax.rsqrt(jnp.mean(value * value, axis=-1, keepdims=True) + epsilon) * gain


def split_heads(value):
    return value.reshape(value.shape[0], H, HD)


def doc_index(positions, doc_ends):
    return jnp.sum((positions[:, None] >= doc_ends[None, :]).astype(jnp.int32), axis=1)


def band_pick(offset_gap, query_rows, key_rows, table_span):
    band_len = query_rows + key_rows + 1
    column = jnp.arange(band_len, dtype=jnp.int32)
    distance = jnp.clip(offset_gap + query_rows - column, 0, table_span - 1)
    return (distance[:, None] == jnp.arange(table_span, dtype=jnp.int32)[None, :]).astype(
        jnp.float32
    )


def relative_bias(table, offset_gap, query_rows, key_rows):
    head_count = table.shape[0]
    band_len = query_rows + key_rows + 1
    band = jnp.dot(
        table, band_pick(offset_gap, query_rows, key_rows, table.shape[1]).T, precision=highest
    )
    tiled = jnp.broadcast_to(band[:, None, :], (head_count, query_rows, band_len)).reshape(
        head_count, query_rows * band_len
    )
    skewed = tiled[:, : query_rows * (band_len - 1)].reshape(head_count, query_rows, band_len - 1)
    return skewed[:, :, query_rows : query_rows + key_rows]


def table_terms(score_grads, offset_gap, table_span):
    head_count, query_rows, key_rows = score_grads.shape
    band_len = query_rows + key_rows + 1
    placed = jnp.pad(score_grads.astype(jnp.float32), ((0, 0), (0, 0), (query_rows, 0)))
    flat = jnp.pad(
        placed.reshape(head_count, query_rows * (band_len - 1)), ((0, 0), (0, query_rows))
    )
    diagonal_sums = jnp.sum(flat.reshape(head_count, query_rows, band_len), axis=1)
    return jnp.dot(
        diagonal_sums, band_pick(offset_gap, query_rows, key_rows, table_span), precision=highest
    )


def self_scores(queries, query_start, keys_part, key_start, doc_ends, table):
    query_rows = queries.shape[0]
    key_rows = keys_part.shape[0]
    query_pos = query_start + jnp.arange(query_rows, dtype=jnp.int32)
    key_pos = key_start + jnp.arange(key_rows, dtype=jnp.int32)
    offset_gap = query_start - key_start
    raw_scores = (
        jnp.einsum(
            "qhd,khd->hqk",
            split_heads(queries),
            split_heads(keys_part),
            preferred_element_type=jnp.float32,
        )
        * 0.125
    )
    allowed = (key_pos[None, :] <= query_pos[:, None]) & (
        doc_index(key_pos, doc_ends)[None, :] == doc_index(query_pos, doc_ends)[:, None]
    )
    scores = jnp.where(
        allowed[None],
        raw_scores + relative_bias(table, offset_gap, query_rows, key_rows),
        masked_out,
    )
    return (scores, allowed[None], offset_gap)


def over_blocks(step, running, pieces):
    rows_total = pieces[0].shape[0]
    block_rows = math.gcd(rows_total, 512)
    block_count = rows_total // block_rows
    stacked = tuple(
        (member.reshape(block_count, block_rows, *member.shape[1:]) for member in pieces)
    )

    def scan_step(inner_running, block_input):
        block_id, members = block_input
        return (step(inner_running, members, block_id * block_rows), None)

    result, ignored = lax.scan(
        scan_step, running, (jnp.arange(block_count, dtype=jnp.int32), stacked)
    )
    return result


def on_device(
    inputs,
    encoder,
    lengths,
    buckets,
    routes,
    norm_gains,
    self_qkv,
    self_out,
    cross_q,
    cross_kv,
    cross_out,
    rel_bias,
    router,
    expert_in,
    expert_out,
    cotangent,
):
    hidden = inputs[0].astype(jnp.float32)
    rows_dev = hidden.shape[0]
    model_width = hidden.shape[1]
    seq_count = lax.axis_size("seq")
    seq_index = lax.axis_index("seq")
    own_start = seq_index * rows_dev
    doc_ends = jnp.cumsum(lengths[0])
    bucket_pick = (
        buckets[:, None] == jnp.arange(rel_bias.shape[0], dtype=jnp.int32)[None, :]
    ).astype(jnp.float32)
    table = jnp.dot(bucket_pick, rel_bias, precision=highest).T
    normed_one, norm_one_back = jax.vjp(rms_norm, hidden, norm_gains[0])
    normed_one = normed_one.astype(jnp.bfloat16)
    qkv_all = jnp.dot(normed_one, self_qkv, preferred_element_type=jnp.float32).astype(jnp.bfloat16)
    queries = qkv_all[:, :model_width]
    keys_own = qkv_all[:, model_width : 2 * model_width]
    values_own = qkv_all[:, 2 * model_width :]

    def forward_step(running, pieces, key_start):
        top_old, denominator, summed = running
        keys_part, values_part = pieces
        scores, allowed, offset_gap = self_scores(
            queries, own_start, keys_part, key_start, doc_ends, table
        )
        top_new = jnp.maximum(top_old, jnp.max(scores, axis=-1))
        weights_raw = jnp.where(allowed, jnp.exp(scores - top_new[..., None]), 0.0)
        rescale = jnp.exp(top_old - top_new)
        denominator = denominator * rescale + jnp.sum(weights_raw, axis=-1)
        summed = summed * rescale[..., None] + jnp.einsum(
            "hqk,khd->hqd",
            weights_raw.astype(jnp.bfloat16),
            split_heads(values_part),
            preferred_element_type=jnp.float32,
        )
        return (top_new, denominator, summed)

    start_state = (
        jnp.full((H, rows_dev), masked_out, jnp.float32),
        jnp.zeros((H, rows_dev), jnp.float32),
        jnp.zeros((H, rows_dev, HD), jnp.float32),
    )
    top_score, denominator, summed = over_blocks(
        forward_step,
        start_state,
        (
            lax.all_gather(keys_own, "seq", axis=0, tiled=True),
            lax.all_gather(values_own, "seq", axis=0, tiled=True),
        ),
    )
    log_total = top_score + jnp.log(denominator)
    attended_full = (
        (summed / denominator[..., None]).transpose(1, 0, 2).reshape(rows_dev, model_width)
    )
    attended = attended_full.astype(jnp.bfloat16)
    after_self = hidden + jnp.dot(attended, self_out, preferred_element_type=jnp.float32)
    enc_kv = jnp.dot(encoder, cross_kv, preferred_element_type=jnp.float32).astype(jnp.bfloat16)
    cross_keys = split_heads(enc_kv[:, :model_width])
    cross_values = split_heads(enc_kv[:, model_width:])
    normed_two, norm_two_back = jax.vjp(rms_norm, after_self, norm_gains[1])
    normed_two = normed_two.astype(jnp.bfloat16)
    cross_queries = jnp.dot(normed_two, cross_q, preferred_element_type=jnp.float32).astype(
        jnp.bfloat16
    )
    cross_scores = (
        jnp.einsum(
            "qhd,khd->hqk",
            split_heads(cross_queries),
            cross_keys,
            preferred_element_type=jnp.float32,
        )
        * 0.125
    )
    cross_raw = jnp.exp(cross_scores - jnp.max(cross_scores, axis=-1, keepdims=True))
    cross_prob = cross_raw / jnp.sum(cross_raw, axis=-1, keepdims=True)
    cross_prob_low = cross_prob.astype(jnp.bfloat16)
    cross_att = (
        jnp.einsum("hqk,khd->qhd", cross_prob_low, cross_values, preferred_element_type=jnp.float32)
        .reshape(rows_dev, model_width)
        .astype(jnp.bfloat16)
    )
    after_cross = after_self + jnp.dot(cross_att, cross_out, preferred_element_type=jnp.float32)
    normed_three, norm_three_back = jax.vjp(rms_norm, after_cross, norm_gains[2])
    routed_in = normed_three.astype(jnp.bfloat16)
    gates = jax.nn.softmax(jnp.dot(routed_in, router, preferred_element_type=jnp.float32), axis=-1)
    expert_total = router.shape[1]
    local_experts = expert_in.shape[0]
    capacity = 5 * rows_dev // (4 * expert_total)
    route_ids = routes[0, :, 0]
    chosen = route_ids[:, None] == jnp.arange(expert_total, dtype=jnp.int32)[None, :]
    slots = jnp.sum(jnp.where(chosen, jnp.cumsum(chosen.astype(jnp.int32), axis=0), 0), axis=1) - 1
    kept = slots < capacity
    picked_gate = jnp.sum(jnp.where(chosen, gates, 0.0), axis=1)
    gate_used = picked_gate * kept.astype(jnp.float32)
    target = jnp.where(kept, route_ids * capacity + slots, -1)
    dispatch = (
        jnp.arange(expert_total * capacity, dtype=jnp.int32)[:, None] == target[None, :]
    ).astype(jnp.bfloat16)
    outgoing = (
        jnp.dot(dispatch, routed_in, preferred_element_type=jnp.float32)
        .astype(jnp.bfloat16)
        .reshape(expert_total, capacity, model_width)
    )
    arrived = lax.all_to_all(outgoing, "exp", split_axis=0, concat_axis=0, tiled=True).reshape(
        -1, local_experts, capacity, model_width
    )
    inner_pre = jnp.einsum("secd,edf->secf", arrived, expert_in, preferred_element_type=jnp.float32)
    active = jax.nn.gelu(inner_pre, approximate=True).astype(jnp.bfloat16)
    produced = jnp.einsum(
        "secf,efd->secd", active, expert_out, preferred_element_type=jnp.float32
    ).astype(jnp.bfloat16)
    returned = lax.all_to_all(
        produced.reshape(-1, capacity, model_width), "exp", split_axis=0, concat_axis=0, tiled=True
    )
    expert_rows = jnp.dot(
        dispatch.T, returned.reshape(-1, model_width), preferred_element_type=jnp.float32
    )
    layer_out = after_cross + gate_used[:, None] * expert_rows
    upstream = cotangent[0].astype(jnp.float32)
    made_grad = (upstream * gate_used[:, None]).astype(jnp.bfloat16)
    sent_grad = (
        jnp.dot(dispatch, made_grad, preferred_element_type=jnp.float32)
        .astype(jnp.bfloat16)
        .reshape(expert_total, capacity, model_width)
    )
    grad_arrived = lax.all_to_all(
        sent_grad, "exp", split_axis=0, concat_axis=0, tiled=True
    ).reshape(-1, local_experts, capacity, model_width)
    inner_again = jnp.einsum(
        "secd,edf->secf", arrived, expert_in, preferred_element_type=jnp.float32
    )
    active_again, gelu_back = jax.vjp(
        lambda value: jax.nn.gelu(value, approximate=True), inner_again
    )
    grad_out_w = jnp.einsum(
        "secf,secd->efd",
        active_again.astype(jnp.bfloat16),
        grad_arrived,
        preferred_element_type=jnp.float32,
    )
    grad_active = jnp.einsum(
        "secd,efd->secf", grad_arrived, expert_out, preferred_element_type=jnp.float32
    )
    grad_inner = gelu_back(grad_active)[0].astype(jnp.bfloat16)
    grad_in_w = jnp.einsum(
        "secd,secf->edf", arrived, grad_inner, preferred_element_type=jnp.float32
    )
    grad_sent_x = jnp.einsum(
        "secf,edf->secd", grad_inner, expert_in, preferred_element_type=jnp.float32
    ).astype(jnp.bfloat16)
    grad_back = lax.all_to_all(
        grad_sent_x.reshape(-1, capacity, model_width),
        "exp",
        split_axis=0,
        concat_axis=0,
        tiled=True,
    )
    grad_routed = jnp.dot(
        dispatch.T, grad_back.reshape(-1, model_width), preferred_element_type=jnp.float32
    )
    expert_sums = (
        lax.psum_scatter(grad_in_w, "seq", scatter_dimension=1, tiled=True),
        lax.psum_scatter(grad_out_w, "seq", scatter_dimension=1, tiled=True),
    )
    gate_grad = jnp.sum(upstream * expert_rows, axis=1) * kept.astype(jnp.float32)
    logit_grad = gates * (
        jnp.where(chosen, gate_grad[:, None], 0.0) - (picked_gate * gate_grad)[:, None]
    )
    router_grad = jnp.dot(routed_in.astype(jnp.float32).T, logit_grad, precision=highest)
    grad_normed_three = (
        jnp.dot(logit_grad, router.astype(jnp.float32).T, precision=highest) + grad_routed
    )
    grad_after_cross, gain_three = norm_three_back(grad_normed_three)
    grad_after_cross = grad_after_cross + upstream
    cross_branch = grad_after_cross.astype(jnp.bfloat16)
    cross_out_grad = jnp.dot(cross_att.T, cross_branch, preferred_element_type=jnp.float32)
    grad_cross_att = split_heads(
        jnp.dot(cross_branch, cross_out.T, preferred_element_type=jnp.float32).astype(jnp.bfloat16)
    )
    cross_prob_grad = jnp.einsum(
        "qhd,khd->hqk", grad_cross_att, cross_values, preferred_element_type=jnp.float32
    )
    cross_delta = jnp.sum(cross_prob * cross_prob_grad, axis=-1, keepdims=True)
    cross_score_grad = (cross_prob * (cross_prob_grad - cross_delta)).astype(jnp.bfloat16)
    grad_cross_queries = (
        (
            jnp.einsum(
                "hqk,khd->qhd", cross_score_grad, cross_keys, preferred_element_type=jnp.float32
            )
            * 0.125
        )
        .reshape(rows_dev, model_width)
        .astype(jnp.bfloat16)
    )
    grad_enc_keys = (
        jnp.einsum(
            "hqk,qhd->khd",
            cross_score_grad,
            split_heads(cross_queries),
            preferred_element_type=jnp.float32,
        )
        * 0.125
    )
    grad_enc_values = jnp.einsum(
        "hqk,qhd->khd", cross_prob_low, grad_cross_att, preferred_element_type=jnp.float32
    )
    enc_terms = jnp.concatenate(
        [grad_enc_keys.reshape(-1, model_width), grad_enc_values.reshape(-1, model_width)], axis=1
    )
    enc_grad_rows = lax.psum_scatter(
        enc_terms, ("seq", "exp"), scatter_dimension=0, tiled=True
    ).astype(jnp.bfloat16)
    enc_count = enc_grad_rows.shape[0]
    flat_index = seq_index * lax.axis_size("exp") + lax.axis_index("exp")
    own_enc = lax.dynamic_slice_in_dim(encoder, flat_index * enc_count, enc_count, 0)
    grad_encoder = jnp.dot(enc_grad_rows, cross_kv.T, preferred_element_type=jnp.float32)
    pair_grad = jnp.dot(own_enc.T, enc_grad_rows, preferred_element_type=jnp.float32)
    query_w_grad = jnp.dot(normed_two.T, grad_cross_queries, preferred_element_type=jnp.float32)
    grad_normed_two = jnp.dot(grad_cross_queries, cross_q.T, preferred_element_type=jnp.float32)
    grad_after_self, gain_two = norm_two_back(grad_normed_two)
    grad_after_self = grad_after_self + grad_after_cross
    self_branch = grad_after_self.astype(jnp.bfloat16)
    self_out_grad = jnp.dot(attended.T, self_branch, preferred_element_type=jnp.float32)
    grad_attended = jnp.dot(self_branch, self_out.T, preferred_element_type=jnp.float32).astype(
        jnp.bfloat16
    )
    row_delta = jnp.sum(
        split_heads(grad_attended).astype(jnp.float32) * split_heads(attended_full), axis=-1
    ).T
    stats_all = (
        lax.all_gather(log_total.T, "seq", axis=0, tiled=True),
        lax.all_gather(row_delta.T, "seq", axis=0, tiled=True),
    )

    def query_step(running, pieces, query_start):
        kv_grad, query_grads, table_grad = running
        queries_part, grads_part = pieces
        piece_rows = queries_part.shape[0]
        lse_part = lax.dynamic_slice_in_dim(stats_all[0], query_start, piece_rows, 0).T
        delta_part = lax.dynamic_slice_in_dim(stats_all[1], query_start, piece_rows, 0).T
        scores, allowed, offset_gap = self_scores(
            queries_part, query_start, keys_own, own_start, doc_ends, table
        )
        probability = jnp.where(allowed, jnp.exp(scores - lse_part[..., None]), 0.0)
        prob_grad = jnp.einsum(
            "qhd,khd->hqk",
            split_heads(grads_part),
            split_heads(values_own),
            preferred_element_type=jnp.float32,
        )
        score_grad = (probability * (prob_grad - delta_part[..., None])).astype(jnp.bfloat16)
        key_grad = (
            jnp.einsum(
                "hqk,qhd->khd",
                score_grad,
                split_heads(queries_part),
                preferred_element_type=jnp.float32,
            )
            * 0.125
        )
        value_grad = jnp.einsum(
            "hqk,qhd->khd",
            probability.astype(jnp.bfloat16),
            split_heads(grads_part),
            preferred_element_type=jnp.float32,
        )
        kv_grad = kv_grad + jnp.concatenate(
            [key_grad.reshape(-1, model_width), value_grad.reshape(-1, model_width)], axis=1
        )
        table_grad = table_grad + table_terms(score_grad, offset_gap, table.shape[1])
        query_part_grad = jnp.einsum(
            "hqk,khd->qhd", score_grad, split_heads(keys_own), preferred_element_type=jnp.float32
        ).reshape(piece_rows, model_width)
        current = lax.dynamic_slice_in_dim(query_grads, query_start, piece_rows, 0)
        query_grads = lax.dynamic_update_slice_in_dim(
            query_grads, current + query_part_grad, query_start, 0
        )
        return (kv_grad, query_grads, table_grad)

    back_start = (
        jnp.zeros((rows_dev, 2 * model_width), jnp.float32),
        jnp.zeros((seq_count * rows_dev, model_width), jnp.float32),
        jnp.zeros(table.shape, jnp.float32),
    )
    kv_grad, query_buffer, table_grad = over_blocks(
        query_step,
        back_start,
        (
            lax.all_gather(queries, "seq", axis=0, tiled=True),
            lax.all_gather(grad_attended, "seq", axis=0, tiled=True),
        ),
    )
    query_grad = lax.psum_scatter(query_buffer, "seq", scatter_dimension=0, tiled=True)
    qkv_grad = jnp.concatenate(
        [(query_grad * 0.125).astype(jnp.bfloat16), kv_grad.astype(jnp.bfloat16)], axis=1
    )
    qkv_w_grad = jnp.dot(normed_one.T, qkv_grad, preferred_element_type=jnp.float32)
    grad_normed_one = jnp.dot(qkv_grad, self_qkv.T, preferred_element_type=jnp.float32)
    grad_hidden, gain_one = norm_one_back(grad_normed_one)
    grad_input = grad_hidden + grad_after_self
    rel_grad = jnp.dot(bucket_pick.T, table_grad.T, precision=highest)
    summed_grads = lax.psum(
        (
            jnp.stack([gain_one, gain_two, gain_three]),
            qkv_w_grad,
            self_out_grad,
            query_w_grad,
            pair_grad,
            cross_out_grad,
            rel_grad,
            router_grad,
        ),
        ("seq", "exp"),
    )
    return (
        layer_out.astype(jnp.bfloat16)[None],
        grad_input[None],
        grad_encoder,
        summed_grads[0],
        summed_grads[1],
        summed_grads[2],
        summed_grads[3],
        summed_grads[4],
        summed_grads[5],
        summed_grads[6],
        summed_grads[7],
        expert_sums[0],
        expert_sums[1],
    )


def solution(mesh):
    in_specs = (
        P("exp", "seq", None),
        P(),
        P("exp", None),
        P(),
        P("exp", "seq", None),
        P(),
        P(),
        P(),
        P(),
        P(),
        P(),
        P(),
        P(),
        P("exp", None, None),
        P("exp", None, None),
        P("exp", "seq", None),
    )
    out_specs = (
        P("exp", "seq", None),
        P("exp", "seq", None),
        P(("seq", "exp"), None),
        P(),
        P(),
        P(),
        P(),
        P(),
        P(),
        P(),
        P(),
        P("exp", "seq", None),
        P("exp", "seq", None),
    )
    return jax.shard_map(
        on_device, mesh=mesh, in_specs=in_specs, out_specs=out_specs, check_vma=False
    )
```

profile of v0, /device:TPU:0, one launch (start us, length us, event | category | flops | bytes accessed | tf_op | source)
XLA Modules:
  0.0 1183.5 jit_solution(7391977543669907090)
XLA Ops:
  35.2 5.8 all-gather.7.cloned.1.call-done
  40.9 27.6 %all-gather.5.cloned.1.call-done = bf16[1024,768]{1,0:T(8,128)(2,1)} async-done(((bf16[128,768]{1,0:T(8,128)(2,1)}), bf16[1024,768]{1,0:T(8,128)(2,1)}) %all-gather.5.cloned.1.call-update) | async-done | bytes 1572880 | tf_op jit(solution)/shard_map/all_gather | solution.py:171
  69.0 75.6 %while.32 = (s32[]{:T(128)}, f32[12,128]{1,0:T(8,128)S(1)}, f32[12,128]{1,0:T(8,128)S(1)}, f32[12,128,64]{1,2,0:T(8,128)}, s32[2]{0:T(128)}, /*index=5*/s32[]{:T...) while((s32[]{:T(128)}, f32[12,128]{1,0:T(8,128)S(1)}, ...), condition=%wide.region_7.8_spmd.clone, body=%wide.region_2.7_spmd.clone.sunk | while | flops 221603712 | bytes 77731864 | solution.py:102
  85.2 6.5 reshape.555
  123.1 6.5 reshape.555
  152.2 4.6 fusion.134
  162.0 13.8 %all_to_all.20 = bf16[4,40,768]{2,1,0:T(8,128)(2,1)S(1)} all-to-all(bf16[4,40,768]{2,1,0:T(8,128)(2,1)S(1)} %bitcast.322), channel_id=1, replica_groups=mesh['seq'=8,'exp'=4] {'exp'}, dimensions={0} | all-to-all | bytes 491520 | tf_op jit(solution)/shard_map/all_to_all | solution.py:228
  178.1 4.4 fusion.56
  182.6 4.0 all-to-all-start.1
  197.8 10.2 all_to_all.21
  208.0 5.2 fusion.49
  214.2 4.7 fusion.53
  218.9 4.0 all-to-all-start.3
  225.5 4.1 all-to-all-done.3
  251.7 10.2 all_gather.21
  273.3 9.2 all_gather.23
  284.7 351.8 %while.33 = (s32[]{:T(128)}, f32[128,1536]{0,1:T(8,128)}, f32[1024,768]{0,1:T(8,128)}, f32[12,128]{1,0:T(8,128)}, bf16[2,512,768]{2,1,0:T(8,128)(2,1)}, /*index=...) while((s32[]{:T(128)}, f32[128,1536]{0,1:T(8,128)}, ...), condition=%wide.region_26.27_spmd.clone, body=%wide.region_22.26_spmd.clone.sunk | while | flops 543354880 | bytes 343136992 | solution.py:102
  297.4 8.9 broadcast_in_dim.233
  306.3 28.2 %reshape.557 = f32[12,328192]{1,0:T(8,128)} reshape(f32[12,512,641]{2,1,0:T(8,128)} %broadcast_in_dim.233) | data formatting | bytes 31506432 | tf_op jit(solution)/shard_map/while/body/eval_jaxpr/reshape | solution.py:44
  334.5 7.0 slice-done
  341.5 8.9 copy.120
  350.3 12.1 %slice.92 = f32[12,512,640]{2,1,0:T(8,128)} slice(f32[16,512,640]{2,1,0:T(8,128)} %bitcast.287), slice={[0:12], [0:512], [0:640]} | slice | bytes 31457280 | tf_op jit(solution)/shard_map/while/body/eval_jaxpr/reshape | solution.py:47
  374.0 4.0 pad.54
  378.0 8.3 pad.55
  386.3 14.0 %copy.122 = bf16[2,8,512,640]{3,1,2,0:T(8,128)(2,1)} copy(bf16[2,8,512,640]{3,2,1,0:T(8,128)(2,1)} %bitcast.289) | data formatting | bytes 20971520 | tf_op jit(solution)/shard_map/while
  400.3 11.8 pad_convert_fusion.2
  412.1 35.1 %reshape.558 = f32[12,512,641]{2,1,0:T(8,128)} reshape(f32[12,328192]{1,0:T(8,128)} %pad_convert_fusion.2) | data formatting | bytes 31506432 | tf_op jit(solution)/shard_map/while/body/eval_jaxpr/reshape | solution.py:58
  447.2 8.0 reduce_sum.285
  469.7 8.7 broadcast_in_dim.233
  478.4 28.0 %reshape.557 = f32[12,328192]{1,0:T(8,128)} reshape(f32[12,512,641]{2,1,0:T(8,128)} %broadcast_in_dim.233) | data formatting | bytes 31506432 | tf_op jit(solution)/shard_map/while/body/eval_jaxpr/reshape | solution.py:44
  506.3 7.0 slice-done
  513.3 8.9 copy.120
  522.2 12.0 %slice.92 = f32[12,512,640]{2,1,0:T(8,128)} slice(f32[16,512,640]{2,1,0:T(8,128)} %bitcast.287), slice={[0:12], [0:512], [0:640]} | slice | bytes 31457280 | tf_op jit(solution)/shard_map/while/body/eval_jaxpr/reshape | solution.py:47
  550.4 8.3 pad.55
  558.7 14.0 %copy.122 = bf16[2,8,512,640]{3,1,2,0:T(8,128)(2,1)} copy(bf16[2,8,512,640]{3,2,1,0:T(8,128)(2,1)} %bitcast.289) | data formatting | bytes 20971520 | tf_op jit(solution)/shard_map/while
  572.7 11.8 pad_convert_fusion.2
  584.5 35.1 %reshape.558 = f32[12,512,641]{2,1,0:T(8,128)} reshape(f32[12,328192]{1,0:T(8,128)} %pad_convert_fusion.2) | data formatting | bytes 31506432 | tf_op jit(solution)/shard_map/while/body/eval_jaxpr/reshape | solution.py:58
  619.6 8.0 reduce_sum.285
  636.6 7.3 convolution_bitcast_fusion.2
  643.9 6.5 convolution_bitcast_fusion.3
  661.2 4.0 fusion.84
  665.2 16.4 %reduce-scatter.7.cloned.1.call-done = f32[128,768]{0,1:T(8,128)} async-done(((f32[1024,768]{0,1:T(8,128)}), f32[128,768]{0,1:T(8,128)}) %reduce-scatter.7.cloned.1.call-update) | async-done | bytes 393232 | tf_op jit(solution)/shard_map/reduce_scatter | solution.py:417
  683.4 5.3 fusion.77
  699.6 40.4 %all-reduce.2 = (f32[3,768]{1,0:T(4,128)}, f32[32,12]{0,1:T(8,128)}, f32[768,4]{0,1:T(4,128)}) all-reduce(f32[3,768]{1,0:T(4,128)} %pad_maximum_fusion.4, f32[32,12]{0,1:T(8,128)} %fusion.96, f32[768,4]{0,1:T(4,128)S(1)} %fusion.109), channel_id=1, replica_groups=mesh['seq'=8,'exp'=4] {'seq','exp'}, use_global_device_ids=true, to_apply=%region_33.34 | all-reduce | flops 5760 | bytes 46080 | tf_op jit(solution)/shard_map/psum | solution.py:426
  742.8 20.5 %reduce-scatter.11.cloned.1.call-done = f32[1,384,768]{2,1,0:T(8,128)} async-done(((f32[1,3072,768]{2,1,0:T(8,128)}), f32[1,384,768]{2,1,0:T(8,128)}) %reduce-scatter.11.cloned.1.call-update) | async-done | bytes 1179664 | tf_op jit(solution)/shard_map/reduce_scatter | solution.py:287
  763.3 81.0 %reduce-scatter.9.cloned.1.call-done = f32[1,96,3072]{2,1,0:T(8,128)} async-done(((f32[1,768,3072]{2,1,0:T(8,128)}), f32[1,96,3072]{2,1,0:T(8,128)}) %reduce-scatter.9.cloned.1.call-update) | async-done | bytes 1179664 | tf_op jit(solution)/shard_map/reduce_scatter | solution.py:286
  844.3 315.4 %all-reduce.6.cloned.1.call-done = (f32[768,2304]{1,0:T(8,128)}, f32[768,768]{1,0:T(8,128)}, f32[768,768]{1,0:T(8,128)}, f32[768,1536]{1,0:T(8,128)}, f32[768,768]{1,0:T(8,128)}) async-done(((f32[768,2304]{1,0:T(8,128)}, f32[768,768]{1,0:T(8,128)}, f32[768,768]{1,0:T(8,128)}, f32[768,1536]{1,0:T(8,128)}, f32[768,768]{1,0:T(8,128)}), (f32[768,2304]{1,0:T(8,128)}, f32[768,768]{1,0:T(8,128)}, ...) | async-done | bytes 18874384 | tf_op jit(solution)/shard_map/psum | solution.py:426
  1159.7 6.6 copy.153
  (359 shorter events, 246.3 us)
Async XLA Ops:
  7.2 33.8 %all-gather.7.cloned.1.call-start = ((), (), s32[]{:S(2)}) async-start(), calls=%async_computation.9 | async-start | bytes 1769472 | tf_op jit(solution)/shard_map/all_gather | solution.py:172
  8.5 3.9 copy-start.57
  12.4 56.2 %all-gather.5.cloned.1.call-start = ((), (), s32[]{:S(2)}) async-start(), calls=%async_computation.8 | async-start | bytes 1769472 | tf_op jit(solution)/shard_map/all_gather | solution.py:171
  100.8 3.2 copy-start.4
  138.7 3.2 copy-start.4
  144.7 4.7 copy-start.27
  144.7 4.7 copy-start.49
  156.8 19.1 %slice-start.2 = ((s8[4718592]{0:T(1024)(128)(4,1)}), s8[4194304]{0:T(1024)(128)(4,1)S(1)}, s32[]{:S(2)}) async-start(s8[4718592]{0:T(1024)(128)(4,1)} %bitcast.300), calls=%async_computation.19 | async-start | bytes 8388608
  156.8 3.0 copy-start.24
  156.8 4.2 copy-start.52
  156.8 19.1 %slice-start.3 = ((s8[4718592]{0:T(1024)(128)(4,1)}), s8[524288]{0:T(1024)(128)(4,1)S(1)}, s32[]{:S(2)}) async-start(s8[4718592]{0:T(1024)(128)(4,1)} %bitcast.300), calls=%async_computation.20 | async-start | bytes 1048576
  182.6 10.7 all-to-all-start.1
  208.0 5.2 copy-start.45
  218.9 10.7 all-to-all-start.3
  222.9 59.7 %all-gather.9.cloned.1.call-start = ((), (), s32[]{:S(2)}) async-start(), calls=%async_computation.10 | async-start | bytes 1769472 | tf_op jit(solution)/shard_map/all_gather | solution.py:413
  223.6 59.0 %all-gather.11.cloned.1.call-start = ((), (), s32[]{:S(2)}) async-start(), calls=%async_computation.11 | async-start | bytes 1769472 | tf_op jit(solution)/shard_map/all_gather | solution.py:414
  229.6 5.8 copy-start.25
  238.4 3.1 copy-start.12
  238.4 3.1 copy-start.54
  242.7 3.2 copy-start.7
  242.7 3.2 copy-start.68
  242.7 3.2 copy-start.22
  243.4 3.5 copy-start.26
  248.1 411.2 %reduce-scatter.13.cloned.1.call-start = ((), (), s32[]{:S(2)}) async-start(), calls=%async_computation.15 | async-start | bytes 3244032
  251.7 14.0 %copy-start.55 = (f32[12,128]{1,0:T(8,128)S(1)}, f32[12,128]{1,0:T(8,128)}, u32[]{:S(2)}) copy-start(f32[12,128]{1,0:T(8,128)} %get-tuple-element.525) | copy-start | bytes 18436
  282.5 399.2 %reduce-scatter.7.cloned.1.call-start = ((), (), s32[]{:S(2)}) async-start(), calls=%async_computation.12 | async-start | bytes 3538944 | tf_op jit(solution)/shard_map/reduce_scatter | solution.py:417
  334.5 7.0 slice-start
  362.5 3.8 copy-start.1
  506.3 7.0 slice-start
  534.1 3.7 copy-start.1
  636.5 126.8 %reduce-scatter.11.cloned.1.call-start = ((), (), s32[]{:S(2)}) async-start(), calls=%async_computation.14 | async-start | bytes 10616832 | tf_op jit(solution)/shard_map/reduce_scatter | solution.py:287
  643.9 200.4 %reduce-scatter.9.cloned.1.call-start = ((), (), s32[]{:S(2)}) async-start(), calls=%async_computation.13 | async-start | bytes 10616832 | tf_op jit(solution)/shard_map/reduce_scatter | solution.py:286
  650.4 509.3 %all-reduce.6.cloned.1.call-start = ((), (), s32[]{:S(2)}) async-start(), calls=%async_computation.16 | async-start | bytes 37748736 | tf_op jit(solution)/shard_map/psum | solution.py:426
  650.5 3.1 copy-start.19
  650.5 3.1 copy-start.36
  650.5 4.9 copy-start.11
  650.5 4.9 copy-start.38
  650.5 4.9 copy-start.51
  650.5 4.9 copy-start.62
  661.2 22.2 %copy-start.47 = (f32[768]{0:T(1024)S(1)}, f32[768]{0:T(1024)}, u32[]{:S(2)}) copy-start(f32[768]{0:T(1024)} %copy-done.46) | copy-start | bytes 9220
  661.2 22.2 %copy-start.58 = (f32[128]{0:T(128)S(1)}, f32[128]{0:T(128)}, u32[]{:S(2)}) copy-start(f32[128]{0:T(128)} %copy-done.57) | copy-start | bytes 1540
  688.7 7.7 copy-start.17
  688.7 7.7 copy-start.39
  688.7 7.7 copy-start.44
  688.7 7.7 copy-start.59
  1159.7 6.6 copy-start.33
  1168.8 3.2 copy-start.23
  1172.0 3.4 copy-start.31
  (48 other events, 70.7 us)
Sparse Core Ops, SparseCore 0:
  12.5 28.3 all-gather.6
  42.8 25.6 all-gather.4
  225.6 26.1 all-gather.8
  254.1 25.7 all-gather.10
  285.2 101.5 reduce-scatter.12
  636.6 44.9 reduce-scatter.6
  686.2 77.0 reduce-scatter.10
  767.8 76.4 reduce-scatter.8
  853.0 306.6 all-reduce.5
where the time goes:
time: 1200 us; the launch traced here: 1180 us
  waiting for transfers between devices  476 us (40%)
  local copies, waits for them, and re-layouts  388 us (32%)
  matrix products  122 us (10%)
  blocking collectives  83.8 us (7%)
  other arithmetic  80.4 us (7%)
  between operations  14.7 us (1%)
    psum x1, waiting for transfers between devices, on_device(): lax.psum((jnp.stack([gain_one, gain_two, gain_three]), qkv_w_grad, self_o...  315 us
    reduce_scatter x1, waiting for transfers between devices, on_device(): lax.psum_scatter(grad_in_w, 'seq', scatter_dimension=1, tiled=True)  81 us
    while x48, local copies, waits for them, and re-layouts  75.3 us
    reshape x2, local copies, waits for them, and re-layouts, table_terms(): flat.reshape(head_count, query_rows, band_len)  70.2 us
    reshape x4, local copies, waits for them, and re-layouts, relative_bias(): jnp.broadcast_to(band[:, None, :], (head_count, query_rows, band_len))  69.1 us
    psum x1, blocking collectives, on_device(): lax.psum((jnp.stack([gain_one, gain_two, gain_three]), qkv_w_grad, self_o...  40.4 us
    unnamed x136, local copies, waits for them, and re-layouts  38.3 us
    dynamic_slice x16, local copies, waits for them, and re-layouts, over_blocks(): lax.scan(scan_step, running, (jnp.arange(block_count, dtype=jnp.int32), s...  32.3 us
  transfers between devices with their start and end apart: 11, of which 8 were waited for; matrix products, arithmetic and copies ran while one was open for 37% of the time, Pallas kernels for 0%

commit v1 on v0

--- a/solution.py
+++ b/solution.py
@@ -1,8 +1,11 @@
+import functools
 import math
 
 import jax
 import jax.numpy as jnp
 from jax import lax
+from jax.experimental import pallas as pl
+from jax.experimental.pallas import tpu as pltpu
 from jax.sharding import PartitionSpec as P
 
 H = 12
@@ -105,7 +108,7 @@
     return result
 
 
-def on_device(
+def streamed(
     inputs,
     encoder,
     lengths,
@@ -453,6 +456,357 @@
     )
 
 
+F32 = jnp.float32
+BF16 = jnp.bfloat16
+MESH = pl.DeviceIdType.MESH
+ANY = pl.BlockSpec(memory_space=pl.ANY)
+VMEM = pl.BlockSpec(memory_space=pltpu.VMEM)
+SMEM = pl.BlockSpec(memory_space=pltpu.SMEM)
+LANES = 128
+
+
+def nn(a, b):
+    return lax.dot_general(a, b, (((1,), (0,)), ((), ())), preferred_element_type=F32)
+
+
+def nt(a, b):
+    return lax.dot_general(a, b, (((1,), (1,)), ((), ())), preferred_element_type=F32)
+
+
+def tn(a, b):
+    return lax.dot_general(a, b, (((0,), (0,)), ((), ())), preferred_element_type=F32)
+
+
+def rms_scale(a):
+    return lax.rsqrt(jnp.mean(a * a, axis=-1, keepdims=True) + epsilon)
+
+
+def pair_lanes(p):
+    return pl.ds(pl.multiple_of(p * LANES, LANES), LANES)
+
+
+def head_stack(pair):
+    lane = lax.broadcasted_iota(jnp.int32, pair.shape, 1)
+    zero = jnp.zeros_like(pair)
+    return jnp.concatenate([jnp.where(lane < HD, pair, zero), jnp.where(lane < HD, zero, pair)], axis=0)
+
+
+def head_unstack(both, rows):
+    feature = lax.broadcasted_iota(jnp.int32, (both.shape[0], rows), 0)
+    return jnp.where(feature < HD, both[:, :rows], both[:, rows:]).T
+
+
+def seq_peers(seq_index, chips):
+    core = lax.rem(seq_index, 2)
+    chip = lax.div(seq_index, 2)
+    partner = seq_index + 1 - 2 * core
+    others = [lax.rem(chip + d, chips) * 2 + core for d in range(1, chips)]
+    sources = [lax.rem(chip - d + chips, chips) * 2 + core for d in range(1, chips)]
+    return core, chip, partner, others, sources
+
+
+def enter(devices):
+    barrier = pltpu.get_barrier_semaphore()
+    for device in devices:
+        pl.semaphore_signal(barrier, inc=1, device_id=device, device_id_type=MESH)
+    pl.semaphore_wait(barrier, len(devices))
+
+
+def remote(src, dst, send_sem, recv_sem, device):
+    return pltpu.make_async_remote_copy(
+        src_ref=src, dst_ref=dst, send_sem=send_sem, recv_sem=recv_sem, device_id=device, device_id_type=MESH
+    )
+
+
+def forward_kernel(
+    seq_count, capacity, stride,
+    x_ref, encoder_hbm, lengths_ref, buckets_ref, routes_ref, gains_ref, qkv_hbm, self_out_hbm, cross_q_hbm,
+    cross_kv_hbm, cross_out_hbm, rel_ref, router_ref, g_ref,
+    n1_hbm, kv_hbm, p_hbm, pc_hbm, ekv_hbm, q_ref, o_ref, n2_ref, qc_ref, oc_ref, x3_ref, r1_ref, r2_ref, gates_ref,
+    place_ref, xs_ref, dms_ref,
+    n1_all, kv_all, prob, cross_prob, ekv, scores, mask, w_qkv, w_self, w_cq, w_ckv, w_co, enc, table_ref,
+    load_sem, store_sem, send_sem, recv_sem,
+):
+    chips = seq_count // 2
+    rows, width = x_ref.shape
+    span = seq_count * rows
+    pairs = width // LANES
+    me = lax.axis_index("seq")
+    core, chip, partner, others, sources = seq_peers(me, chips)
+
+    loads = [
+        pltpu.make_async_copy(src, dst, load_sem.at[i])
+        for i, (src, dst) in enumerate(
+            [(qkv_hbm, w_qkv), (cross_kv_hbm, w_ckv), (encoder_hbm, enc), (self_out_hbm, w_self), (cross_q_hbm, w_cq),
+             (cross_out_hbm, w_co)]
+        )
+    ]
+    for load in loads:
+        load.start()
+    x = x_ref[...].astype(F32)
+    n1_all[me] = (x * rms_scale(x) * gains_ref[0:1, :]).astype(BF16)
+    enter([{"seq": partner}] + [{"seq": other} for other in others])
+    own = remote(n1_all.at[me], n1_all.at[me], send_sem.at[0], recv_sem.at[0], {"seq": partner})
+    direct = [
+        remote(n1_all.at[me], n1_all.at[me], send_sem.at[d], recv_sem.at[d], {"seq": others[d - 1]})
+        for d in range(1, chips)
+    ]
+    own.start()
+    for copy in direct:
+        copy.start()
+
+    loads[0].wait()
+    q = nn(n1_all[me], w_qkv[:, :width]).astype(BF16)
+    q_ref[...] = q * jnp.asarray(0.125, BF16)
+    loads[1].wait()
+    loads[2].wait()
+    ekv[...] = nn(enc[...], w_ckv[...]).astype(BF16)
+    store_ekv = pltpu.make_async_copy(ekv, ekv_hbm, store_sem.at[0])
+    store_ekv.start()
+    pick = (buckets_ref[...] == lax.broadcasted_iota(jnp.int32, (rel_ref.shape[0], LANES), 0)).astype(F32)
+    table = lax.dot_general(
+        rel_ref[...], pick, (((0,), (0,)), ((), ())), precision=highest, preferred_element_type=F32
+    )
+    table = table - table[:, LANES - 1 :]
+    table_ref[...] = jnp.concatenate([jnp.zeros_like(table), table], axis=1)
+    query_pos = me * rows + lax.broadcasted_iota(jnp.int32, (1, rows), 1)
+    start = jnp.zeros((1, rows), jnp.int32)
+    end = jnp.int32(0)
+    for i in range(lengths_ref.shape[1]):
+        end = end + lengths_ref[0, i]
+        start = jnp.where(end <= query_pos, end, start)
+    key_pos = lax.broadcasted_iota(jnp.int32, (span, rows), 0)
+    seen = jnp.where((key_pos >= start) & (key_pos <= query_pos), 0.0, masked_out)
+    mask[...] = jnp.concatenate([seen, seen], axis=1)
+
+    forwards = []
+    for d in range(1, chips):
+        direct[d - 1].wait_recv()
+        block = n1_all.at[sources[d - 1]]
+        forward = remote(
+            block, block, send_sem.at[chips - 1 + d], recv_sem.at[chips - 1 + d], {"seq": partner}
+        )
+        forward.start()
+        forwards.append(forward)
+    own.wait_recv()
+    for forward in forwards:
+        forward.wait_recv()
+    store_n1 = pltpu.make_async_copy(n1_all, n1_hbm, store_sem.at[1])
+    store_n1.start()
+
+    @pl.loop(0, chips)
+    def _(c):
+        part = n1_all[pl.ds(c * 2, 2)].reshape(2 * rows, width)
+        at = pl.ds(pl.multiple_of(c * 2 * rows, 2 * rows), 2 * rows)
+        kv_all[at, :] = nn(part, w_qkv[:, width:]).astype(BF16)
+
+    store_kv = pltpu.make_async_copy(kv_all, kv_hbm, store_sem.at[2])
+    store_kv.start()
+
+    near = pl.ds(pl.multiple_of(me * rows, rows), 2 * rows)
+
+    @pl.loop(0, pairs)
+    def _(p):
+        lanes = pair_lanes(p)
+        q_both = head_stack(q_ref[:, lanes])
+        scores[pl.ds(rows, span), :] = nt(kv_all[:, lanes], q_both) + mask[...]
+        biases = []
+        for h in range(2):
+            band = jnp.broadcast_to(table_ref[pl.ds(2 * p + h, 1), :], (2 * rows, 2 * LANES))
+            biases.append(pltpu.roll(band, 0, 1, stride=1, stride_axis=0)[:, :rows])
+        scores[near, :] = scores[near, :] + jnp.concatenate(biases, axis=1)
+        s = scores[pl.ds(rows, span), :]
+        weights = jnp.exp(s - jnp.max(s, axis=0, keepdims=True))
+        weights = (weights * (1.0 / jnp.sum(weights, axis=0, keepdims=True))).astype(BF16)
+        prob[p] = weights
+        both = tn(kv_all[:, pair_lanes(pairs + p)], weights)
+        o_ref[:, lanes] = head_unstack(both, rows).astype(BF16)
+
+    store_p = pltpu.make_async_copy(prob, p_hbm, store_sem.at[3])
+    store_p.start()
+    loads[3].wait()
+    loads[4].wait()
+    loads[5].wait()
+    r1 = x_ref[...].astype(F32) + nn(o_ref[...], w_self[...])
+    r1_ref[...] = r1
+    n2 = (r1 * rms_scale(r1) * gains_ref[1:2, :]).astype(BF16)
+    n2_ref[...] = n2
+    qc_ref[...] = nn(n2, w_cq[...]).astype(BF16) * jnp.asarray(0.125, BF16)
+
+    @pl.loop(0, pairs)
+    def _(p):
+        lanes = pair_lanes(p)
+        s = nt(ekv[:, lanes], head_stack(qc_ref[:, lanes]))
+        weights = jnp.exp(s - jnp.max(s, axis=0, keepdims=True))
+        weights = (weights * (1.0 / jnp.sum(weights, axis=0, keepdims=True))).astype(BF16)
+        cross_prob[p] = weights
+        both = tn(ekv[:, pair_lanes(pairs + p)], weights)
+        oc_ref[:, lanes] = head_unstack(both, rows).astype(BF16)
+
+    store_pc = pltpu.make_async_copy(cross_prob, pc_hbm, store_sem.at[4])
+    store_pc.start()
+    r2 = r1_ref[...] + nn(oc_ref[...], w_co[...])
+    r2_ref[...] = r2
+    x3 = (r2 * rms_scale(r2) * gains_ref[2:3, :]).astype(BF16)
+    x3_ref[...] = x3
+    experts = router_ref.shape[1]
+    logits = nn(x3, router_ref[...])
+    top = jnp.exp(logits - jnp.max(logits, axis=-1, keepdims=True))
+    gates = top / jnp.sum(top, axis=-1, keepdims=True)
+    gates_ref[...] = gates
+    route = routes_ref[...]
+    chosen = (route == lax.broadcasted_iota(jnp.int32, (rows, experts), 1)).astype(F32)
+    earlier = (
+        lax.broadcasted_iota(jnp.int32, (rows, rows), 1) < lax.broadcasted_iota(jnp.int32, (rows, rows), 0)
+    ).astype(BF16)
+    slot = jnp.sum(nn(earlier, chosen.astype(BF16)) * chosen, axis=1, keepdims=True).astype(jnp.int32)
+    kept = slot < capacity
+    gate_used = jnp.sum(gates * chosen, axis=1, keepdims=True) * kept.astype(F32)
+    target = jnp.where(kept, route * stride + slot, -1)
+    place = (
+        lax.broadcasted_iota(jnp.int32, (rows, experts * stride), 1) == target
+    ).astype(BF16)
+    place_ref[...] = place
+    xs_ref[...] = tn(place, x3).astype(BF16)
+    made_grad = (g_ref[...].astype(F32) * gate_used).astype(BF16)
+    dms_ref[...] = tn(place, made_grad).astype(BF16)
+
+    own.wait_send()
+    for copy in direct + forwards:
+        copy.wait_send()
+    for store in (store_ekv, store_n1, store_kv, store_p, store_pc):
+        store.wait()
+
+
+def forward_call(seq_count, capacity, stride, x, encoder, lengths, buckets, routes, gains, w_qkv, w_self, w_cq, w_ckv,
+                 w_co, rel, router, g):
+    rows, width = x.shape
+    span = seq_count * rows
+    pairs = width // LANES
+    enc_rows = encoder.shape[0]
+    experts = router.shape[1]
+    chips = seq_count // 2
+    shape = jax.ShapeDtypeStruct
+    wide = shape((rows, width), BF16)
+    outs = (
+        shape((seq_count, rows, width), BF16), shape((span, 2 * width), BF16), shape((pairs, span, 2 * rows), BF16),
+        shape((pairs, enc_rows, 2 * rows), BF16), shape((enc_rows, 2 * width), BF16), wide, wide, wide, wide, wide, wide,
+        shape((rows, width), F32), shape((rows, width), F32), shape((rows, experts), F32),
+        shape((rows, experts * stride), BF16), shape((experts * stride, width), BF16), shape((experts * stride, width), BF16),
+    )
+    return pl.pallas_call(
+        functools.partial(forward_kernel, seq_count, capacity, stride),
+        out_shape=outs,
+        in_specs=[VMEM, ANY, SMEM, VMEM, VMEM, VMEM, ANY, ANY, ANY, ANY, ANY, VMEM, VMEM, VMEM],
+        out_specs=tuple([ANY] * 5 + [VMEM] * 12),
+        scratch_shapes=[
+            pltpu.VMEM((seq_count, rows, width), BF16), pltpu.VMEM((span, 2 * width), BF16),
+            pltpu.VMEM((pairs, span, 2 * rows), BF16), pltpu.VMEM((pairs, enc_rows, 2 * rows), BF16),
+            pltpu.VMEM((enc_rows, 2 * width), BF16), pltpu.VMEM((span + rows, 2 * rows), F32),
+            pltpu.VMEM((span, 2 * rows), F32), pltpu.VMEM(w_qkv.shape, BF16), pltpu.VMEM(w_self.shape, BF16),
+            pltpu.VMEM(w_cq.shape, BF16), pltpu.VMEM(w_ckv.shape, BF16), pltpu.VMEM(w_co.shape, BF16),
+            pltpu.VMEM(encoder.shape, BF16), pltpu.VMEM((rel.shape[1], 2 * LANES), F32),
+            pltpu.SemaphoreType.DMA((6,)), pltpu.SemaphoreType.DMA((5,)),
+            pltpu.SemaphoreType.DMA((2 * chips - 1,)), pltpu.SemaphoreType.DMA((2 * chips - 1,)),
+        ],
+        compiler_params=pltpu.CompilerParams(collective_id=0, has_side_effects=True, vmem_limit_bytes=56 << 20),
+        name="forward",
+    )(x, encoder, lengths, buckets, routes, gains, w_qkv, w_self, w_cq, w_ckv, w_co, rel, router, g)
+
+
+def fused(inputs, encoder, lengths, buckets, routes, norm_gains, self_qkv, self_out, cross_q, cross_kv, cross_out,
+          rel_bias, router, expert_in, expert_out, cotangent):
+    seq_count = lax.axis_size("seq")
+    seq_index = lax.axis_index("seq")
+    rows, width = inputs.shape[1:]
+    experts = router.shape[1]
+    capacity = 5 * rows // (4 * experts)
+    stride = -(-capacity // 16) * 16
+    (n1_all, kv_all, prob, cross_prob, ekv, q, o, n2, qc, oc, x3, r1, r2, gates, place, xs, dms) = forward_call(
+        seq_count, capacity, stride, inputs[0], encoder, lengths, buckets[None, :], routes[0], norm_gains, self_qkv,
+        self_out, cross_q, cross_kv, cross_out, rel_bias, router, cotangent[0])
+    pairs = width // LANES
+    hidden = inputs[0].astype(F32)
+    upstream = cotangent[0].astype(F32)
+    a2a = lambda v: lax.all_to_all(v.reshape(experts, stride, width), "exp", split_axis=0, concat_axis=0, tiled=True)
+    arrived = a2a(xs).reshape(-1, width)
+    grad_arrived = a2a(dms).reshape(-1, width)
+    hid, gelu_back = jax.vjp(lambda v: jax.nn.gelu(v, approximate=True), nn(arrived, expert_in[0]))
+    act = hid.astype(BF16)
+    made = nn(act, expert_out[0]).astype(BF16)
+    expert_rows = nn(place, a2a(made).reshape(-1, width))
+    chosen = (routes[0] == jnp.arange(experts)[None, :])
+    picked = jnp.sum(jnp.where(chosen, gates, 0.0), axis=1, keepdims=True)
+    kept = jnp.sum(place.astype(F32), axis=1, keepdims=True)
+    layer_out = r2 + picked * kept * expert_rows
+    dh = gelu_back(nt(grad_arrived, expert_out[0]))[0].astype(BF16)
+    gout = tn(act, grad_arrived)
+    gin = tn(arrived, dh)
+    dx3 = nn(place, a2a(nt(dh, expert_in[0]).astype(BF16)).reshape(-1, width))
+    expert_sums = (
+        lax.psum_scatter(gin[None], "seq", scatter_dimension=1, tiled=True),
+        lax.psum_scatter(gout[None], "seq", scatter_dimension=1, tiled=True),
+    )
+    gate_grad = jnp.sum(upstream * expert_rows, axis=1, keepdims=True) * kept
+    dl = gates * (jnp.where(chosen, gate_grad, 0.0) - picked * gate_grad)
+    router_grad = jnp.dot(x3.astype(F32).T, dl, precision=highest)
+    dx3 = dx3 + jnp.dot(dl, router.astype(F32).T, precision=highest)
+    _, back3 = jax.vjp(rms_norm, r2, norm_gains[2])
+    dr2, gain3 = back3(dx3)
+    dr2 = dr2 + upstream
+    do2 = dr2.astype(BF16)
+    cross_out_grad = tn(oc, do2)
+    doc2 = nt(do2, cross_out).astype(BF16)
+    heads = lambda v: v.reshape(v.shape[0], H, HD)
+    unstack = lambda v: v.reshape(pairs, -1, 2, rows).transpose(0, 2, 1, 3).reshape(H, -1, rows)
+    pc = unstack(cross_prob).astype(F32)
+    kc, vc = heads(ekv[:, :width]), heads(ekv[:, width:])
+    dp = jnp.einsum("qhd,khd->hkq", heads(doc2), vc, preferred_element_type=F32)
+    dc = (pc * (dp - jnp.sum(pc * dp, axis=1, keepdims=True))).astype(BF16)
+    dqc = (jnp.einsum("hkq,khd->qhd", dc, kc, preferred_element_type=F32) * 0.125).reshape(rows, width).astype(BF16)
+    dkc = jnp.einsum("hkq,qhd->khd", dc, heads(qc), preferred_element_type=F32).reshape(-1, width)
+    dvc = jnp.einsum("hkq,qhd->khd", pc.astype(BF16), heads(doc2), preferred_element_type=F32).reshape(-1, width)
+    dekv = lax.psum_scatter(jnp.concatenate([dkc, dvc], axis=1), ("seq", "exp"), scatter_dimension=0, tiled=True).astype(BF16)
+    enc_count = dekv.shape[0]
+    flat_index = seq_index * lax.axis_size("exp") + lax.axis_index("exp")
+    own_enc = lax.dynamic_slice_in_dim(encoder, flat_index * enc_count, enc_count, 0)
+    grad_encoder = nt(dekv, cross_kv)
+    pair_grad = tn(own_enc, dekv)
+    cq_grad = tn(n2, dqc)
+    _, back2 = jax.vjp(rms_norm, r1, norm_gains[1])
+    dr1, gain2 = back2(nt(dqc, cross_q))
+    dr1 = dr1 + dr2
+    do1 = dr1.astype(BF16)
+    self_out_grad = tn(o, do1)
+    dob = nt(do1, self_out).astype(BF16)
+    pr = unstack(prob).astype(F32)
+    k, v = heads(kv_all[:, :width]), heads(kv_all[:, width:])
+    dp = jnp.einsum("qhd,khd->hkq", heads(dob), v, preferred_element_type=F32)
+    ds = (pr * (dp - jnp.sum(pr * dp, axis=1, keepdims=True))).astype(BF16)
+    dq = (jnp.einsum("hkq,khd->qhd", ds, k, preferred_element_type=F32) * 0.125).reshape(rows, width).astype(BF16)
+    dk = jnp.einsum("hkq,qhd->khd", ds, heads(q), preferred_element_type=F32).reshape(-1, width)
+    dv = jnp.einsum("hkq,qhd->khd", pr.astype(BF16), heads(dob), preferred_element_type=F32).reshape(-1, width)
+    dkv = lax.psum_scatter(jnp.concatenate([dk, dv], axis=1), "seq", scatter_dimension=0, tiled=True).astype(BF16)
+    distance = jnp.clip(seq_index * rows + jnp.arange(rows)[None, :] - jnp.arange(seq_count * rows)[:, None], 0, 127)
+    table_grad = jax.vmap(lambda d: jnp.zeros((128,), F32).at[distance.reshape(-1)].add(d.reshape(-1).astype(F32)))(ds)
+    bucket_pick = (buckets[:, None] == jnp.arange(rel_bias.shape[0])[None, :]).astype(F32)
+    rel_grad = jnp.dot(bucket_pick.T, table_grad.T, precision=highest)
+    dqkv = jnp.concatenate([dq, dkv], axis=1)
+    qkv_grad = tn(n1_all[seq_index], dqkv)
+    _, back1 = jax.vjp(rms_norm, hidden, norm_gains[0])
+    dx, gain1 = back1(nt(dqkv, self_qkv))
+    grad_input = dx + dr1
+    summed = lax.psum((jnp.stack([gain1, gain2, gain3]), qkv_grad, self_out_grad, cq_grad, pair_grad, cross_out_grad,
+                       rel_grad, router_grad), ("seq", "exp"))
+    return (layer_out.astype(BF16)[None], grad_input[None], grad_encoder, *summed, *expert_sums)
+
+
+def on_device(*operands):
+    if lax.axis_size("seq") * operands[0].shape[1] <= 1024 and lax.axis_size("seq") % 2 == 0:
+        return fused(*operands)
+    return streamed(*operands)
+
+
 def solution(mesh):
     in_specs = (
         P("exp", "seq", None),

time: 1200 us -> 1300 us (1.083)
  other arithmetic: 80.4 us -> 906 us
  waiting for transfers between devices: 476 us -> 119 us
  local copies, waits for them, and re-layouts: 388 us -> 83.5 us
  matrix products: 122 us -> 72.6 us
  blocking collectives: 83.8 us -> 40.6 us
  Pallas kernels: 0 us -> 32.4 us
    scatter-add x0 -> x1, other arithmetic: none -> 885 us  [fused(): jnp.zeros((128,), F32).at[distance.reshape(-1)]]
    psum x1, waiting for transfers between devices: 315 us -> 0.01 us  [fused(): lax.psum((jnp.stack([gain1, gain2, gain3]), qkv_grad, self_out_grad, cq_g...]
    reshape x8 -> x0, local copies, waits for them, and re-layouts: 163 us -> none  [the longest x2 70.2 us: table_terms(): flat.reshape(head_count, query_rows, band_len)]
    while x48 -> x0, local copies, waits for them, and re-layouts: 75.3 us -> none
    reduce_scatter x3, waiting for transfers between devices: 118 us -> 58.8 us  [the longest x1 58.8 us: fused(): lax.psum_scatter(jnp.concatenate([dk, dv], axis=1), 'seq', scatter_dimens...]
    unnamed x10 -> x6, waiting for transfers between devices: 1.49 us -> 53.3 us
    dot_general x55 -> x29, matrix products: 117 us -> 72.6 us  [the longest x7 29.8 us: tn(): lax.dot_general(a, b, (((0,), (0,)), ((), ())), preferred_element_type=F32)]
    all_gather x4 -> x0, waiting for transfers between devices: 33.4 us -> none  [the longest x1 27.6 us: on_device(): lax.all_gather(keys_own, 'seq', axis=0, tiled=True)]
  transfers between devices with their start and end apart: 11 -> 9, of which waited for: 8 -> 4; matrix products, arithmetic and copies ran while one was open for 37% -> 79% of each run, Pallas kernels for 0% -> 0%
where the time goes in v1:
time: 1300 us; the launch traced here: 1290 us
  other arithmetic  906 us (70%)
  waiting for transfers between devices  119 us (9%)
  local copies, waits for them, and re-layouts  83.5 us (6%)
  matrix products  72.6 us (6%)
  blocking collectives  40.6 us (3%)
  Pallas kernels  32.4 us (2%)
  starting transfers between devices  20.5 us (2%)
  between operations  14.8 us (1%)
    scatter-add x1, other arithmetic, fused(): jnp.zeros((128,), F32).at[distance.reshape(-1)]  885 us
    reduce_scatter x1, waiting for transfers between devices, fused(): lax.psum_scatter(jnp.concatenate([dk, dv], axis=1), 'seq', scatter_dimens...  58.8 us
    unnamed x6, waiting for transfers between devices  53.3 us
    psum x1, blocking collectives, fused(): lax.psum((jnp.stack([gain1, gain2, gain3]), qkv_grad, self_out_grad, cq_g...  40.6 us
    unnamed x115, local copies, waits for them, and re-layouts  34.5 us
    pallas_call x1, Pallas kernels, forward_call(): pl.pallas_call(functools.partial(forward_kernel, seq_count, capacity, str...  32.4 us
    dot_general x7, matrix products, tn(): lax.dot_general(a, b, (((0,), (0,)), ((), ())), preferred_element_type=F32)  29.8 us
    convert_element_type x1, local copies, waits for them, and re-layouts, fused(): d.reshape(-1).astype(F32)  28.6 us
  transfers between devices with their start and end apart: 9, of which 4 were waited for; matrix products, arithmetic and copies ran while one was open for 79% of the time, Pallas kernels for 0%

profile of v1, /device:TPU:0, one launch (start us, length us, event | category | flops | bytes accessed | tf_op | source)
XLA Modules:
  0.0 1288.4 jit_solution(5927005436306630430)
XLA Ops:
  9.9 1.5 copy.57.router_ref
  11.5 32.4 %forward.1 = (bf16[8,128,768]{2,1,0:T(8,128)(2,1)}, bf16[1024,1536]{1,0:T(8,128)(2,1)}, bf16[6,1024,256]{2,1,0:T(8,128)(2,1)}, bf16[6,512,256]{2,1,0:T(8,128)(2,...) custom-call(bf16[128,768]{1,0:T(8,128)(2,1)} %bitcast.142, ...), custom_call_target="tpu_custom_call" | custom-call | tf_op jit(solution)/shard_map/forward/pallas_call | solution.py:697
  43.8 4.9 all-to-all-start
  52.0 1.5 fusion.79
  54.6 1.5 fusion.80
  58.1 3.2 fusion.77
  61.3 1.6 copy.59
  62.9 1.7 copy.65
  65.5 5.1 all-to-all-start.2
  70.6 3.4 fusion.8
  75.5 4.6 fusion.24
  80.7 4.6 all-to-all-start.1
  85.3 5.5 fusion.18
  91.8 4.9 fusion.21
  96.7 5.2 all-to-all-start.3
  102.0 2.0 fusion.29
  105.2 5.8 all-to-all-done.3
  111.0 1.4 multiply_reduce_fusion
  112.5 1.9 convert_add_fusion
  121.4 2.4 copy.68
  124.1 1.6 copy-done.16
  126.7 1.7 copy-done.2
  132.3 1.8 copy.63
  134.0 2.3 fusion.82
  137.7 2.8 fusion.1
  141.7 3.3 pad_maximum_fusion
  145.1 6.5 convolution_bitcast_fusion.1
  151.6 7.4 convolution_bitcast_fusion
  159.4 2.6 copy.58
  162.9 3.0 fusion.85
  165.9 1.9 fusion.46
  167.8 1.9 fusion.49
  171.1 53.2 %reduce-scatter.13.cloned.1.call-done = f32[16,1536]{1,0:T(8,128)} async-done(((f32[512,1536]{1,0:T(8,128)}), f32[16,1536]{1,0:T(8,128)}) %reduce-scatter.13.cloned.1.call-update) | async-done | bytes 98320
  224.3 1.8 copy.69
  226.1 4.0 fusion.42
  230.1 58.8 %reduce-scatter.7.cloned.1.call-done = f32[128,1536]{0,1:T(8,128)} async-done(((f32[1024,1536]{0,1:T(8,128)}), f32[128,1536]{0,1:T(8,128)}) %reduce-scatter.7.cloned.1.call-update) | async-done | bytes 786448 | tf_op jit(solution)/shard_map/reduce_scatter | solution.py:789
  290.9 5.1 fusion.37
  296.0 2.4 compare_select_fusion
  300.6 28.6 %copy.67 = f32[12,1024,128]{0,2,1:T(8,128)} copy(bf16[12,1024,128]{2,1,0:T(8,128)(2,1)S(1)} %fusion.1) | data formatting | bytes 9437184 | tf_op jit(solution)/shard_map/vmap()/convert_element_type | solution.py:791
  329.2 885.4 %scatter_custom_fusion = f32[12,128]{0,1:T(8,128)S(1)} fusion(s32[131072]{0:T(1024)} %bitcast.153, f32[131072,12]{1,0:T(8,128)} %bitcast.44, f32[]{:T(128)} %constant.21.clone.1), kind=kCustom, calls=%fused_computation.92 | custom fusion | flops 1572864 | bytes 6656 | tf_op jit(solution)/shard_map/vmap()/scatter-add | solution.py:791
  1216.2 3.2 fusion.86
  1219.4 3.4 fusion.36
  1222.8 40.6 %all-reduce = (f32[3,768]{1,0:T(4,128)}, f32[32,12]{0,1:T(8,128)}, f32[768,4]{0,1:T(4,128)}) all-reduce(f32[3,768]{1,0:T(4,128)S(1)} %pad_maximum_fusion.7, f32[32,12]{0,1:T(8,128)S(1)} %fusion.52, f32[768,4]{0,1:T(4,128)S(1)} %fusion.53), channel_id=1, replica_groups=mesh['seq'=8,'exp'=4] {'seq','exp'}, use_global_device_ids=true, to_apply=%region_16.17 | all-reduce | flops 5760 | bytes 46080 | tf_op jit(solution)/shard_map/psum | solution.py:799
  1264.3 6.6 copy.75
  1270.9 1.4 copy.76
  1273.4 1.4 copy.77
  1274.8 1.8 copy-done.12
  1276.6 2.4 copy.78
  (166 shorter events, 41.6 us)
Async XLA Ops:
  11.5 37.2 %copy-start.39 = (f32[3,768]{1,0:T(4,128)S(1)}, f32[3,768]{1,0:T(4,128)}, u32[]{:S(2)}) copy-start(f32[3,768]{1,0:T(4,128)} %gains_ref.1) | copy-start | bytes 27652
  43.8 21.7 %all-to-all-start = ((bf16[4,48,768]{2,1,0:T(8,128)(2,1)}), bf16[4,48,768]{2,1,0:T(8,128)(2,1)S(1)}, u32[]{:S(2)}, u32[]{:S(2)}) async-start(bf16[4,48,768]{2,1,0:T(8,128)(2,1)} %bitcast.155), calls=%async_computation | async-start | bytes 589824 | tf_op jit(solution)/shard_map/all_to_all | solution.py:731
  49.9 15.1 %copy-start.48 = (f32[128]{0:T(128)}, f32[128]{0:T(128)S(1)}, u32[]{:S(2)}) copy-start(f32[128]{0:T(128)S(1)} %multiply_reduce_fusion.5) | copy-start | bytes 1540
  51.9 13.1 %copy-start.46 = (f32[128]{0:T(128)}, f32[128]{0:T(128)S(1)}, u32[]{:S(2)}) copy-start(f32[128]{0:T(128)S(1)} %multiply_reduce_fusion.3) | copy-start | bytes 1540
  54.6 2.7 copy-start.38
  61.3 3.4 copy-start.35
  61.3 3.4 copy-start.41
  65.5 8.5 copy-start.13
  65.5 15.2 %all-to-all-start.2 = ((bf16[4,48,768]{2,1,0:T(8,128)(2,1)}), bf16[4,48,768]{2,1,0:T(8,128)(2,1)S(1)}, u32[]{:S(2)}, u32[]{:S(2)}) async-start(bf16[4,48,768]{2,1,0:T(8,128)(2,1)} %bitcast.154), calls=%async_computation.2 | async-start | bytes 589824 | tf_op jit(solution)/shard_map/all_to_all | solution.py:731
  80.7 10.1 copy-start.28
  80.7 16.0 %all-to-all-start.1 = ((bf16[4,48,768]{2,1,0:T(8,128)(2,1)}), bf16[4,48,768]{2,1,0:T(8,128)(2,1)S(1)}, u32[]{:S(2)}, u32[]{:S(2)}) async-start(bf16[4,48,768]{2,1,0:T(8,128)(2,1)} %bitcast.9), calls=%async_computation.1 | async-start | bytes 589824 | tf_op jit(solution)/shard_map/all_to_all | solution.py:731
  91.8 10.2 copy-start.25
  91.8 10.2 copy-start.34
  91.8 12.2 copy-start.40
  91.8 19.2 %copy-start.15 = (f32[128,768]{1,0:T(8,128)S(1)}, f32[128,768]{1,0:T(8,128)}, u32[]{:S(2)}) copy-start(f32[128,768]{1,0:T(8,128)} %get-tuple-element.30) | copy-start | bytes 1179652
  96.7 15.7 %copy-start.49 = (f32[128]{0:T(128)S(1)}, f32[128]{0:T(128)}, u32[]{:S(2)}) copy-start(f32[128]{0:T(128)} %copy-done.48) | copy-start | bytes 1540
  96.7 5.2 copy-start.29
  96.7 14.3 %all-to-all-start.3 = ((bf16[4,48,768]{2,1,0:T(8,128)(2,1)}), bf16[4,48,768]{2,1,0:T(8,128)(2,1)}, u32[]{:S(2)}, u32[]{:S(2)}) async-start(bf16[4,48,768]{2,1,0:T(8,128)(2,1)} %bitcast.20), calls=%async_computation.3 | async-start | bytes 589824 | tf_op jit(solution)/shard_map/all_to_all | solution.py:731
  102.0 122.3 %reduce-scatter.13.cloned.1.call-start = ((), (), s32[]{:S(2)}) async-start(), calls=%async_computation.11 | async-start | bytes 3244032
  102.0 13.1 %copy-start.9 = (bf16[768,768]{1,0:T(8,128)(2,1)S(1)}, bf16[768,768]{1,0:T(8,128)(2,1)}, u32[]{:S(2)}) copy-start(bf16[768,768]{1,0:T(8,128)(2,1)} %cross_out_hbm.1) | copy-start | bytes 3538948
  104.0 10.3 copy-start.42
  104.0 10.3 copy-start.43
  115.1 3.0 copy-start.18
  123.9 165.1 %reduce-scatter.7.cloned.1.call-start = ((), (), s32[]{:S(2)}) async-start(), calls=%async_computation.8 | async-start | bytes 7077888 | tf_op jit(solution)/shard_map/reduce_scatter | solution.py:789
  126.5 2.7 copy-start.17
  126.7 9.6 copy-start
  126.7 2.9 copy-start.11
  126.7 3.0 copy-start.14
  126.7 3.0 copy-start.44
  134.0 2.3 copy-start.22
  137.7 2.8 copy-start.31
  145.0 1119.3 %reduce-scatter.9.cloned.1.call-start = ((), (), s32[]{:S(2)}) async-start(), calls=%async_computation.9 | async-start | bytes 10616832 | tf_op jit(solution)/shard_map/reduce_scatter | solution.py:747
  151.6 1112.7 %reduce-scatter.11.cloned.1.call-start = ((), (), s32[]{:S(2)}) async-start(), calls=%async_computation.10 | async-start | bytes 10616832 | tf_op jit(solution)/shard_map/reduce_scatter | solution.py:748
  159.1 1105.2 %all-reduce.4.cloned.1.call-start = ((), (), s32[]{:S(2)}) async-start(), calls=%async_computation.12 | async-start | bytes 37748736 | tf_op jit(solution)/shard_map/psum | solution.py:799
  162.0 3.9 copy-start.37
  162.9 4.9 copy-start.8
  162.9 4.9 copy-start.36
  165.9 3.8 copy-start.5
  300.6 914.1 %copy-start.45 = (s32[128]{0:T(128)S(1)}, s32[128]{0:T(128)}, u32[]{:S(2)}) copy-start(s32[128]{0:T(128)} %param.19) | copy-start | bytes 1540
  329.2 890.2 %copy-start.23 = (bf16[1,128,768]{2,1,0:T(8,128)(2,1)S(1)}, bf16[1,128,768]{2,1,0:T(8,128)(2,1)}, u32[]{:S(2)}) copy-start(bf16[1,128,768]{2,1,0:T(8,128)(2,1)} %param.16) | copy-start | bytes 589828
  329.2 890.2 %copy-start.27 = (bf16[128,1536]{0,1:T(8,128)(2,1)S(1)}, bf16[128,1536]{0,1:T(8,128)(2,1)}, u32[]{:S(2)}) copy-start(bf16[128,1536]{0,1:T(8,128)(2,1)} %copy-done.26) | copy-start | bytes 1179652
  329.2 890.2 %copy-start.32 = (bf16[12,64,128]{2,1,0:T(8,128)(2,1)S(1)}, bf16[12,64,128]{2,1,0:T(8,128)(2,1)}, u32[]{:S(2)}) copy-start(bf16[12,64,128]{2,1,0:T(8,128)(2,1)} %fusion.28) | copy-start | bytes 589828
  329.2 890.2 %copy-start.50 = (f32[128]{0:T(128)S(1)}, f32[128]{0:T(128)}, u32[]{:S(2)}) copy-start(f32[128]{0:T(128)} %fusion.71) | copy-start | bytes 1540
  1219.4 44.0 %copy-start.52 = (f32[128]{0:T(128)S(1)}, f32[128]{0:T(128)}, u32[]{:S(2)}) copy-start(f32[128]{0:T(128)} %copy-done.51) | copy-start | bytes 1540
  1264.3 6.6 copy-start.21
  1270.9 2.5 copy-start.20
  1273.4 3.2 copy-start.12
  1276.6 3.4 copy-start.19
  (14 other events, 17.9 us)
Sparse Core Ops, SparseCore 0:
  124.0 100.2 reduce-scatter.12
  228.2 60.6 reduce-scatter.6
  293.4 76.5 reduce-scatter.8
  374.3 76.4 reduce-scatter.10
  459.4 306.6 all-reduce.3

commit v2 on v1

--- a/solution.py
+++ b/solution.py
@@ -714,10 +714,722 @@
     )(x, encoder, lengths, buckets, routes, gains, w_qkv, w_self, w_cq, w_ckv, w_co, rel, router, g)
 
 
+def expert_peers(exp_index, experts):
+    return [lax.rem(exp_index + d, experts) for d in range(1, experts)]
+
+
+def gelu_parts(hid):
+    root, cubic = 0.7978845608028654, 0.044715
+    square = hid * hid
+    bent = jnp.tanh(root * hid * (1.0 + cubic * square))
+    half = 0.5 * (1.0 + bent)
+    return hid * half, half + 0.5 * hid * (1.0 - bent * bent) * (root + 3.0 * root * cubic * square)
+
+
+def experts_kernel(
+    seq_count, experts, stride,
+    xs_ref, dms_ref, w_in_hbm, w_out_hbm,
+    made_ref, dx_ref, x_hbm, dm_hbm,
+    x_all, dm_all, made_out, made_back, dx_out, dx_back, act, slope, w_in, w_out,
+    load_sem, own_sem, store_sem, zx_send, zx_recv, zd_send, zd_recv, zm_send, zm_recv, zg_send, zg_recv,
+    x_send, x_recv, d_send, d_recv,
+):
+    chips = seq_count // 2
+    width = xs_ref.shape[-1]
+    rows = experts * stride
+    hidden = w_in.shape[1]
+    chunk = width
+    me = lax.axis_index("seq")
+    mine = lax.axis_index("exp")
+    core, chip, partner, others, sources = seq_peers(me, chips)
+    peers = expert_peers(mine, experts)
+    loads = [
+        pltpu.make_async_copy(w_in_hbm, w_in, load_sem.at[0]),
+        pltpu.make_async_copy(w_out_hbm, w_out, load_sem.at[1]),
+    ]
+    for load in loads:
+        load.start()
+    own_copies = [
+        pltpu.make_async_copy(xs_ref.at[mine], x_all.at[me, mine], own_sem.at[0]),
+        pltpu.make_async_copy(dms_ref.at[mine], dm_all.at[me, mine], own_sem.at[1]),
+    ]
+    for copy in own_copies:
+        copy.start()
+    enter([{"seq": partner}] + [{"seq": other} for other in others] + [{"exp": peer} for peer in peers])
+
+    def over_exp(src, dst, send, recv):
+        copies = [
+            remote(src.at[peer], dst.at[mine], send.at[d], recv.at[d], {"exp": peer}) for d, peer in enumerate(peers)
+        ]
+        for copy in copies:
+            copy.start()
+        return copies
+
+    def over_seq(buffer, send, recv):
+        copies = [remote(buffer.at[me], buffer.at[me], send.at[0], recv.at[0], {"seq": partner})] + [
+            remote(buffer.at[me], buffer.at[me], send.at[d], recv.at[d], {"seq": others[d - 1]}) for d in range(1, chips)
+        ]
+        for copy in copies:
+            copy.start()
+        return copies
+
+    def pass_on(copies, buffer, send, recv):
+        forwards = []
+        for d in range(1, chips):
+            copies[d].wait_recv()
+            block = buffer.at[sources[d - 1]]
+            forward = remote(block, block, send.at[chips - 1 + d], recv.at[chips - 1 + d], {"seq": partner})
+            forward.start()
+            forwards.append(forward)
+        return forwards
+
+    x_moves = over_exp(xs_ref, x_all.at[me], zx_send, zx_recv)
+    dm_moves = over_exp(dms_ref, dm_all.at[me], zd_send, zd_recv)
+    own_copies[0].wait()
+    for move in x_moves:
+        move.wait_recv()
+    x_copies = over_seq(x_all, x_send, x_recv)
+    x = x_all[me].reshape(rows, width)
+    loads[0].wait()
+    loads[1].wait()
+    made = jnp.zeros((rows, width), F32)
+    for n in range(hidden // chunk):
+        at = slice(n * chunk, (n + 1) * chunk)
+        value, derivative = gelu_parts(nn(x, w_in[:, at]))
+        slope[:, at] = derivative
+        value = value.astype(BF16)
+        made = made + nn(value, w_out[at, :])
+    made_out[...] = made.astype(BF16).reshape(experts, stride, width)
+    made_moves = over_exp(made_out, made_back, zm_send, zm_recv)
+    made_back[mine] = made_out[mine]
+
+    own_copies[1].wait()
+    for move in dm_moves:
+        move.wait_recv()
+    dm_copies = over_seq(dm_all, d_send, d_recv)
+    dm = dm_all[me].reshape(rows, width)
+    dx = jnp.zeros((rows, width), F32)
+    for n in range(hidden // chunk):
+        at = slice(n * chunk, (n + 1) * chunk)
+        dh = (nt(dm, w_out[at, :]) * slope[:, at]).astype(BF16)
+        dx = dx + nt(dh, w_in[:, at])
+    dx_out[...] = dx.astype(BF16).reshape(experts, stride, width)
+    dx_moves = over_exp(dx_out, dx_back, zg_send, zg_recv)
+    dx_back[mine] = dx_out[mine]
+
+    x_forwards = pass_on(x_copies, x_all, x_send, x_recv)
+    for move in made_moves:
+        move.wait_recv()
+    made_ref[...] = made_back[...]
+    dm_forwards = pass_on(dm_copies, dm_all, d_send, d_recv)
+    for move in dx_moves:
+        move.wait_recv()
+    dx_ref[...] = dx_back[...]
+    x_copies[0].wait_recv()
+    for forward in x_forwards:
+        forward.wait_recv()
+    store_x = pltpu.make_async_copy(x_all, x_hbm, store_sem.at[0])
+    store_x.start()
+    dm_copies[0].wait_recv()
+    for forward in dm_forwards:
+        forward.wait_recv()
+    store_dm = pltpu.make_async_copy(dm_all, dm_hbm, store_sem.at[1])
+    store_dm.start()
+    for copy in x_moves + dm_moves + made_moves + dx_moves + x_copies + dm_copies + x_forwards + dm_forwards:
+        copy.wait_send()
+    store_x.wait()
+    store_dm.wait()
+
+
+def experts_call(seq_count, experts, stride, xs, dms, w_in, w_out):
+    width = xs.shape[-1]
+    chips = seq_count // 2
+    shape = jax.ShapeDtypeStruct
+    block = (experts, stride, width)
+    every = (seq_count,) + block
+    dma = lambda n: pltpu.SemaphoreType.DMA((n,))
+    z = experts - 1
+    return pl.pallas_call(
+        functools.partial(experts_kernel, seq_count, experts, stride),
+        out_shape=(shape(block, BF16), shape(block, BF16), shape(every, BF16), shape(every, BF16)),
+        in_specs=[VMEM, VMEM, ANY, ANY],
+        out_specs=(VMEM, VMEM, ANY, ANY),
+        scratch_shapes=[
+            pltpu.VMEM(every, BF16), pltpu.VMEM(every, BF16), pltpu.VMEM(block, BF16), pltpu.VMEM(block, BF16),
+            pltpu.VMEM(block, BF16), pltpu.VMEM(block, BF16), pltpu.VMEM((8, 128), BF16),
+            pltpu.VMEM((experts * stride, w_in.shape[1]), F32), pltpu.VMEM(w_in.shape, BF16), pltpu.VMEM(w_out.shape, BF16),
+            dma(2), dma(2), dma(2), dma(z), dma(z), dma(z), dma(z), dma(z), dma(z), dma(z), dma(z),
+            dma(2 * chips - 1), dma(2 * chips - 1), dma(2 * chips - 1), dma(2 * chips - 1),
+        ],
+        compiler_params=pltpu.CompilerParams(collective_id=1, has_side_effects=True, vmem_limit_bytes=56 << 20),
+        name="experts",
+    )(xs.reshape(block), dms.reshape(block), w_in, w_out)
+
+
+def rms_back(a, gain, grad):
+    scale = rms_scale(a)
+    weighted = grad * gain
+    da = scale * weighted - a * (scale * scale * scale * jnp.mean(a * weighted, axis=-1, keepdims=True))
+    return da, jnp.sum(grad * (a * scale), axis=0, keepdims=True)
+
+
+def in_two(value):
+    high = value.astype(BF16)
+    return high, (value - high.astype(F32)).astype(BF16)
+
+
+def backward_kernel(
+    seq_count, experts,
+    made_ref, dxb_ref, g_ref, x_ref, r1_ref, r2_ref, gates_ref, place_ref, routes_ref, x3_ref, n2_ref, o_ref, oc_ref,
+    q_ref, qc_ref, gains_ref, router_ref, buckets_ref, kv_hbm, p_hbm, pc_hbm, ekv_hbm, co_hbm, cq_hbm, so_hbm, qkv_hbm,
+    out_ref, dx_ref, dqkv_t_ref, squares_ref, dekv_ref, small_ref,
+    kv_all, prob, cross_prob, ekv, w_co, w_cq, w_so, w_qkv, dr_ref, doc_ref, dqc_ref, dqkv_ref, ds_ref, diag_ref, total_ref,
+    e_out, e_pair, e_chip, e_mine, e_exp, t_out, t_pair, t_chip, w_out, w_pair, w_chip,
+    load_sem, ep_send, ep_recv, ec_send, ec_recv, ee_send, ee_recv, tp_send, tp_recv, tc_send, tc_recv,
+    wp_send, wp_recv, wc_send, wc_recv,
+):
+    chips = seq_count // 2
+    rows, width = x_ref.shape
+    span = seq_count * rows
+    pairs = width // LANES
+    me = lax.axis_index("seq")
+    mine = lax.axis_index("exp")
+    core, chip, partner, others, sources = seq_peers(me, chips)
+    other_core = 1 - core
+    other_chips = [lax.rem(chip + d, chips) for d in range(1, chips)]
+    peers = expert_peers(mine, experts)
+    loads = [
+        pltpu.make_async_copy(src, dst, load_sem.at[i])
+        for i, (src, dst) in enumerate(
+            [(co_hbm, w_co), (ekv_hbm, ekv), (pc_hbm, cross_prob), (cq_hbm, w_cq), (so_hbm, w_so), (kv_hbm, kv_all),
+             (p_hbm, prob), (qkv_hbm, w_qkv)]
+        )
+    ]
+    for load in loads:
+        load.start()
+    enter([{"seq": partner}] + [{"seq": other} for other in others] + [{"exp": peer} for peer in peers])
+
+    made = nn(place_ref[...], made_ref[...])
+    kept = jnp.sum(place_ref[...].astype(F32), axis=1, keepdims=True)
+    gates = gates_ref[...]
+    chosen = (routes_ref[...] == lax.broadcasted_iota(jnp.int32, gates.shape, 1)).astype(F32)
+    picked = jnp.sum(gates * chosen, axis=1, keepdims=True)
+    g = g_ref[...].astype(F32)
+    out_ref[...] = (r2_ref[...] + (picked * kept) * made).astype(BF16)
+    gate_grad = jnp.sum(g * made, axis=1, keepdims=True) * kept
+    dl = gates * (chosen * gate_grad - picked * gate_grad)
+    dl_high, dl_low = in_two(dl)
+    x3 = x3_ref[...]
+    small_ref[...] = jnp.zeros_like(small_ref)
+    small_ref[4 : 4 + experts, :] = tn(dl_high, x3) + tn(dl_low, x3)
+    dx3 = nn(place_ref[...], dxb_ref[...]) + nt(dl_high, router_ref[...]) + nt(dl_low, router_ref[...])
+    da, dw = rms_back(r2_ref[...], gains_ref[2:3, :], dx3)
+    small_ref[2:3, :] = dw
+    dr_ref[...] = g + da
+    do2 = dr_ref[...].astype(BF16)
+    loads[0].wait()
+    doc_ref[...] = nt(do2, w_co[...]).astype(BF16)
+
+    part = width // seq_count
+
+    def square_start(i, left, right):
+        grad = tn(left, right).astype(BF16).reshape(chips, 2, part, width)
+        at = pl.ds(i * part, part)
+        for k in range(2):
+            w_out[k, :, at, :] = grad[:, k]
+        copy = remote(w_out.at[other_core, :, at, :], w_pair.at[:, at, :], wp_send.at[i], wp_recv.at[i], {"seq": partner})
+        copy.start()
+        return copy
+
+    def square_chips(i, pair_copy):
+        at = pl.ds(i * part, part)
+        pair_copy.wait_recv()
+        w_out[core, :, at, :] = (w_out[core, :, at, :].astype(F32) + w_pair[:, at, :].astype(F32)).astype(BF16)
+        copies = [
+            remote(w_out.at[core, other_chips[d], at, :], w_chip.at[d, at, :], wc_send.at[i, d], wc_recv.at[i, d],
+                   {"seq": others[d]})
+            for d in range(chips - 1)
+        ]
+        for copy in copies:
+            copy.start()
+        return copies
+
+    def square_sum(i, copies):
+        at = pl.ds(i * part, part)
+        total = w_out[core, chip, at, :].astype(F32)
+        for d, copy in enumerate(copies):
+            copy.wait_recv()
+            total = total + w_chip[d, at, :].astype(F32)
+        squares_ref[at, :] = total.astype(BF16)
+
+    co_pair = square_start(2, oc_ref[...], do2)
+
+    loads[1].wait()
+    loads[2].wait()
+    enc_rows = ekv.shape[0]
+    enc_part = enc_rows // seq_count
+
+    @pl.loop(0, pairs)
+    def _(p):
+        lanes, value_lanes = pair_lanes(p), pair_lanes(pairs + p)
+        doc_both = head_stack(doc_ref[:, lanes])
+        weights = cross_prob[p]
+        wide = weights.astype(F32)
+        dp = nt(ekv[:, value_lanes], doc_both)
+        dc = (wide * (dp - jnp.sum(wide * dp, axis=0, keepdims=True))).astype(BF16)
+        dk = nn(dc, head_stack(qc_ref[:, lanes])).astype(BF16).reshape(chips, 2, enc_part, LANES)
+        dv = nn(weights, doc_both).astype(BF16).reshape(chips, 2, enc_part, LANES)
+        for k in range(2):
+            e_out[k, :, :, lanes] = dk[:, k]
+            e_out[k, :, :, value_lanes] = dv[:, k]
+        dqc_ref[:, lanes] = (head_unstack(tn(ekv[:, lanes], dc), rows) * 0.125).astype(BF16)
+
+    e_pair_copy = remote(e_out.at[other_core], e_pair, ep_send.at[0], ep_recv.at[0], {"seq": partner})
+    e_pair_copy.start()
+    co_chips = square_chips(2, co_pair)
+    dqc = dqc_ref[...]
+    loads[3].wait()
+    loads[4].wait()
+    da, dw = rms_back(r1_ref[...], gains_ref[1:2, :], nt(dqc, w_cq[...]))
+    small_ref[1:2, :] = dw
+    dr_ref[...] = dr_ref[...] + da
+    do1 = dr_ref[...].astype(BF16)
+    doc_ref[...] = nt(do1, w_so[...]).astype(BF16)
+    e_pair_copy.wait_recv()
+    e_out[core] = (e_out[core].astype(F32) + e_pair[...].astype(F32)).astype(BF16)
+    e_chip_copies = [
+        remote(e_out.at[core, other_chips[d]], e_chip.at[d], ec_send.at[d], ec_recv.at[d], {"seq": others[d]})
+        for d in range(chips - 1)
+    ]
+    for copy in e_chip_copies:
+        copy.start()
+    cq_pair = square_start(1, n2_ref[...], dqc)
+    so_pair = square_start(0, o_ref[...], do1)
+    cq_chips = square_chips(1, cq_pair)
+    so_chips = square_chips(0, so_pair)
+
+    loads[5].wait()
+    loads[6].wait()
+    ds_ref[pl.ds(0, rows), :] = jnp.zeros((rows, 2 * rows), BF16)
+    near = pl.ds(pl.multiple_of(me * rows, rows), 2 * rows)
+    flip = (
+        lax.broadcasted_iota(jnp.int32, (2 * rows, 2 * rows), 0) + lax.broadcasted_iota(jnp.int32, (2 * rows, 2 * rows), 1)
+        == 2 * rows - 1
+    ).astype(BF16)
+
+    def pair_copy(p):
+        return remote(t_out.at[p, other_core], t_pair.at[p], tp_send.at[p], tp_recv.at[p], {"seq": partner})
+
+    def chip_copies(p):
+        return [
+            remote(t_out.at[p, core, other_chips[d]], t_chip.at[p, d], tc_send.at[p, d], tc_recv.at[p, d], {"seq": others[d]})
+            for d in range(chips - 1)
+        ]
+
+    @pl.loop(0, pairs + 2)
+    def _(t):
+        @pl.when(t < pairs)
+        def _():
+            p = jnp.minimum(t, pairs - 1)
+            lanes, value_lanes = pair_lanes(p), pair_lanes(pairs + p)
+            do_both = head_stack(doc_ref[:, lanes])
+            weights = prob[p]
+            wide = weights.astype(F32)
+            dp = nt(kv_all[:, value_lanes], do_both)
+            ds_wide = wide * (dp - jnp.sum(wide * dp, axis=0, keepdims=True))
+            ds = ds_wide.astype(BF16)
+            ds_ref[pl.ds(rows, span), :] = ds
+            total_ref[pl.ds(p, 1), :] = jnp.sum(ds.astype(F32), axis=0, keepdims=True)
+            dk = nn(ds, head_stack(q_ref[:, lanes])).astype(BF16).reshape(chips, 2, rows, LANES)
+            dv = nn(weights, do_both).astype(BF16).reshape(chips, 2, rows, LANES)
+            for k in range(2):
+                t_out[p, k, :, :, :LANES] = dk[:, k]
+                t_out[p, k, :, :, LANES:] = dv[:, k]
+            pair_copy(p).start()
+            dqkv_ref[:, lanes] = (head_unstack(tn(kv_all[:, lanes], ds), rows) * 0.125).astype(BF16)
+            turned = nn(flip, ds_ref[near, :])
+            for h in range(2):
+                one = turned[:, h * rows : (h + 1) * rows]
+                one = jnp.concatenate([one, jnp.zeros_like(one)], axis=1)
+                one = pltpu.roll(one, 1, 1, stride=1, stride_axis=0)
+                diag_ref[pl.ds(2 * p + h, 1), :] = jnp.sum(one, axis=0, keepdims=True)
+
+        @pl.when((t >= 1) & (t <= pairs))
+        def _():
+            p = jnp.clip(t - 1, 0, pairs - 1)
+            pair_copy(p).wait_recv()
+            t_out[p, core] = (t_out[p, core].astype(F32) + t_pair[p].astype(F32)).astype(BF16)
+            for copy in chip_copies(p):
+                copy.start()
+
+        @pl.when(t >= 2)
+        def _():
+            p = jnp.clip(t - 2, 0, pairs - 1)
+            total = t_out[p, core, chip].astype(F32)
+            for d, copy in enumerate(chip_copies(p)):
+                copy.wait_recv()
+                total = total + t_chip[p, d].astype(F32)
+            dqkv_ref[:, pair_lanes(pairs + p)] = total[:, :LANES].astype(BF16)
+            dqkv_ref[:, pair_lanes(2 * pairs + p)] = total[:, LANES:].astype(BF16)
+
+    dqkv = dqkv_ref[...]
+    loads[7].wait()
+    x = x_ref[...].astype(F32)
+    da, dw = rms_back(x, gains_ref[0:1, :], nt(dqkv, w_qkv[...]))
+    small_ref[0:1, :] = dw
+    dx_ref[...] = dr_ref[...] + da
+    dqkv_t_ref[...] = dqkv.T
+
+    heads = 2 * pairs
+    table = diag_ref[:, 2 * rows - LANES :]
+    totals = total_ref[...]
+    first = jnp.sum(totals[:, :rows], axis=1, keepdims=True)
+    second = jnp.sum(totals[:, rows:], axis=1, keepdims=True)
+    head = lax.broadcasted_iota(jnp.int32, (heads, pairs), 0)
+    pair = lax.broadcasted_iota(jnp.int32, (heads, pairs), 1)
+    spread = lambda odd, v: jnp.dot((head == 2 * pair + odd).astype(F32), v, precision=highest, preferred_element_type=F32)
+    whole = spread(0, jnp.broadcast_to(first, (pairs, LANES))) + spread(1, jnp.broadcast_to(second, (pairs, LANES)))
+    rest = whole - jnp.sum(table, axis=1, keepdims=True)
+    lane = lax.broadcasted_iota(jnp.int32, table.shape, 1)
+    table = table + jnp.where(lane == LANES - 1, rest, 0.0)
+    bucket = lax.broadcasted_iota(jnp.int32, (LANES, LANES), 0)
+    pick = (buckets_ref[...] == bucket).astype(F32)
+    small_ref[8 : 8 + heads, :LANES] = lax.dot_general(
+        table, pick, (((1,), (1,)), ((), ())), precision=highest, preferred_element_type=F32
+    )
+
+    total = e_out[core, chip].astype(F32)
+    for d, copy in enumerate(e_chip_copies):
+        copy.wait_recv()
+        total = total + e_chip[d].astype(F32)
+    e_mine[...] = total.astype(BF16).reshape(e_mine.shape)
+    e_exp_copies = [
+        remote(e_mine.at[peer], e_exp.at[d], ee_send.at[d], ee_recv.at[d], {"exp": peer}) for d, peer in enumerate(peers)
+    ]
+    for copy in e_exp_copies:
+        copy.start()
+    square_sum(2, co_chips)
+    square_sum(1, cq_chips)
+    square_sum(0, so_chips)
+    total = e_mine[mine].astype(F32)
+    for d, copy in enumerate(e_exp_copies):
+        copy.wait_recv()
+        total = total + e_exp[d].astype(F32)
+    dekv_ref[...] = total.astype(BF16)
+
+    for copy in [co_pair, cq_pair, so_pair, e_pair_copy] + co_chips + cq_chips + so_chips + e_chip_copies + e_exp_copies:
+        copy.wait_send()
+
+    @pl.loop(0, pairs)
+    def _(p):
+        pair_copy(p).wait_send()
+        for copy in chip_copies(p):
+            copy.wait_send()
+
+
+def backward_call(seq_count, experts, made, dxb, g, x, r1, r2, gates, place, routes, x3, n2, o, oc, q, qc, gains, router,
+                  buckets, kv, p, pc, ekv, co, cq, so, qkv):
+    rows, width = x.shape
+    span = seq_count * rows
+    pairs = width // LANES
+    chips = seq_count // 2
+    enc_rows = ekv.shape[0]
+    part = 3 * width // seq_count
+    enc_part = enc_rows // seq_count
+    shape = jax.ShapeDtypeStruct
+    dma = lambda *n: pltpu.SemaphoreType.DMA(n)
+    vmem = pltpu.VMEM
+    return pl.pallas_call(
+        functools.partial(backward_kernel, seq_count, experts),
+        out_shape=(
+            shape((rows, width), BF16), shape((rows, width), F32), shape((3 * width, rows), BF16), shape((part, width), BF16),
+            shape((enc_part // experts, 2 * width), BF16), shape((24, width), F32),
+        ),
+        in_specs=[VMEM] * 18 + [ANY] * 8,
+        out_specs=(VMEM,) * 6,
+        scratch_shapes=[
+            vmem((span, 2 * width), BF16), vmem((pairs, span, 2 * rows), BF16), vmem((pairs, enc_rows, 2 * rows), BF16),
+            vmem((enc_rows, 2 * width), BF16), vmem(co.shape, BF16), vmem(cq.shape, BF16), vmem(so.shape, BF16),
+            vmem(qkv.shape, BF16), vmem((rows, width), F32), vmem((rows, width), BF16), vmem((rows, width), BF16),
+            vmem((rows, 3 * width), BF16), vmem((span + rows, 2 * rows), BF16), vmem((2 * pairs, 2 * rows), F32),
+            vmem((pairs, 2 * rows), F32),
+            vmem((2, chips, enc_part, 2 * width), BF16), vmem((chips, enc_part, 2 * width), BF16),
+            vmem((chips - 1, enc_part, 2 * width), BF16), vmem((experts, enc_part // experts, 2 * width), BF16),
+            vmem((experts - 1, enc_part // experts, 2 * width), BF16),
+            vmem((pairs, 2, chips, rows, 2 * LANES), BF16), vmem((pairs, chips, rows, 2 * LANES), BF16),
+            vmem((pairs, chips - 1, rows, 2 * LANES), BF16),
+            vmem((2, chips, part, width), BF16), vmem((chips, part, width), BF16), vmem((chips - 1, part, width), BF16),
+            dma(8), dma(1), dma(1), dma(chips - 1), dma(chips - 1), dma(experts - 1), dma(experts - 1), dma(pairs), dma(pairs),
+            dma(pairs, chips - 1), dma(pairs, chips - 1), dma(3), dma(3), dma(3, chips - 1), dma(3, chips - 1),
+        ],
+        compiler_params=pltpu.CompilerParams(collective_id=2, has_side_effects=True, vmem_limit_bytes=60 << 20),
+        name="backward",
+    )(made, dxb, g, x, r1, r2, gates, place, routes, x3, n2, o, oc, q, qc, gains, router, buckets, kv, p, pc, ekv, co, cq, so, qkv)
+
+
+def weights_kernel(
+    seq_count, experts,
+    dqkv_t_ref, squares_ref, dekv_ref, small_ref, n1_hbm, x_hbm, dm_hbm, w_in_hbm, w_out_hbm, ckv_hbm,
+    square_out_ref, qkv_out_ref, dekv_out_ref, small_out_ref, gin_ref, gout_ref, genc_ref,
+    n1_all, x_all, dm_all, w_in, w_out, w_ckv, right, turned, mine_q, sq_slots, q_slots, sq_all, q_all, dekv_all, gin_out, gin_in,
+    small_a, small_b, small_c, small_pair, small_chip, small_exp,
+    load_sem, r_send, r_recv, sz_send, sz_recv, sg_send, sg_recv, sa_send, sa_recv, qz_send, qz_recv, qg_send, qg_recv,
+    qa_send, qa_recv, ez_send, ez_recv, ea_send, ea_recv, g_send, g_recv, s1_send, s1_recv, s2_send, s2_recv, s3_send, s3_recv,
+):
+    chips = seq_count // 2
+    part, width = squares_ref.shape
+    rows = dqkv_t_ref.shape[1]
+    me = lax.axis_index("seq")
+    mine = lax.axis_index("exp")
+    core, chip, partner, others, sources = seq_peers(me, chips)
+    peers = expert_peers(mine, experts)
+    everyone = [lax.rem(me + d, seq_count) for d in range(1, seq_count)]
+    hidden = w_in.shape[1]
+    at_hidden = pl.ds(pl.multiple_of(me * hidden, hidden), hidden)
+    loads = [
+        pltpu.make_async_copy(src, dst, load_sem.at[i])
+        for i, (src, dst) in enumerate(
+            [(n1_hbm, n1_all), (x_hbm, x_all), (w_in_hbm.at[:, at_hidden], w_in), (dm_hbm, dm_all),
+             (w_out_hbm.at[at_hidden, :], w_out), (ckv_hbm, w_ckv)]
+        )
+    ]
+    for load in loads:
+        load.start()
+    enter([{"seq": device} for device in everyone] + [{"exp": peer} for peer in peers])
+    started = []
+
+    def send(src, dst, send_sem, recv_sem, device):
+        copy = remote(src, dst, send_sem, recv_sem, device)
+        copy.start()
+        started.append(copy)
+        return copy
+
+    own_lanes = pl.ds(pl.multiple_of(me * rows, rows), rows)
+    own_rows = pl.ds(pl.multiple_of(me * part, part), part)
+    rights = [
+        send(dqkv_t_ref.at[pl.ds(pl.multiple_of(peer * part, part), part), :], right.at[:, own_lanes], r_send.at[d], r_recv.at[d],
+             {"seq": peer})
+        for d, peer in enumerate(everyone)
+    ]
+    right[:, own_lanes] = dqkv_t_ref[own_rows, :]
+
+    half_rows, half_lanes = part // 2, width // (experts // 2)
+
+    def quarter(e):
+        return (
+            pl.ds(pl.multiple_of(lax.div(e, experts // 2) * half_rows, half_rows), half_rows),
+            pl.ds(pl.multiple_of(lax.rem(e, experts // 2) * half_lanes, half_lanes), half_lanes),
+        )
+
+    def scatter_exp(src, slots, sends, recvs):
+        return [
+            send(src.at[quarter(peer)], slots.at[d], sends.at[d], recvs.at[d], {"exp": peer}) for d, peer in enumerate(peers)
+        ]
+
+    def gather_exp(src, slots, copies, every, sends, recvs):
+        total = src[quarter(mine)].astype(F32)
+        for d, copy in enumerate(copies):
+            copy.wait_recv()
+            total = total + slots[d].astype(F32)
+        block = (me,) + quarter(mine)
+        every[block] = total.astype(BF16)
+        return [
+            send(every.at[block], every.at[block], sends.at[d], recvs.at[d], {"exp": peer}) for d, peer in enumerate(peers)
+        ]
+
+    def gather_seq(every, block, copies, sends, recvs):
+        for copy in copies:
+            copy.wait_recv()
+        return [send(every.at[block], every.at[block], sends.at[d], recvs.at[d], {"seq": others[d - 1]}) for d in range(1, chips)] + [
+            send(every.at[block], every.at[block], sends.at[0], recvs.at[0], {"seq": partner})
+        ]
+
+    def pass_on(every, copies, sends, recvs):
+        forwards = []
+        for d in range(1, chips):
+            copies[d - 1].wait_recv()
+            block = every.at[sources[d - 1]]
+            forwards.append(send(block, block, sends.at[chips - 1 + d], recvs.at[chips - 1 + d], {"seq": partner}))
+        return forwards
+
+    sq_scatter = scatter_exp(squares_ref, sq_slots, sz_send, sz_recv)
+    dekv_all[me, mine] = dekv_ref[...]
+    e_exp = [
+        send(dekv_all.at[me, mine], dekv_all.at[me, mine], ez_send.at[d], ez_recv.at[d], {"exp": peer})
+        for d, peer in enumerate(peers)
+    ]
+    small_a[...] = small_ref[...]
+    s_pair = send(small_a, small_pair, s1_send.at[0], s1_recv.at[0], {"seq": partner})
+
+    for load in loads[:1]:
+        load.wait()
+    for copy in rights:
+        copy.wait_recv()
+    turned[...] = nn(right[...], n1_all[...].reshape(seq_count * rows, width)).astype(BF16)
+    q_scatter = scatter_exp(turned, q_slots, qz_send, qz_recv)
+    sq_gather = gather_exp(squares_ref, sq_slots, sq_scatter, sq_all, sg_send, sg_recv)
+    e_seq = gather_seq(dekv_all, me, e_exp, ea_send, ea_recv)
+    s_pair.wait_recv()
+    small_b[...] = small_a[...] + small_pair[...]
+    s_chip = [
+        send(small_b, small_chip.at[d], s2_send.at[d], s2_recv.at[d], {"seq": others[d]}) for d in range(chips - 1)
+    ]
+
+    for load in loads[1:5]:
+        load.wait()
+    x = x_all[...].reshape(-1, width)
+    value, slope = gelu_parts(nn(x, w_in[...]))
+    dm = dm_all[...].reshape(-1, width)
+    gout_ref[...] = tn(value.astype(BF16), dm)
+    sq_seq = gather_seq(sq_all, me, sq_gather, sa_send, sa_recv)
+    dh = (nt(dm, w_out[...]) * slope).astype(BF16)
+    gin_out[...] = tn(x, dh).astype(BF16).reshape(gin_out.shape)
+    gins = [
+        send(gin_out.at[peer], gin_in.at[:, at_hidden], g_send.at[d], g_recv.at[d], {"seq": peer})
+        for d, peer in enumerate(everyone)
+    ]
+    gin_in[:, at_hidden] = gin_out[me]
+    q_gather = gather_exp(turned, q_slots, q_scatter, q_all, qg_send, qg_recv)
+    e_forwards = pass_on(dekv_all, e_seq, ea_send, ea_recv)
+    loads[5].wait()
+    genc_ref[...] = nt(dekv_ref[...], w_ckv[...])
+    total = small_b[...]
+    for d, copy in enumerate(s_chip):
+        copy.wait_recv()
+        total = total + small_chip[d]
+    small_c[...] = total
+    s_exp = [send(small_c, small_exp.at[d], s3_send.at[d], s3_recv.at[d], {"exp": peer}) for d, peer in enumerate(peers)]
+    q_seq = gather_seq(q_all, me, q_gather, qa_send, qa_recv)
+    sq_forwards = pass_on(sq_all, sq_seq, sa_send, sa_recv)
+    total = small_c[...]
+    for d, copy in enumerate(s_exp):
+        copy.wait_recv()
+        total = total + small_exp[d]
+    small_out_ref[...] = total
+    for copy in gins:
+        copy.wait_recv()
+    gin_ref[...] = gin_in[...]
+    e_seq[-1].wait_recv()
+    for copy in e_forwards:
+        copy.wait_recv()
+    dekv_out_ref[...] = dekv_all[...]
+    sq_seq[-1].wait_recv()
+    for copy in sq_forwards:
+        copy.wait_recv()
+    square_out_ref[...] = sq_all[...]
+    q_forwards = pass_on(q_all, q_seq, qa_send, qa_recv)
+    q_seq[-1].wait_recv()
+    for copy in q_forwards:
+        copy.wait_recv()
+    qkv_out_ref[...] = q_all[...]
+    for copy in started:
+        copy.wait_send()
+
+
+def weights_call(seq_count, experts, dqkv_t, squares, dekv, small, n1_all, x_all, dm_all, w_in, w_out, ckv):
+    part, width = squares.shape
+    chips = seq_count // 2
+    hidden = w_in.shape[1] // seq_count
+    shape = jax.ShapeDtypeStruct
+    vmem = pltpu.VMEM
+    dma = lambda n: pltpu.SemaphoreType.DMA((n,))
+    every = (seq_count, part, width)
+    every_e = (seq_count, experts) + dekv.shape
+    d_part = width // seq_count
+    z, c, a = experts - 1, chips - 1, 2 * chips - 1
+    return pl.pallas_call(
+        functools.partial(weights_kernel, seq_count, experts),
+        out_shape=(
+            shape(every, BF16), shape(every, BF16), shape(every_e, BF16), shape(small.shape, F32),
+            shape((d_part, w_in.shape[1]), BF16), shape((hidden, width), F32), shape((dekv.shape[0], width), F32),
+        ),
+        in_specs=[VMEM] * 4 + [ANY] * 6,
+        out_specs=(VMEM,) * 7,
+        scratch_shapes=[
+            vmem(n1_all.shape, BF16), vmem(x_all.shape, BF16), vmem(dm_all.shape, BF16), vmem((width, hidden), BF16),
+            vmem((hidden, width), BF16), vmem(ckv.shape, BF16), vmem((part, seq_count * dqkv_t.shape[1]), BF16),
+            vmem((part, width), BF16), vmem((8, 128), BF16), vmem((z, part // 2, width // (experts // 2)), BF16),
+            vmem((z, part // 2, width // (experts // 2)), BF16), vmem(every, BF16), vmem(every, BF16), vmem(every_e, BF16),
+            vmem((seq_count, d_part, hidden), BF16), vmem((d_part, w_in.shape[1]), BF16),
+            vmem(small.shape, F32), vmem(small.shape, F32), vmem(small.shape, F32), vmem(small.shape, F32),
+            vmem((c,) + small.shape, F32), vmem((z,) + small.shape, F32),
+            dma(6), dma(seq_count - 1), dma(seq_count - 1), dma(z), dma(z), dma(z), dma(z), dma(a), dma(a),
+            dma(z), dma(z), dma(z), dma(z), dma(a), dma(a), dma(z), dma(z), dma(a), dma(a),
+            dma(seq_count - 1), dma(seq_count - 1), dma(1), dma(1), dma(c), dma(c), dma(z), dma(z),
+        ],
+        compiler_params=pltpu.CompilerParams(collective_id=3, has_side_effects=True, vmem_limit_bytes=60 << 20),
+        name="weights",
+    )(dqkv_t, squares, dekv, small, n1_all, x_all, dm_all, w_in, w_out, ckv)
+
+
+def finish_kernel(
+    experts, square_ref, qkv_ref, dekv_ref, small_ref, gin_ref, gout_ref, genc_ref, layer_ref, dx_ref, enc_ref,
+    layer_out, dx_out, genc_out, gains_out, qkv_hbm, so_hbm, cq_hbm, ckv_hbm, co_hbm, rel_out, router_out, gin_out, gout_out,
+    squares, qkv, ckv, sem,
+):
+    seq_count, part, width = square_ref.shape
+    each = part // 3
+    copies = []
+
+    def store(src, dst):
+        copy = pltpu.make_async_copy(src, dst, sem.at[len(copies)])
+        copy.start()
+        copies.append(copy)
+
+    for i, out in enumerate((so_hbm, cq_hbm, co_hbm)):
+        for s in range(seq_count):
+            squares[i, s * each : (s + 1) * each, :] = square_ref[s, i * each : (i + 1) * each, :].astype(F32)
+        store(squares.at[i], out)
+    flat = qkv_ref[...].reshape(seq_count * part, width)
+    for n in range(3):
+        for block in range(width // LANES):
+            at = slice(n * width + block * LANES, n * width + (block + 1) * LANES)
+            qkv[:, at] = flat[at, :].astype(F32).T
+        at = slice(n * width, (n + 1) * width)
+        store(qkv.at[:, at], qkv_hbm.at[:, at])
+    dekv = dekv_ref[...].reshape(-1, 2 * width)
+    for n in range(2):
+        at = slice(n * width, (n + 1) * width)
+        ckv[:, at] = tn(enc_ref[...], dekv[:, at])
+        store(ckv.at[:, at], ckv_hbm.at[:, at])
+    layer_out[...] = layer_ref[...]
+    dx_out[...] = dx_ref[...]
+    genc_out[...] = genc_ref[...]
+    gains_out[...] = small_ref[0:3, :]
+    router_out[...] = small_ref[4 : 4 + experts, :].T
+    heads, buckets = rel_out.shape[1], rel_out.shape[0]
+    rel_out[...] = small_ref[8 : 8 + heads, :buckets].T
+    gin_out[...] = gin_ref[...].astype(F32)
+    gout_out[...] = gout_ref[...]
+    for copy in copies:
+        copy.wait()
+
+
+def finish_call(experts, buckets, square, qkv, dekv, small, gin, gout, genc, layer, dx, enc):
+    seq_count, part, width = square.shape
+    shape = jax.ShapeDtypeStruct
+    return pl.pallas_call(
+        functools.partial(finish_kernel, experts),
+        out_shape=(
+            shape(layer.shape, BF16), shape(dx.shape, F32), shape(genc.shape, F32), shape((3, width), F32),
+            shape((width, 3 * width), F32), shape((width, width), F32), shape((width, width), F32), shape((width, 2 * width), F32),
+            shape((width, width), F32), shape((buckets, width // HD), F32), shape((width, experts), F32), shape(gin.shape, F32),
+            shape(gout.shape, F32),
+        ),
+        in_specs=[VMEM] * 10,
+        out_specs=(VMEM,) * 4 + (ANY,) * 5 + (VMEM,) * 4,
+        scratch_shapes=[
+            pltpu.VMEM((3, width, width), F32), pltpu.VMEM((width, 3 * width), F32), pltpu.VMEM((width, 2 * width), F32),
+            pltpu.SemaphoreType.DMA((8,)),
+        ],
+        compiler_params=pltpu.CompilerParams(vmem_limit_bytes=60 << 20),
+        name="finish",
+    )(square, qkv, dekv, small, gin, gout, genc, layer, dx, enc)
+
+
 def fused(inputs, encoder, lengths, buckets, routes, norm_gains, self_qkv, self_out, cross_q, cross_kv, cross_out,
           rel_bias, router, expert_in, expert_out, cotangent):
     seq_count = lax.axis_size("seq")
-    seq_index = lax.axis_index("seq")
     rows, width = inputs.shape[1:]
     experts = router.shape[1]
     capacity = 5 * rows // (4 * experts)
@@ -725,80 +1437,17 @@
     (n1_all, kv_all, prob, cross_prob, ekv, q, o, n2, qc, oc, x3, r1, r2, gates, place, xs, dms) = forward_call(
         seq_count, capacity, stride, inputs[0], encoder, lengths, buckets[None, :], routes[0], norm_gains, self_qkv,
         self_out, cross_q, cross_kv, cross_out, rel_bias, router, cotangent[0])
-    pairs = width // LANES
-    hidden = inputs[0].astype(F32)
-    upstream = cotangent[0].astype(F32)
-    a2a = lambda v: lax.all_to_all(v.reshape(experts, stride, width), "exp", split_axis=0, concat_axis=0, tiled=True)
-    arrived = a2a(xs).reshape(-1, width)
-    grad_arrived = a2a(dms).reshape(-1, width)
-    hid, gelu_back = jax.vjp(lambda v: jax.nn.gelu(v, approximate=True), nn(arrived, expert_in[0]))
-    act = hid.astype(BF16)
-    made = nn(act, expert_out[0]).astype(BF16)
-    expert_rows = nn(place, a2a(made).reshape(-1, width))
-    chosen = (routes[0] == jnp.arange(experts)[None, :])
-    picked = jnp.sum(jnp.where(chosen, gates, 0.0), axis=1, keepdims=True)
-    kept = jnp.sum(place.astype(F32), axis=1, keepdims=True)
-    layer_out = r2 + picked * kept * expert_rows
-    dh = gelu_back(nt(grad_arrived, expert_out[0]))[0].astype(BF16)
-    gout = tn(act, grad_arrived)
-    gin = tn(arrived, dh)
-    dx3 = nn(place, a2a(nt(dh, expert_in[0]).astype(BF16)).reshape(-1, width))
-    expert_sums = (
-        lax.psum_scatter(gin[None], "seq", scatter_dimension=1, tiled=True),
-        lax.psum_scatter(gout[None], "seq", scatter_dimension=1, tiled=True),
-    )
-    gate_grad = jnp.sum(upstream * expert_rows, axis=1, keepdims=True) * kept
-    dl = gates * (jnp.where(chosen, gate_grad, 0.0) - picked * gate_grad)
-    router_grad = jnp.dot(x3.astype(F32).T, dl, precision=highest)
-    dx3 = dx3 + jnp.dot(dl, router.astype(F32).T, precision=highest)
-    _, back3 = jax.vjp(rms_norm, r2, norm_gains[2])
-    dr2, gain3 = back3(dx3)
-    dr2 = dr2 + upstream
-    do2 = dr2.astype(BF16)
-    cross_out_grad = tn(oc, do2)
-    doc2 = nt(do2, cross_out).astype(BF16)
-    heads = lambda v: v.reshape(v.shape[0], H, HD)
-    unstack = lambda v: v.reshape(pairs, -1, 2, rows).transpose(0, 2, 1, 3).reshape(H, -1, rows)
-    pc = unstack(cross_prob).astype(F32)
-    kc, vc = heads(ekv[:, :width]), heads(ekv[:, width:])
-    dp = jnp.einsum("qhd,khd->hkq", heads(doc2), vc, preferred_element_type=F32)
-    dc = (pc * (dp - jnp.sum(pc * dp, axis=1, keepdims=True))).astype(BF16)
-    dqc = (jnp.einsum("hkq,khd->qhd", dc, kc, preferred_element_type=F32) * 0.125).reshape(rows, width).astype(BF16)
-    dkc = jnp.einsum("hkq,qhd->khd", dc, heads(qc), preferred_element_type=F32).reshape(-1, width)
-    dvc = jnp.einsum("hkq,qhd->khd", pc.astype(BF16), heads(doc2), preferred_element_type=F32).reshape(-1, width)
-    dekv = lax.psum_scatter(jnp.concatenate([dkc, dvc], axis=1), ("seq", "exp"), scatter_dimension=0, tiled=True).astype(BF16)
-    enc_count = dekv.shape[0]
-    flat_index = seq_index * lax.axis_size("exp") + lax.axis_index("exp")
-    own_enc = lax.dynamic_slice_in_dim(encoder, flat_index * enc_count, enc_count, 0)
-    grad_encoder = nt(dekv, cross_kv)
-    pair_grad = tn(own_enc, dekv)
-    cq_grad = tn(n2, dqc)
-    _, back2 = jax.vjp(rms_norm, r1, norm_gains[1])
-    dr1, gain2 = back2(nt(dqc, cross_q))
-    dr1 = dr1 + dr2
-    do1 = dr1.astype(BF16)
-    self_out_grad = tn(o, do1)
-    dob = nt(do1, self_out).astype(BF16)
-    pr = unstack(prob).astype(F32)
-    k, v = heads(kv_all[:, :width]), heads(kv_all[:, width:])
-    dp = jnp.einsum("qhd,khd->hkq", heads(dob), v, preferred_element_type=F32)
-    ds = (pr * (dp - jnp.sum(pr * dp, axis=1, keepdims=True))).astype(BF16)
-    dq = (jnp.einsum("hkq,khd->qhd", ds, k, preferred_element_type=F32) * 0.125).reshape(rows, width).astype(BF16)
-    dk = jnp.einsum("hkq,qhd->khd", ds, heads(q), preferred_element_type=F32).reshape(-1, width)
-    dv = jnp.einsum("hkq,qhd->khd", pr.astype(BF16), heads(dob), preferred_element_type=F32).reshape(-1, width)
-    dkv = lax.psum_scatter(jnp.concatenate([dk, dv], axis=1), "seq", scatter_dimension=0, tiled=True).astype(BF16)
-    distance = jnp.clip(seq_index * rows + jnp.arange(rows)[None, :] - jnp.arange(seq_count * rows)[:, None], 0, 127)
-    table_grad = jax.vmap(lambda d: jnp.zeros((128,), F32).at[distance.reshape(-1)].add(d.reshape(-1).astype(F32)))(ds)
-    bucket_pick = (buckets[:, None] == jnp.arange(rel_bias.shape[0])[None, :]).astype(F32)
-    rel_grad = jnp.dot(bucket_pick.T, table_grad.T, precision=highest)
-    dqkv = jnp.concatenate([dq, dkv], axis=1)
-    qkv_grad = tn(n1_all[seq_index], dqkv)
-    _, back1 = jax.vjp(rms_norm, hidden, norm_gains[0])
-    dx, gain1 = back1(nt(dqkv, self_qkv))
-    grad_input = dx + dr1
-    summed = lax.psum((jnp.stack([gain1, gain2, gain3]), qkv_grad, self_out_grad, cq_grad, pair_grad, cross_out_grad,
-                       rel_grad, router_grad), ("seq", "exp"))
-    return (layer_out.astype(BF16)[None], grad_input[None], grad_encoder, *summed, *expert_sums)
+    made, dxb, x_all, dm_all = experts_call(seq_count, experts, stride, xs, dms, expert_in[0], expert_out[0])
+    (layer_out, grad_input, dqkv_t, squares, dekv, small) = backward_call(
+        seq_count, experts, made.reshape(-1, width), dxb.reshape(-1, width), cotangent[0], inputs[0], r1, r2, gates, place,
+        routes[0], x3, n2, o, oc, q, qc, norm_gains, router, buckets[None, :], kv_all, prob, cross_prob, ekv, cross_out,
+        cross_q, self_out, self_qkv)
+    square_all, qkv_all, dekv_all, small, gin, gout, grad_encoder = weights_call(
+        seq_count, experts, dqkv_t, squares, dekv, small, n1_all, x_all, dm_all, expert_in[0], expert_out[0], cross_kv)
+    (layer_out, grad_input, grad_encoder, gains, g_qkv, g_so, g_cq, g_ckv, g_co, g_rel, g_router, gin, gout) = finish_call(
+        experts, rel_bias.shape[0], square_all, qkv_all, dekv_all, small, gin, gout, grad_encoder, layer_out, grad_input, encoder)
+    return (layer_out[None], grad_input[None], grad_encoder, gains, g_qkv, g_so, g_cq, g_ckv, g_co, g_rel, g_router,
+            gin[None], gout[None])
 
 
 def on_device(*operands):

time: 1300 us -> 257 us (0.20)
  other arithmetic: 906 us -> 0 us
  Pallas kernels: 32.4 us -> 248 us
  waiting for transfers between devices: 119 us -> 0 us
  local copies, waits for them, and re-layouts: 83.5 us -> 7.43 us
  matrix products: 72.6 us -> 0 us
  blocking collectives: 40.6 us -> 0 us
  starting transfers between devices: 20.5 us -> 0 us
  between operations: 14.8 us -> 0.69 us
    scatter-add x1 -> x0, other arithmetic: 885 us -> none  [fused(): jnp.zeros((128,), F32).at[distance.reshape(-1)]]
    pallas_call x0 -> x4, Pallas kernels: none -> 215 us  [the longest x1 88.6 us: weights_call(): pl.pallas_call(functools.partial(weights_kernel, seq_count, experts), out...]
    dot_general x29 -> x0, matrix products: 72.6 us -> none  [the longest x7 29.8 us: tn(): lax.dot_general(a, b, (((0,), (0,)), ((), ())), preferred_element_type=F32)]
    reduce_scatter x3 -> x0, waiting for transfers between devices: 58.8 us -> none  [the longest x1 58.8 us: fused(): lax.psum_scatter(jnp.concatenate([dk, dv], axis=1), 'seq', scatter_dimens...]
    unnamed x6 -> x0, waiting for transfers between devices: 53.3 us -> none
    psum x1 -> x0, blocking collectives: 40.6 us -> none  [fused(): lax.psum((jnp.stack([gain1, gain2, gain3]), qkv_grad, self_out_grad, cq_g...]
    convert_element_type x3 -> x0, local copies, waits for them, and re-layouts: 31.5 us -> none  [the longest x1 28.6 us: fused(): d.reshape(-1).astype(F32)]
    unnamed x115 -> x4, local copies, waits for them, and re-layouts: 34.5 us -> 6.05 us
  transfers between devices with their start and end apart: 9 -> 0, of which waited for: 4 -> 0; matrix products, arithmetic and copies ran while one was open for 79% -> 0% of each run, Pallas kernels for 0% -> 0%
where the time goes in v2:
time: 257 us; the launch traced here: 256 us
  Pallas kernels  248 us (96%)
  local copies, waits for them, and re-layouts  7.43 us (3%)
    pallas_call x1, Pallas kernels, weights_call(): pl.pallas_call(functools.partial(weights_kernel, seq_count, experts), out...  88.6 us
    pallas_call x1, Pallas kernels, backward_call(): pl.pallas_call(functools.partial(backward_kernel, seq_count, experts), ou...  70.7 us
    pallas_call x1, Pallas kernels, experts_call(): pl.pallas_call(functools.partial(experts_kernel, seq_count, experts, stri...  42.6 us
    pallas_call x1, Pallas kernels, forward_call(): pl.pallas_call(functools.partial(forward_kernel, seq_count, capacity, str...  32.4 us
    pallas_call x1, Pallas kernels, finish_call(): pl.pallas_call(functools.partial(finish_kernel, experts), out_shape=(shap...  13.4 us
    unnamed x4, local copies, waits for them, and re-layouts  6.05 us

profile of v2, /device:TPU:0, one launch (start us, length us, event | category | flops | bytes accessed | tf_op | source)
XLA Modules:
  0.0 255.7 jit_solution(5655116131562414660)
XLA Ops:
  0.6 1.4 copy.30.rel_ref
  2.0 1.4 copy.29.routes_ref
  3.4 1.5 copy.31.router_ref
  4.9 32.4 %forward.1 = (bf16[8,128,768]{2,1,0:T(8,128)(2,1)}, bf16[1024,1536]{1,0:T(8,128)(2,1)}, bf16[6,1024,256]{2,1,0:T(8,128)(2,1)}, bf16[6,512,256]{2,1,0:T(8,128)(2,...) custom-call(bf16[128,768]{1,0:T(8,128)(2,1)} %bitcast.18, ...), custom_call_target="tpu_custom_call" | custom-call | tf_op jit(solution)/shard_map/forward/pallas_call | solution.py:697
  37.3 42.6 %experts.1 = (bf16[4,48,768]{2,1,0:T(8,128)(2,1)}, bf16[4,48,768]{2,1,0:T(8,128)(2,1)}, bf16[8,4,48,768]{3,2,1,0:T(8,128)(2,1)}, bf16[8,4,48,768]{3,2,1,0:T(8,128)(2,1)}) custom-call(bf16[4,48,768]{2,1,0:T(8,128)(2,1)} %bitcast.22, bf16[4,48,768]{2,1,0:T(8,128)(2,1)} %bitcast.23, bf16[768,3072]{1,0:T(8,128)(2,1)} %bitcast.14, bf16[3072,768]{1,0:T(8,128)(2,1)} %bitcast.16), custom_call_target="tpu_custom_call" | custom-call | tf_op jit(solution)/shard_map/experts/pallas_call | solution.py:852
  79.9 70.7 %backward.1 = (bf16[128,768]{1,0:T(8,128)(2,1)}, f32[128,768]{1,0:T(8,128)}, bf16[2304,128]{1,0:T(8,128)(2,1)}, bf16[288,768]{1,0:T(8,128)(2,1)}, bf16[16,1536]{1,0:T(8,128)(2,1)}, /*index=5*/f32[24,768]{1,0:T(8,128)}) custom-call(bf16[192,768]{1,0:T(8,128)(2,1)} %bitcast.24, bf16[192,768]{1,0:T(8,128)(2,1)} %bitcast.25, bf16[128,768]{1,0:T(8,128)(2,1)} %bitcast.21, ...), custom_call_target="tpu_custom_call" | custom-call | tf_op jit(solution)/shard_map/backward/pallas_call | solution.py:1142
  150.6 88.6 %weights.1 = (bf16[8,288,768]{2,1,0:T(8,128)(2,1)}, bf16[8,288,768]{2,1,0:T(8,128)(2,1)}, bf16[8,4,16,1536]{3,2,1,0:T(8,128)(2,1)}, f32[24,768]{1,0:T(8,128)}, b...) custom-call(bf16[2304,128]{1,0:T(8,128)(2,1)} %get-tuple-element.78.dqkv_t_ref, ...), custom_call_target="tpu_custom_call" | custom-call | tf_op jit(solution)/shard_map/weights/pallas_call | solution.py:1340
  239.2 13.4 %finish.1 = (bf16[128,768]{1,0:T(8,128)(2,1)}, f32[128,768]{1,0:T(8,128)}, f32[16,768]{1,0:T(8,128)}, f32[3,768]{1,0:T(4,128)}, f32[768,2304]{1,0:T(8,128)}, /*i...) custom-call(bf16[8,288,768]{2,1,0:T(8,128)(2,1)} %get-tuple-element., ...), custom_call_target="tpu_custom_call" | custom-call | tf_op jit(solution)/shard_map/finish/pallas_call | solution.py:1411
  252.6 1.4 copy.34
  254.0 1.7 copy.35

commit v3 on v1

--- a/solution.py
+++ b/solution.py
@@ -485,6 +485,10 @@
     return pl.ds(pl.multiple_of(p * LANES, LANES), LANES)
 
 
+def block_of(index, size):
+    return pl.ds(pl.multiple_of(index * size, size), size)
+
+
 def head_stack(pair):
     lane = lax.broadcasted_iota(jnp.int32, pair.shape, 1)
     zero = jnp.zeros_like(pair)
@@ -496,13 +500,39 @@
     return jnp.where(feature < HD, both[:, :rows], both[:, rows:]).T
 
 
-def seq_peers(seq_index, chips):
-    core = lax.rem(seq_index, 2)
-    chip = lax.div(seq_index, 2)
-    partner = seq_index + 1 - 2 * core
-    others = [lax.rem(chip + d, chips) * 2 + core for d in range(1, chips)]
-    sources = [lax.rem(chip - d + chips, chips) * 2 + core for d in range(1, chips)]
-    return core, chip, partner, others, sources
+def pack_slots(value, experts):
+    slots = value.shape[0] // experts
+    blocks = value.shape[1] // LANES
+    return jnp.stack([
+        jnp.concatenate(
+            [value[e * slots : (e + 1) * slots, b * LANES : (b + 1) * LANES] for b in range(blocks)], axis=0
+        )
+        for e in range(experts)
+    ])
+
+
+def unpack_slots(packed, slots):
+    experts, blocks = packed.shape[0], packed.shape[1] // slots
+    wide = packed.astype(F32)
+    return jnp.concatenate(
+        [
+            jnp.concatenate([wide[e, b * slots : (b + 1) * slots] for e in range(experts)], axis=0)
+            for b in range(blocks)
+        ],
+        axis=1,
+    )
+
+
+class Place:
+    def __init__(self):
+        self.me = lax.axis_index("seq")
+        self.core = lax.rem(self.me, 2)
+        self.chip = lax.div(self.me, 2)
+        self.partner = self.me + 1 - 2 * self.core
+        self.x_chip = self.chip + 1 - 2 * lax.rem(self.chip, 2)
+        self.y_chip = lax.rem(self.chip + 2, 4)
+        self.far_chip = 3 - self.chip
+        self.x, self.y, self.far = (c * 2 + self.core for c in (self.x_chip, self.y_chip, self.far_chip))
 
 
 def enter(devices):
@@ -518,21 +548,128 @@
     )
 
 
+class Gather:
+    def __init__(self, place, every, half, sends, recvs):
+        self.place, self.every, self.half, self.sends, self.recvs = place, every, half, sends, recvs
+
+    def copy(self, slot):
+        place, every = self.place, self.every
+        block, device = (
+            lambda: (every.at[place.me], place.partner),
+            lambda: (every.at[place.me], place.x),
+            lambda: (every.at[place.me], place.y),
+            lambda: (every.at[place.x, pl.ds(0, self.half)], place.y),
+            lambda: (every.at[place.y, pl.ds(self.half, self.half)], place.x),
+            lambda: (every.at[place.x], place.partner),
+            lambda: (every.at[place.y], place.partner),
+            lambda: (every.at[place.far], place.partner),
+        )[slot]()
+        return remote(block, block, self.sends.at[slot], self.recvs.at[slot], {"seq": device})
+
+    def send(self, *slots):
+        for slot in slots:
+            self.copy(slot).start()
+
+    def wait(self, *slots):
+        for slot in slots:
+            self.copy(slot).wait_recv()
+
+    def start(self):
+        self.send(1, 2, 0)
+
+    def relay(self):
+        self.wait(1)
+        self.send(3)
+        self.wait(2)
+        self.send(4, 5, 6)
+
+    def relay_far(self):
+        self.wait(3, 4)
+        self.send(7)
+
+    def finish(self):
+        self.wait(0, 5, 6, 7)
+
+    def drain(self):
+        for slot in range(8):
+            self.copy(slot).wait_send()
+
+
+class Scatter:
+    def __init__(self, place, out, pair, turn, side, half, sems):
+        self.place, self.out, self.pair, self.turn, self.side, self.half = place, out, pair, turn, side, half
+        self.pair_sems, self.turn_sems, self.side_sems = sems
+
+    def pair_copy(self):
+        send, recv = self.pair_sems
+        return remote(self.out.at[1 - self.place.core], self.pair, send, recv, {"seq": self.place.partner})
+
+    def turn_copies(self):
+        place = self.place
+        send, recv = self.turn_sems
+        far = self.out.at[place.core, place.far_chip]
+        return (
+            remote(far.at[pl.ds(0, self.half)], self.turn.at[0], send.at[0], recv.at[0], {"seq": place.x}),
+            remote(far.at[pl.ds(self.half, self.half)], self.turn.at[1], send.at[1], recv.at[1], {"seq": place.y}),
+        )
+
+    def side_copies(self):
+        place = self.place
+        send, recv = self.side_sems
+        return (
+            remote(self.out.at[place.core, place.x_chip], self.side.at[0], send.at[0], recv.at[0], {"seq": place.x}),
+            remote(self.out.at[place.core, place.y_chip], self.side.at[1], send.at[1], recv.at[1], {"seq": place.y}),
+        )
+
+    def start(self):
+        self.pair_copy().start()
+
+    def turn_on(self):
+        core = self.place.core
+        self.pair_copy().wait_recv()
+        self.out[core] = (self.out[core].astype(F32) + self.pair[...].astype(F32)).astype(BF16)
+        for copy in self.turn_copies():
+            copy.start()
+
+    def side_on(self):
+        place = self.place
+        first, second = pl.ds(0, self.half), pl.ds(self.half, self.half)
+        from_x, from_y = self.turn_copies()
+        from_x.wait_recv()
+        at = (place.core, place.y_chip, first)
+        self.out[at] = (self.out[at].astype(F32) + self.turn[0].astype(F32)).astype(BF16)
+        from_y.wait_recv()
+        at = (place.core, place.x_chip, second)
+        self.out[at] = (self.out[at].astype(F32) + self.turn[1].astype(F32)).astype(BF16)
+        for copy in self.side_copies():
+            copy.start()
+
+    def total(self):
+        for copy in self.side_copies():
+            copy.wait_recv()
+        own = self.out[self.place.core, self.place.chip].astype(F32)
+        return own + self.side[0].astype(F32) + self.side[1].astype(F32)
+
+    def drain(self):
+        self.pair_copy().wait_send()
+        for copy in self.turn_copies() + self.side_copies():
+            copy.wait_send()
+
+
 def forward_kernel(
-    seq_count, capacity, stride,
+    seq_count, capacity,
     x_ref, encoder_hbm, lengths_ref, buckets_ref, routes_ref, gains_ref, qkv_hbm, self_out_hbm, cross_q_hbm,
     cross_kv_hbm, cross_out_hbm, rel_ref, router_ref, g_ref,
     n1_hbm, kv_hbm, p_hbm, pc_hbm, ekv_hbm, q_ref, o_ref, n2_ref, qc_ref, oc_ref, x3_ref, r1_ref, r2_ref, gates_ref,
-    place_ref, xs_ref, dms_ref,
+    chosen_ref, place_ref, xs_ref, dms_ref,
     n1_all, kv_all, prob, cross_prob, ekv, scores, mask, w_qkv, w_self, w_cq, w_ckv, w_co, enc, table_ref,
     load_sem, store_sem, send_sem, recv_sem,
 ):
-    chips = seq_count // 2
     rows, width = x_ref.shape
     span = seq_count * rows
     pairs = width // LANES
-    me = lax.axis_index("seq")
-    core, chip, partner, others, sources = seq_peers(me, chips)
+    place = Place()
+    me = place.me
 
     loads = [
         pltpu.make_async_copy(src, dst, load_sem.at[i])
@@ -545,28 +682,27 @@
         load.start()
     x = x_ref[...].astype(F32)
     n1_all[me] = (x * rms_scale(x) * gains_ref[0:1, :]).astype(BF16)
-    enter([{"seq": partner}] + [{"seq": other} for other in others])
-    own = remote(n1_all.at[me], n1_all.at[me], send_sem.at[0], recv_sem.at[0], {"seq": partner})
-    direct = [
-        remote(n1_all.at[me], n1_all.at[me], send_sem.at[d], recv_sem.at[d], {"seq": others[d - 1]})
-        for d in range(1, chips)
-    ]
-    own.start()
-    for copy in direct:
-        copy.start()
+    enter([{"seq": device} for device in (place.partner, place.x, place.y)])
+    gather = Gather(place, n1_all, rows // 2, send_sem, recv_sem)
+    gather.start()
+
+    def project(chip):
+        part = n1_all[pl.ds(chip * 2, 2)].reshape(2 * rows, width)
+        kv_all[block_of(chip, 2 * rows), :] = nn(part, w_qkv[:, width:]).astype(BF16)
 
     loads[0].wait()
     q = nn(n1_all[me], w_qkv[:, :width]).astype(BF16)
     q_ref[...] = q * jnp.asarray(0.125, BF16)
+    gather.wait(0)
+    project(place.chip)
     loads[1].wait()
     loads[2].wait()
     ekv[...] = nn(enc[...], w_ckv[...]).astype(BF16)
     store_ekv = pltpu.make_async_copy(ekv, ekv_hbm, store_sem.at[0])
     store_ekv.start()
-    pick = (buckets_ref[...] == lax.broadcasted_iota(jnp.int32, (rel_ref.shape[0], LANES), 0)).astype(F32)
-    table = lax.dot_general(
-        rel_ref[...], pick, (((0,), (0,)), ((), ())), precision=highest, preferred_element_type=F32
-    )
+    gather.relay()
+    pick = (buckets_ref[...] == lax.broadcasted_iota(jnp.int32, (rel_ref.shape[1], LANES), 0)).astype(F32)
+    table = jnp.dot(rel_ref[...], pick, precision=highest, preferred_element_type=F32)
     table = table - table[:, LANES - 1 :]
     table_ref[...] = jnp.concatenate([jnp.zeros_like(table), table], axis=1)
     query_pos = me * rows + lax.broadcasted_iota(jnp.int32, (1, rows), 1)
@@ -579,27 +715,14 @@
     seen = jnp.where((key_pos >= start) & (key_pos <= query_pos), 0.0, masked_out)
     mask[...] = jnp.concatenate([seen, seen], axis=1)
 
-    forwards = []
-    for d in range(1, chips):
-        direct[d - 1].wait_recv()
-        block = n1_all.at[sources[d - 1]]
-        forward = remote(
-            block, block, send_sem.at[chips - 1 + d], recv_sem.at[chips - 1 + d], {"seq": partner}
-        )
-        forward.start()
-        forwards.append(forward)
-    own.wait_recv()
-    for forward in forwards:
-        forward.wait_recv()
+    gather.wait(5, 6)
+    project(place.x_chip)
+    project(place.y_chip)
+    gather.relay_far()
+    gather.wait(7)
+    project(place.far_chip)
     store_n1 = pltpu.make_async_copy(n1_all, n1_hbm, store_sem.at[1])
     store_n1.start()
-
-    @pl.loop(0, chips)
-    def _(c):
-        part = n1_all[pl.ds(c * 2, 2)].reshape(2 * rows, width)
-        at = pl.ds(pl.multiple_of(c * 2 * rows, 2 * rows), 2 * rows)
-        kv_all[at, :] = nn(part, w_qkv[:, width:]).astype(BF16)
-
     store_kv = pltpu.make_async_copy(kv_all, kv_hbm, store_sem.at[2])
     store_kv.start()
 
@@ -649,160 +772,768 @@
     r2_ref[...] = r2
     x3 = (r2 * rms_scale(r2) * gains_ref[2:3, :]).astype(BF16)
     x3_ref[...] = x3
-    experts = router_ref.shape[1]
-    logits = nn(x3, router_ref[...])
+    experts = router_ref.shape[0]
+    logits = nt(x3, router_ref[...])
     top = jnp.exp(logits - jnp.max(logits, axis=-1, keepdims=True))
     gates = top / jnp.sum(top, axis=-1, keepdims=True)
     gates_ref[...] = gates
-    route = routes_ref[...]
-    chosen = (route == lax.broadcasted_iota(jnp.int32, (rows, experts), 1)).astype(F32)
+    chosen = (routes_ref[...] == lax.broadcasted_iota(jnp.int32, (LANES, rows), 0)).astype(F32).T[:, :experts]
+    chosen_ref[...] = chosen
     earlier = (
         lax.broadcasted_iota(jnp.int32, (rows, rows), 1) < lax.broadcasted_iota(jnp.int32, (rows, rows), 0)
     ).astype(BF16)
     slot = jnp.sum(nn(earlier, chosen.astype(BF16)) * chosen, axis=1, keepdims=True).astype(jnp.int32)
     kept = slot < capacity
     gate_used = jnp.sum(gates * chosen, axis=1, keepdims=True) * kept.astype(F32)
-    target = jnp.where(kept, route * stride + slot, -1)
-    place = (
-        lax.broadcasted_iota(jnp.int32, (rows, experts * stride), 1) == target
-    ).astype(BF16)
-    place_ref[...] = place
-    xs_ref[...] = tn(place, x3).astype(BF16)
+    expert = lax.broadcasted_iota(jnp.int32, (rows, experts), 1).astype(F32)
+    route = jnp.sum(chosen * expert, axis=1, keepdims=True).astype(jnp.int32)
+    target = jnp.where(kept, route * capacity + slot, -1)
+    slots = (lax.broadcasted_iota(jnp.int32, (rows, experts * capacity), 1) == target).astype(BF16)
+    place_ref[...] = slots
+    xs_ref[...] = pack_slots(tn(slots, x3), experts).astype(BF16)
     made_grad = (g_ref[...].astype(F32) * gate_used).astype(BF16)
-    dms_ref[...] = tn(place, made_grad).astype(BF16)
-
-    own.wait_send()
-    for copy in direct + forwards:
-        copy.wait_send()
+    dms_ref[...] = pack_slots(tn(slots, made_grad), experts).astype(BF16)
+
+    gather.drain()
     for store in (store_ekv, store_n1, store_kv, store_p, store_pc):
         store.wait()
 
 
-def forward_call(seq_count, capacity, stride, x, encoder, lengths, buckets, routes, gains, w_qkv, w_self, w_cq, w_ckv,
-                 w_co, rel, router, g):
+def forward_call(seq_count, capacity, x, encoder, lengths, buckets, routes, gains, w_qkv, w_self, w_cq, w_ckv, w_co, rel,
+                 router, g):
     rows, width = x.shape
     span = seq_count * rows
     pairs = width // LANES
     enc_rows = encoder.shape[0]
-    experts = router.shape[1]
-    chips = seq_count // 2
+    experts = router.shape[0]
     shape = jax.ShapeDtypeStruct
     wide = shape((rows, width), BF16)
+    packed = shape((experts, capacity * pairs, LANES), BF16)
+    narrow = shape((rows, experts), F32)
     outs = (
         shape((seq_count, rows, width), BF16), shape((span, 2 * width), BF16), shape((pairs, span, 2 * rows), BF16),
         shape((pairs, enc_rows, 2 * rows), BF16), shape((enc_rows, 2 * width), BF16), wide, wide, wide, wide, wide, wide,
-        shape((rows, width), F32), shape((rows, width), F32), shape((rows, experts), F32),
-        shape((rows, experts * stride), BF16), shape((experts * stride, width), BF16), shape((experts * stride, width), BF16),
+        shape((rows, width), F32), shape((rows, width), F32), narrow, narrow,
+        shape((rows, experts * capacity), BF16), packed, packed,
     )
     return pl.pallas_call(
-        functools.partial(forward_kernel, seq_count, capacity, stride),
+        functools.partial(forward_kernel, seq_count, capacity),
         out_shape=outs,
         in_specs=[VMEM, ANY, SMEM, VMEM, VMEM, VMEM, ANY, ANY, ANY, ANY, ANY, VMEM, VMEM, VMEM],
-        out_specs=tuple([ANY] * 5 + [VMEM] * 12),
+        out_specs=tuple([ANY] * 5 + [VMEM] * 13),
         scratch_shapes=[
             pltpu.VMEM((seq_count, rows, width), BF16), pltpu.VMEM((span, 2 * width), BF16),
             pltpu.VMEM((pairs, span, 2 * rows), BF16), pltpu.VMEM((pairs, enc_rows, 2 * rows), BF16),
             pltpu.VMEM((enc_rows, 2 * width), BF16), pltpu.VMEM((span + rows, 2 * rows), F32),
             pltpu.VMEM((span, 2 * rows), F32), pltpu.VMEM(w_qkv.shape, BF16), pltpu.VMEM(w_self.shape, BF16),
             pltpu.VMEM(w_cq.shape, BF16), pltpu.VMEM(w_ckv.shape, BF16), pltpu.VMEM(w_co.shape, BF16),
-            pltpu.VMEM(encoder.shape, BF16), pltpu.VMEM((rel.shape[1], 2 * LANES), F32),
+            pltpu.VMEM(encoder.shape, BF16), pltpu.VMEM((rel.shape[0], 2 * LANES), F32),
             pltpu.SemaphoreType.DMA((6,)), pltpu.SemaphoreType.DMA((5,)),
-            pltpu.SemaphoreType.DMA((2 * chips - 1,)), pltpu.SemaphoreType.DMA((2 * chips - 1,)),
+            pltpu.SemaphoreType.DMA((8,)), pltpu.SemaphoreType.DMA((8,)),
         ],
         compiler_params=pltpu.CompilerParams(collective_id=0, has_side_effects=True, vmem_limit_bytes=56 << 20),
         name="forward",
     )(x, encoder, lengths, buckets, routes, gains, w_qkv, w_self, w_cq, w_ckv, w_co, rel, router, g)
 
 
+def expert_peers(exp_index, experts):
+    return [lax.rem(exp_index + d, experts) for d in range(1, experts)]
+
+
+def gelu_parts(hid):
+    root, cubic = 0.7978845608028654, 0.044715
+    square = hid * hid
+    bent = jnp.tanh(root * hid * (1.0 + cubic * square))
+    half = 0.5 * (1.0 + bent)
+    return hid * half, half + 0.5 * hid * (1.0 - bent * bent) * (root + 3.0 * root * cubic * square)
+
+
+def experts_kernel(
+    seq_count, experts, slots,
+    xs_ref, dms_ref, w_in_hbm, w_out_hbm,
+    made_ref, dx_ref, x_hbm, dm_hbm,
+    x_all, dm_all, x_in, dm_in, made_out, made_back, dx_out, dx_back, slope, w_in, w_out,
+    load_sem, store_sem, zx_send, zx_recv, zd_send, zd_recv, zm_send, zm_recv, zg_send, zg_recv,
+    x_send, x_recv, d_send, d_recv,
+):
+    width = x_all.shape[-1]
+    rows = experts * slots
+    hidden = w_in.shape[1]
+    place = Place()
+    mine = lax.axis_index("exp")
+    peers = expert_peers(mine, experts)
+    loads = [
+        pltpu.make_async_copy(w_in_hbm, w_in, load_sem.at[0]),
+        pltpu.make_async_copy(w_out_hbm, w_out, load_sem.at[1]),
+    ]
+    for load in loads:
+        load.start()
+    enter([{"seq": device} for device in (place.partner, place.x, place.y)] + [{"exp": peer} for peer in peers])
+
+    def over_exp(src, dst, send, recv):
+        copies = [
+            remote(src.at[peer], dst.at[mine], send.at[d], recv.at[d], {"exp": peer}) for d, peer in enumerate(peers)
+        ]
+        for copy in copies:
+            copy.start()
+        dst[mine] = src[mine]
+        return copies
+
+    x_moves = over_exp(xs_ref, x_in, zx_send, zx_recv)
+    dm_moves = over_exp(dms_ref, dm_in, zd_send, zd_recv)
+    for move in x_moves:
+        move.wait_recv()
+    x_all[place.me] = unpack_slots(x_in[...], slots).astype(BF16)
+    x_gather = Gather(place, x_all, rows // 2, x_send, x_recv)
+    x_gather.start()
+    x = x_all[place.me]
+    loads[0].wait()
+    loads[1].wait()
+    made = jnp.zeros((rows, width), F32)
+    for n in range(hidden // width):
+        at = slice(n * width, (n + 1) * width)
+        value, derivative = gelu_parts(nn(x, w_in[:, at]))
+        slope[:, at] = derivative
+        made = made + nn(value.astype(BF16), w_out[at, :])
+    made_out[...] = pack_slots(made, experts).astype(BF16)
+    made_moves = over_exp(made_out, made_back, zm_send, zm_recv)
+
+    for move in dm_moves:
+        move.wait_recv()
+    dm_all[place.me] = unpack_slots(dm_in[...], slots).astype(BF16)
+    dm_gather = Gather(place, dm_all, rows // 2, d_send, d_recv)
+    dm_gather.start()
+    dm = dm_all[place.me]
+    dx = jnp.zeros((rows, width), F32)
+    for n in range(hidden // width):
+        at = slice(n * width, (n + 1) * width)
+        dh = (nt(dm, w_out[at, :]) * slope[:, at]).astype(BF16)
+        dx = dx + nt(dh, w_in[:, at])
+    dx_out[...] = pack_slots(dx, experts).astype(BF16)
+    dx_moves = over_exp(dx_out, dx_back, zg_send, zg_recv)
+
+    x_gather.relay()
+    for move in made_moves:
+        move.wait_recv()
+    made_ref[...] = unpack_slots(made_back[...], slots).astype(BF16)
+    x_gather.relay_far()
+    dm_gather.relay()
+    for move in dx_moves:
+        move.wait_recv()
+    dx_ref[...] = unpack_slots(dx_back[...], slots).astype(BF16)
+    x_gather.finish()
+    store_x = pltpu.make_async_copy(x_all, x_hbm, store_sem.at[0])
+    store_x.start()
+    dm_gather.relay_far()
+    dm_gather.finish()
+    store_dm = pltpu.make_async_copy(dm_all, dm_hbm, store_sem.at[1])
+    store_dm.start()
+    for copy in x_moves + dm_moves + made_moves + dx_moves:
+        copy.wait_send()
+    x_gather.drain()
+    dm_gather.drain()
+    store_x.wait()
+    store_dm.wait()
+
+
+def experts_call(seq_count, slots, width, xs, dms, w_in, w_out):
+    experts = xs.shape[0]
+    rows = experts * slots
+    shape = jax.ShapeDtypeStruct
+    every = (seq_count, rows, width)
+    dma = lambda n: pltpu.SemaphoreType.DMA((n,))
+    z = experts - 1
+    return pl.pallas_call(
+        functools.partial(experts_kernel, seq_count, experts, slots),
+        out_shape=(shape((rows, width), BF16), shape((rows, width), BF16), shape(every, BF16), shape(every, BF16)),
+        in_specs=[VMEM, VMEM, ANY, ANY],
+        out_specs=(VMEM, VMEM, ANY, ANY),
+        scratch_shapes=[pltpu.VMEM(every, BF16)] * 2 + [pltpu.VMEM(xs.shape, BF16)] * 6 + [
+            pltpu.VMEM((rows, w_in.shape[1]), F32), pltpu.VMEM(w_in.shape, BF16), pltpu.VMEM(w_out.shape, BF16),
+            dma(2), dma(2)] + [dma(z)] * 8 + [dma(8)] * 4,
+        compiler_params=pltpu.CompilerParams(collective_id=1, has_side_effects=True, vmem_limit_bytes=56 << 20),
+        name="experts",
+    )(xs, dms, w_in, w_out)
+
+
+def rms_back(a, gain, grad):
+    scale = rms_scale(a)
+    weighted = grad * gain
+    da = scale * weighted - a * (scale * scale * scale * jnp.mean(a * weighted, axis=-1, keepdims=True))
+    return da, jnp.sum(grad * (a * scale), axis=0, keepdims=True)
+
+
+def in_two(value):
+    high = value.astype(BF16)
+    return high, (value - high.astype(F32)).astype(BF16)
+
+
+class Chunk:
+    def __init__(self, place, quarters, mine, peers, src, slots, own, every, sems, gather_sems, local_sem):
+        self.place, self.quarters, self.mine, self.peers = place, quarters, mine, peers
+        self.src, self.slots, self.own, self.every = src, slots, own, every
+        self.scatter_sems, self.gather_sems, self.local_sem = sems[:2], sems[2:], local_sem
+        self.over_seq = Gather(place, every, src.shape[0] // 2, *gather_sems)
+
+    def scatter_copies(self):
+        send, recv = self.scatter_sems
+        return [
+            remote(self.src.at[self.quarters[1 + d]], self.slots.at[d], send.at[d], recv.at[d], {"exp": peer})
+            for d, peer in enumerate(self.peers)
+        ]
+
+    def gather_copies(self):
+        send, recv = self.gather_sems
+        target = self.every.at[(self.place.me,) + self.quarters[0]]
+        return [remote(self.own, target, send.at[d], recv.at[d], {"exp": peer}) for d, peer in enumerate(self.peers)]
+
+    def local_copy(self):
+        return pltpu.make_async_copy(self.own, self.every.at[(self.place.me,) + self.quarters[0]], self.local_sem)
+
+    def over_exp(self, value):
+        self.src[...] = value.astype(BF16)
+        for copy in self.scatter_copies():
+            copy.start()
+
+    def back_over_exp(self):
+        total = self.src[self.quarters[0]].astype(F32)
+        for d, copy in enumerate(self.scatter_copies()):
+            copy.wait_recv()
+            total = total + self.slots[d].astype(F32)
+        self.own[...] = total.astype(BF16)
+        self.local_copy().start()
+        for copy in self.gather_copies():
+            copy.start()
+
+    def spread(self):
+        self.local_copy().wait()
+        for copy in self.gather_copies():
+            copy.wait_recv()
+        self.over_seq.start()
+
+    def drain(self):
+        for copy in self.scatter_copies() + self.gather_copies():
+            copy.wait_send()
+        self.over_seq.drain()
+
+
+def backward_kernel(
+    seq_count, experts,
+    made_ref, dxb_ref, g_ref, x_ref, r1_ref, r2_ref, gates_ref, chosen_ref, slots_ref, x3_ref, n2_ref, o_ref, oc_ref,
+    q_ref, qc_ref, gains_ref, router_ref, buckets_ref, kv_hbm, p_hbm, pc_hbm, ekv_hbm, co_hbm, cq_hbm, so_hbm, qkv_hbm,
+    n1_hbm, x_hbm, dm_hbm, in_hbm, out_hbm, ckv_hbm,
+    out_ref, dx_ref, weights_hbm, dekv_hbm, small_out_ref, gin_ref, gout_ref, genc_ref,
+    kv_all, prob, cross_prob, ekv, w_co, w_cq, w_so, w_qkv, dr_ref, doc_ref, dqc_ref, dqkv_ref, ds_ref, diag_ref, total_ref,
+    e_out, e_pair, e_turn, e_side, e_mine, e_exp, dekv, t_out, t_pair, t_turn, t_side, w_out, w_pair, w_turn, w_side,
+    c_src, c_slots, c_own, dqkv_t, right, n1_all, x_all, dm_all, w_ein, w_eout, w_ckv, gin_out, gin_in,
+    small_a, small_b, small_c, small_pair, small_chip, small_exp,
+    load_sem, local_sem, ep_send, ep_recv, et_send, et_recv, es_send, es_recv, ez_send, ez_recv, eg_send, eg_recv, ea_send, ea_recv,
+    tp_send, tp_recv, tt_send, tt_recv, ts_send, ts_recv, wp_send, wp_recv, wt_send, wt_recv, ws_send, ws_recv,
+    cs_send, cs_recv, cg_send, cg_recv, ca_send, ca_recv, r_send, r_recv, g_send, g_recv,
+    s1_send, s1_recv, s2_send, s2_recv, s3_send, s3_recv,
+):
+    rows, width = x_ref.shape
+    span = seq_count * rows
+    pairs = width // LANES
+    place = Place()
+    me = place.me
+    mine = lax.axis_index("exp")
+    peers = expert_peers(mine, experts)
+    everyone = [lax.rem(me + d, seq_count) for d in range(1, seq_count)]
+    part = width // seq_count
+    half_rows, half_lanes = part // 2, width // (experts // 2)
+    quarters = [
+        (block_of(lax.div(e, experts // 2), half_rows), block_of(lax.rem(e, experts // 2), half_lanes)) for e in [mine] + peers
+    ]
+    at_hidden = block_of(me, w_ein.shape[1])
+    loads = [
+        pltpu.make_async_copy(src, dst, load_sem.at[i])
+        for i, (src, dst) in enumerate(
+            [(co_hbm, w_co), (ekv_hbm, ekv), (pc_hbm, cross_prob), (cq_hbm, w_cq), (so_hbm, w_so), (kv_hbm, kv_all),
+             (p_hbm, prob), (qkv_hbm, w_qkv), (n1_hbm, n1_all), (x_hbm, x_all), (in_hbm.at[:, at_hidden], w_ein),
+             (dm_hbm, dm_all), (out_hbm.at[at_hidden, :], w_eout), (ckv_hbm, w_ckv)]
+        )
+    ]
+    for load in loads:
+        load.start()
+    enter([{"seq": device} for device in everyone] + [{"exp": peer} for peer in peers])
+    started = []
+
+    def send(src, dst, send_sem, recv_sem, device):
+        copy = remote(src, dst, send_sem, recv_sem, device)
+        copy.start()
+        started.append(copy)
+        return copy
+
+    enc_scatter = Scatter(
+        place, e_out, e_pair, e_turn, e_side, e_turn.shape[1],
+        ((ep_send.at[0], ep_recv.at[0]), (et_send, et_recv), (es_send, es_recv)),
+    )
+    squares = [
+        Scatter(
+            place, w_out.at[i], w_pair.at[i], w_turn.at[i], w_side.at[i], half_rows,
+            ((wp_send.at[i], wp_recv.at[i]), (wt_send.at[i], wt_recv.at[i]), (ws_send.at[i], ws_recv.at[i])),
+        )
+        for i in range(3)
+    ]
+    chunks = [
+        Chunk(
+            place, quarters, mine, peers, c_src.at[i], c_slots.at[i], c_own.at[i], weights_hbm.at[i],
+            (cs_send.at[i], cs_recv.at[i], cg_send.at[i], cg_recv.at[i]), (ca_send.at[i], ca_recv.at[i]), local_sem.at[i],
+        )
+        for i in range(6)
+    ]
+    dekv_gather = Gather(place, dekv_hbm, experts // 2, ea_send, ea_recv)
+
+    def enc_over_exp():
+        return [
+            remote(e_mine.at[peer], e_exp.at[d], ez_send.at[d], ez_recv.at[d], {"exp": peer}) for d, peer in enumerate(peers)
+        ]
+
+    def dekv_over_exp():
+        return [
+            remote(dekv, dekv_hbm.at[me, mine], eg_send.at[d], eg_recv.at[d], {"exp": peer}) for d, peer in enumerate(peers)
+        ]
+
+    def dekv_local():
+        return pltpu.make_async_copy(dekv, dekv_hbm.at[me, mine], local_sem.at[6])
+
+    def square_start(i, left, right_factor):
+        grad = tn(left, right_factor).astype(BF16).reshape(4, 2, part, width)
+        for k in range(2):
+            w_out[i, k] = grad[:, k]
+        squares[i].start()
+
+    made = nn(slots_ref[...], made_ref[...])
+    kept = jnp.sum(slots_ref[...].astype(F32), axis=1, keepdims=True)
+    gates = gates_ref[...]
+    chosen = chosen_ref[...]
+    picked = jnp.sum(gates * chosen, axis=1, keepdims=True)
+    g = g_ref[...].astype(F32)
+    out_ref[...] = (r2_ref[...] + (picked * kept) * made).astype(BF16)
+    gate_grad = jnp.sum(g * made, axis=1, keepdims=True) * kept
+    dl = gates * (chosen * gate_grad - picked * gate_grad)
+    dl_high, dl_low = in_two(dl)
+    x3 = x3_ref[...]
+    small_a[...] = jnp.zeros_like(small_a)
+    small_a[4 : 4 + experts, :width] = tn(dl_high, x3) + tn(dl_low, x3)
+    dx3 = nn(slots_ref[...], dxb_ref[...]) + nn(dl_high, router_ref[...]) + nn(dl_low, router_ref[...])
+    da, dw = rms_back(r2_ref[...], gains_ref[2:3, :], dx3)
+    small_a[2:3, :width] = dw
+    dr_ref[...] = g + da
+    do2 = dr_ref[...].astype(BF16)
+    loads[0].wait()
+    doc_ref[...] = nt(do2, w_co[...]).astype(BF16)
+    square_start(2, oc_ref[...], do2)
+
+    loads[1].wait()
+    loads[2].wait()
+    enc_rows = ekv.shape[0]
+    enc_part = enc_rows // seq_count
+
+    @pl.loop(0, pairs)
+    def _(p):
+        lanes, value_lanes = pair_lanes(p), pair_lanes(pairs + p)
+        doc_both = head_stack(doc_ref[:, lanes])
+        weights = cross_prob[p]
+        wide = weights.astype(F32)
+        dp = nt(ekv[:, value_lanes], doc_both)
+        dc = (wide * (dp - jnp.sum(wide * dp, axis=0, keepdims=True))).astype(BF16)
+        dk = nn(dc, head_stack(qc_ref[:, lanes])).astype(BF16).reshape(4, 2, enc_part, LANES)
+        dv = nn(weights, doc_both).astype(BF16).reshape(4, 2, enc_part, LANES)
+        for k in range(2):
+            e_out[k, :, :, lanes] = dk[:, k]
+            e_out[k, :, :, value_lanes] = dv[:, k]
+        dqc_ref[:, lanes] = (head_unstack(tn(ekv[:, lanes], dc), rows) * 0.125).astype(BF16)
+
+    enc_scatter.start()
+    squares[2].turn_on()
+    dqc = dqc_ref[...]
+    loads[3].wait()
+    loads[4].wait()
+    da, dw = rms_back(r1_ref[...], gains_ref[1:2, :], nt(dqc, w_cq[...]))
+    small_a[1:2, :width] = dw
+    dr_ref[...] = dr_ref[...] + da
+    do1 = dr_ref[...].astype(BF16)
+    doc_ref[...] = nt(do1, w_so[...]).astype(BF16)
+    enc_scatter.turn_on()
+    square_start(1, n2_ref[...], dqc)
+    square_start(0, o_ref[...], do1)
+    squares[2].side_on()
+    squares[1].turn_on()
+    squares[0].turn_on()
+
+    loads[5].wait()
+    loads[6].wait()
+    ds_ref[pl.ds(0, rows), :] = jnp.zeros((rows, 2 * rows), BF16)
+    near = pl.ds(pl.multiple_of(me * rows, rows), 2 * rows)
+    flip = (
+        lax.broadcasted_iota(jnp.int32, (2 * rows, 2 * rows), 0) + lax.broadcasted_iota(jnp.int32, (2 * rows, 2 * rows), 1)
+        == 2 * rows - 1
+    ).astype(BF16)
+
+    def terms(p):
+        return Scatter(
+            place, t_out.at[p], t_pair.at[p], t_turn.at[p], t_side.at[p], rows // 2,
+            ((tp_send.at[p], tp_recv.at[p]), (tt_send.at[p], tt_recv.at[p]), (ts_send.at[p], ts_recv.at[p])),
+        )
+
+    @pl.loop(0, pairs + 3)
+    def _(t):
+        @pl.when(t < pairs)
+        def _():
+            p = jnp.minimum(t, pairs - 1)
+            lanes, value_lanes = pair_lanes(p), pair_lanes(pairs + p)
+            do_both = head_stack(doc_ref[:, lanes])
+            weights = prob[p]
+            wide = weights.astype(F32)
+            dp = nt(kv_all[:, value_lanes], do_both)
+            ds_wide = wide * (dp - jnp.sum(wide * dp, axis=0, keepdims=True))
+            ds = ds_wide.astype(BF16)
+            ds_ref[pl.ds(rows, span), :] = ds
+            total_ref[pl.ds(p, 1), :] = jnp.sum(ds.astype(F32), axis=0, keepdims=True)
+            dk = nn(ds, head_stack(q_ref[:, lanes])).astype(BF16).reshape(4, 2, rows, LANES)
+            dv = nn(weights, do_both).astype(BF16).reshape(4, 2, rows, LANES)
+            for k in range(2):
+                t_out[p, k, :, :, :LANES] = dk[:, k]
+                t_out[p, k, :, :, LANES:] = dv[:, k]
+            terms(p).start()
+            dqkv_ref[:, lanes] = (head_unstack(tn(kv_all[:, lanes], ds), rows) * 0.125).astype(BF16)
+            turned = nn(flip, ds_ref[near, :])
+            for h in range(2):
+                one = turned[:, h * rows : (h + 1) * rows]
+                one = jnp.concatenate([one, jnp.zeros_like(one)], axis=1)
+                one = pltpu.roll(one, 1, 1, stride=1, stride_axis=0)
+                diag_ref[pl.ds(2 * p + h, 1), :] = jnp.sum(one, axis=0, keepdims=True)
+
+        @pl.when((t >= 1) & (t <= pairs))
+        def _():
+            terms(jnp.clip(t - 1, 0, pairs - 1)).turn_on()
+
+        @pl.when((t >= 2) & (t <= pairs + 1))
+        def _():
+            terms(jnp.clip(t - 2, 0, pairs - 1)).side_on()
+
+        @pl.when(t >= 3)
+        def _():
+            p = jnp.clip(t - 3, 0, pairs - 1)
+            total = terms(p).total()
+            dqkv_ref[:, pair_lanes(pairs + p)] = total[:, :LANES].astype(BF16)
+            dqkv_ref[:, pair_lanes(2 * pairs + p)] = total[:, LANES:].astype(BF16)
+
+        @pl.when(t == 0)
+        def _():
+            enc_scatter.side_on()
+
+        @pl.when(t == 1)
+        def _():
+            squares[1].side_on()
+            chunks[2].over_exp(squares[2].total())
+
+        @pl.when(t == 2)
+        def _():
+            squares[0].side_on()
+            e_mine[...] = enc_scatter.total().astype(BF16).reshape(e_mine.shape)
+            for copy in enc_over_exp():
+                copy.start()
+
+        @pl.when(t == 3)
+        def _():
+            chunks[1].over_exp(squares[1].total())
+            chunks[2].back_over_exp()
+
+        @pl.when(t == 4)
+        def _():
+            chunks[0].over_exp(squares[0].total())
+            total = e_mine[mine].astype(F32)
+            for d, copy in enumerate(enc_over_exp()):
+                copy.wait_recv()
+                total = total + e_exp[d].astype(F32)
+            dekv[...] = total.astype(BF16)
+            dekv_local().start()
+            for copy in dekv_over_exp():
+                copy.start()
+
+        @pl.when(t == 5)
+        def _():
+            chunks[1].back_over_exp()
+
+        @pl.when(t == 6)
+        def _():
+            chunks[0].back_over_exp()
+
+    dqkv = dqkv_ref[...]
+    dqkv_t[...] = dqkv.T
+    own_lanes = block_of(me, rows)
+    rights = []
+    for i in range(3):
+        rights.append([
+            send(dqkv_t.at[pl.ds(pl.multiple_of(i * width + peer * part, part), part), :], right.at[i, :, own_lanes],
+                 r_send.at[i, d], r_recv.at[i, d], {"seq": peer})
+            for d, peer in enumerate(everyone)
+        ])
+        right[i, :, own_lanes] = dqkv_t[pl.ds(pl.multiple_of(i * width + me * part, part), part), :]
+    for i in (2, 1, 0):
+        chunks[i].spread()
+    dekv_local().wait()
+    for copy in dekv_over_exp():
+        copy.wait_recv()
+    dekv_gather.start()
+
+    loads[7].wait()
+    x = x_ref[...].astype(F32)
+    da, dw = rms_back(x, gains_ref[0:1, :], nt(dqkv, w_qkv[...]))
+    small_a[0:1, :width] = dw
+    dx_ref[...] = dr_ref[...] + da
+    heads = 2 * pairs
+    table = diag_ref[:, 2 * rows - LANES :]
+    totals = total_ref[...]
+    first = jnp.sum(totals[:, :rows], axis=1, keepdims=True)
+    second = jnp.sum(totals[:, rows:], axis=1, keepdims=True)
+    head = lax.broadcasted_iota(jnp.int32, (heads, pairs), 0)
+    pair = lax.broadcasted_iota(jnp.int32, (heads, pairs), 1)
+    spread = lambda odd, v: jnp.dot((head == 2 * pair + odd).astype(F32), v, precision=highest, preferred_element_type=F32)
+    whole = spread(0, jnp.broadcast_to(first, (pairs, LANES))) + spread(1, jnp.broadcast_to(second, (pairs, LANES)))
+    rest = whole - jnp.sum(table, axis=1, keepdims=True)
+    lane = lax.broadcasted_iota(jnp.int32, table.shape, 1)
+    table = table + jnp.where(lane == LANES - 1, rest, 0.0)
+    bucket = lax.broadcasted_iota(jnp.int32, (LANES, LANES), 0)
+    pick = (buckets_ref[...] == bucket).astype(F32)
+    by_bucket = lax.dot_general(table, pick, (((1,), (1,)), ((), ())), precision=highest, preferred_element_type=F32)
+    small_a[0:8, width : width + LANES] = by_bucket[0:8]
+    small_a[0 : heads - 8, width + LANES :] = by_bucket[8:heads]
+    s_pair = send(small_a, small_pair, s1_send.at[0], s1_recv.at[0], {"seq": place.partner})
+
+    loads[8].wait()
+    n1 = n1_all[...].reshape(span, width)
+    for i in range(3):
+        for copy in rights[i]:
+            copy.wait_recv()
+        chunks[3 + i].over_exp(nn(right[i], n1))
+    s_pair.wait_recv()
+    small_b[...] = small_a[...] + small_pair[...]
+    s_chip = [
+        send(small_b, small_chip.at[d], s2_send.at[d], s2_recv.at[d], {"seq": device})
+        for d, device in enumerate((place.x, place.y, place.far))
+    ]
+    for load in loads[9:13]:
+        load.wait()
+    xs = x_all[...].reshape(-1, width)
+    value, slope = gelu_parts(nn(xs, w_ein[...]))
+    dm = dm_all[...].reshape(-1, width)
+    gout_ref[...] = tn(value.astype(BF16), dm)
+    chunks[2].over_seq.relay()
+    chunks[3].back_over_exp()
+    chunks[1].over_seq.relay()
+    dh = (nt(dm, w_eout[...]) * slope).astype(BF16)
+    gin_out[...] = tn(xs, dh).astype(BF16).reshape(gin_out.shape)
+    gins = [
+        send(gin_out.at[peer], gin_in.at[:, at_hidden], g_send.at[d], g_recv.at[d], {"seq": peer})
+        for d, peer in enumerate(everyone)
+    ]
+    gin_in[:, at_hidden] = gin_out[me]
+    chunks[4].back_over_exp()
+    chunks[3].spread()
+    chunks[5].back_over_exp()
+    chunks[0].over_seq.relay()
+    dekv_gather.relay()
+    chunks[4].spread()
+    loads[13].wait()
+    genc_ref[...] = nt(dekv[...], w_ckv[...])
+    total = small_b[...]
+    for d, copy in enumerate(s_chip):
+        copy.wait_recv()
+        total = total + small_chip[d]
+    small_c[...] = total
+    s_exp = [
+        send(small_c, small_exp.at[d], s3_send.at[d], s3_recv.at[d], {"exp": peer}) for d, peer in enumerate(peers)
+    ]
+    chunks[5].spread()
+    for i in (2, 1, 0):
+        chunks[i].over_seq.relay_far()
+    dekv_gather.relay_far()
+    total = small_c[...]
+    for d, copy in enumerate(s_exp):
+        copy.wait_recv()
+        total = total + small_exp[d]
+    small_out_ref[...] = total
+    for copy in gins:
+        copy.wait_recv()
+    gin_ref[...] = gin_in[...].astype(F32)
+    for i in (3, 4, 5):
+        chunks[i].over_seq.relay()
+    for i in (3, 4, 5):
+        chunks[i].over_seq.relay_far()
+    for chunk in chunks:
+        chunk.over_seq.finish()
+    dekv_gather.finish()
+
+    for copy in started + enc_over_exp() + dekv_over_exp():
+        copy.wait_send()
+    for scatter in squares + [enc_scatter]:
+        scatter.drain()
+    for chunk in chunks:
+        chunk.drain()
+    dekv_gather.drain()
+
+    @pl.loop(0, pairs)
+    def _(p):
+        terms(p).drain()
+
+
+def backward_call(seq_count, experts, made, dxb, g, x, r1, r2, gates, chosen, slots, x3, n2, o, oc, q, qc, gains, router,
+                  buckets, kv, p, pc, ekv, co, cq, so, qkv, n1, x_all, dm_all, w_in, w_out, ckv):
+    rows, width = x.shape
+    span = seq_count * rows
+    pairs = width // LANES
+    enc_rows = ekv.shape[0]
+    part = width // seq_count
+    enc_part = enc_rows // seq_count
+    own_enc = enc_part // experts
+    hidden = w_in.shape[1] // seq_count
+    z = experts - 1
+    quarter = (part // 2, width // (experts // 2))
+    small = (8, width + 2 * LANES)
+    shape = jax.ShapeDtypeStruct
+    dma = lambda *n: pltpu.SemaphoreType.DMA(n)
+    bf = lambda *n: pltpu.VMEM(n, BF16)
+    f32 = lambda *n: pltpu.VMEM(n, F32)
+    return pl.pallas_call(
+        functools.partial(backward_kernel, seq_count, experts),
+        out_shape=(
+            shape((rows, width), BF16), shape((rows, width), F32), shape((6, seq_count, part, width), BF16),
+            shape((seq_count, experts, own_enc, 2 * width), BF16), shape(small, F32), shape((part, w_in.shape[1]), F32),
+            shape((hidden, width), F32), shape((own_enc, width), F32),
+        ),
+        in_specs=[VMEM] * 18 + [ANY] * 14,
+        out_specs=(VMEM, VMEM, ANY, ANY, VMEM, VMEM, VMEM, VMEM),
+        scratch_shapes=[
+            bf(span, 2 * width), bf(pairs, span, 2 * rows), bf(pairs, enc_rows, 2 * rows), bf(enc_rows, 2 * width),
+            bf(*co.shape), bf(*cq.shape), bf(*so.shape), bf(*qkv.shape), f32(rows, width), bf(rows, width), bf(rows, width),
+            bf(rows, 3 * width), bf(span + rows, 2 * rows), f32(2 * pairs, 2 * rows), f32(pairs, 2 * rows),
+            bf(2, 4, enc_part, 2 * width), bf(4, enc_part, 2 * width), bf(2, enc_part // 2, 2 * width),
+            bf(2, enc_part, 2 * width), bf(experts, own_enc, 2 * width), bf(z, own_enc, 2 * width), bf(own_enc, 2 * width),
+            bf(pairs, 2, 4, rows, 2 * LANES), bf(pairs, 4, rows, 2 * LANES), bf(pairs, 2, rows // 2, 2 * LANES),
+            bf(pairs, 2, rows, 2 * LANES),
+            bf(3, 2, 4, part, width), bf(3, 4, part, width), bf(3, 2, part // 2, width), bf(3, 2, part, width),
+            bf(6, part, width), bf(6, z, *quarter), bf(6, *quarter), bf(3 * width, rows), bf(3, part, span),
+            bf(*n1.shape), bf(*x_all.shape), bf(*dm_all.shape), bf(width, hidden), bf(hidden, width), bf(*ckv.shape),
+            bf(seq_count, part, hidden), bf(part, w_in.shape[1]),
+            f32(*small), f32(*small), f32(*small), f32(*small), f32(3, *small), f32(z, *small),
+            dma(14), dma(7), dma(1), dma(1), dma(2), dma(2), dma(2), dma(2), dma(z), dma(z), dma(z), dma(z), dma(8), dma(8),
+            dma(pairs), dma(pairs), dma(pairs, 2), dma(pairs, 2), dma(pairs, 2), dma(pairs, 2),
+            dma(3), dma(3), dma(3, 2), dma(3, 2), dma(3, 2), dma(3, 2),
+            dma(6, z), dma(6, z), dma(6, z), dma(6, z), dma(6, 8), dma(6, 8),
+            dma(3, seq_count - 1), dma(3, seq_count - 1), dma(seq_count - 1), dma(seq_count - 1),
+            dma(1), dma(1), dma(3), dma(3), dma(z), dma(z),
+        ],
+        compiler_params=pltpu.CompilerParams(collective_id=2, has_side_effects=True, vmem_limit_bytes=63 << 20),
+        name="backward",
+    )(made, dxb, g, x, r1, r2, gates, chosen, slots, x3, n2, o, oc, q, qc, gains, router, buckets, kv, p, pc, ekv, co, cq, so,
+      qkv, n1, x_all, dm_all, w_in, w_out, ckv)
+
+
+def finish_kernel(
+    experts, weights_hbm, dekv_hbm, enc_hbm, small_ref, layer_hbm, dx_hbm, genc_hbm, gin_hbm, gout_hbm,
+    layer_out, dx_out, genc_out, gains_out, qkv_hbm, so_hbm, cq_hbm, ckv_hbm, co_hbm, rel_out, router_out, gin_out, gout_out,
+    weights, dekv, enc, squares, qkv, ckv, layer, dx, genc, gin, gout, load_sem, sem,
+):
+    seq_count, part, width = weights.shape[1:]
+    loads = [pltpu.make_async_copy(weights_hbm.at[i], weights.at[i], load_sem.at[i]) for i in range(6)] + [
+        pltpu.make_async_copy(dekv_hbm, dekv, load_sem.at[6]), pltpu.make_async_copy(enc_hbm, enc, load_sem.at[7])
+    ]
+    through = ((gout_hbm, gout, gout_out), (gin_hbm, gin, gin_out), (dx_hbm, dx, dx_out), (layer_hbm, layer, layer_out),
+               (genc_hbm, genc, genc_out))
+    loads += [pltpu.make_async_copy(src, held, load_sem.at[8 + i]) for i, (src, held, _) in enumerate(through)]
+    for load in loads:
+        load.start()
+    copies = []
+
+    def store(src, dst):
+        copy = pltpu.make_async_copy(src, dst, sem.at[len(copies)])
+        copy.start()
+        copies.append(copy)
+
+    gains_out[...] = small_ref[0:3, :width]
+    router_out[...] = small_ref[4 : 4 + experts, :width]
+    heads, buckets = rel_out.shape
+    rel_out[0:8, :] = small_ref[0:8, width : width + buckets]
+    rel_out[8:heads, :] = small_ref[0 : heads - 8, width + LANES : width + LANES + buckets]
+    for i, out in enumerate((so_hbm, cq_hbm, co_hbm)):
+        loads[i].wait()
+        squares[i] = weights[i].reshape(seq_count * part, width).astype(F32)
+        store(squares.at[i], out)
+    for i, (_, held, out) in enumerate(through):
+        loads[8 + i].wait()
+        store(held, out)
+    for i in range(3):
+        loads[3 + i].wait()
+        at = slice(i * width, (i + 1) * width)
+        for block in range(width // LANES):
+            rows = slice(block * LANES, (block + 1) * LANES)
+            qkv[:, i * width + block * LANES : i * width + (block + 1) * LANES] = (
+                weights[3 + i].reshape(seq_count * part, width)[rows, :].astype(F32).T
+            )
+        store(qkv.at[:, at], qkv_hbm.at[:, at])
+    loads[6].wait()
+    loads[7].wait()
+    for n in range(2):
+        at = slice(n * width, (n + 1) * width)
+        ckv[:, at] = tn(enc[...], dekv[...].reshape(enc.shape[0], 2 * width)[:, at])
+        store(ckv.at[:, at], ckv_hbm.at[:, at])
+    for copy in copies:
+        copy.wait()
+
+
+def finish_call(heads, buckets, experts, weights, dekv, enc, small, layer, dx, genc, gin, gout):
+    seq_count, part, width = weights.shape[1:]
+    shape = jax.ShapeDtypeStruct
+    f32 = lambda *n: shape(n, F32)
+    return pl.pallas_call(
+        functools.partial(finish_kernel, experts),
+        out_shape=(
+            shape(layer.shape, BF16), f32(*dx.shape), f32(*genc.shape), f32(3, width), f32(width, 3 * width), f32(width, width),
+            f32(width, width), f32(width, 2 * width), f32(width, width), f32(heads, buckets), f32(experts, width),
+            f32(*gin.shape), f32(*gout.shape),
+        ),
+        in_specs=[ANY, ANY, ANY, VMEM, ANY, ANY, ANY, ANY, ANY],
+        out_specs=(ANY, ANY, ANY, VMEM, ANY, ANY, ANY, ANY, ANY, VMEM, VMEM, ANY, ANY),
+        scratch_shapes=[
+            pltpu.VMEM(weights.shape, BF16), pltpu.VMEM(dekv.shape, BF16), pltpu.VMEM(enc.shape, BF16),
+            pltpu.VMEM((3, width, width), F32), pltpu.VMEM((width, 3 * width), F32), pltpu.VMEM((width, 2 * width), F32),
+            pltpu.VMEM(layer.shape, BF16), pltpu.VMEM(dx.shape, F32), pltpu.VMEM(genc.shape, F32), pltpu.VMEM(gin.shape, F32),
+            pltpu.VMEM(gout.shape, F32), pltpu.SemaphoreType.DMA((13,)), pltpu.SemaphoreType.DMA((13,)),
+        ],
+        compiler_params=pltpu.CompilerParams(vmem_limit_bytes=60 << 20),
+        name="finish",
+    )(weights, dekv, enc, small, layer, dx, genc, gin, gout)
+
+
 def fused(inputs, encoder, lengths, buckets, routes, norm_gains, self_qkv, self_out, cross_q, cross_kv, cross_out,
           rel_bias, router, expert_in, expert_out, cotangent):
     seq_count = lax.axis_size("seq")
-    seq_index = lax.axis_index("seq")
     rows, width = inputs.shape[1:]
     experts = router.shape[1]
     capacity = 5 * rows // (4 * experts)
-    stride = -(-capacity // 16) * 16
-    (n1_all, kv_all, prob, cross_prob, ekv, q, o, n2, qc, oc, x3, r1, r2, gates, place, xs, dms) = forward_call(
-        seq_count, capacity, stride, inputs[0], encoder, lengths, buckets[None, :], routes[0], norm_gains, self_qkv,
-        self_out, cross_q, cross_kv, cross_out, rel_bias, router, cotangent[0])
-    pairs = width // LANES
-    hidden = inputs[0].astype(F32)
-    upstream = cotangent[0].astype(F32)
-    a2a = lambda v: lax.all_to_all(v.reshape(experts, stride, width), "exp", split_axis=0, concat_axis=0, tiled=True)
-    arrived = a2a(xs).reshape(-1, width)
-    grad_arrived = a2a(dms).reshape(-1, width)
-    hid, gelu_back = jax.vjp(lambda v: jax.nn.gelu(v, approximate=True), nn(arrived, expert_in[0]))
-    act = hid.astype(BF16)
-    made = nn(act, expert_out[0]).astype(BF16)
-    expert_rows = nn(place, a2a(made).reshape(-1, width))
-    chosen = (routes[0] == jnp.arange(experts)[None, :])
-    picked = jnp.sum(jnp.where(chosen, gates, 0.0), axis=1, keepdims=True)
-    kept = jnp.sum(place.astype(F32), axis=1, keepdims=True)
-    layer_out = r2 + picked * kept * expert_rows
-    dh = gelu_back(nt(grad_arrived, expert_out[0]))[0].astype(BF16)
-    gout = tn(act, grad_arrived)
-    gin = tn(arrived, dh)
-    dx3 = nn(place, a2a(nt(dh, expert_in[0]).astype(BF16)).reshape(-1, width))
-    expert_sums = (
-        lax.psum_scatter(gin[None], "seq", scatter_dimension=1, tiled=True),
-        lax.psum_scatter(gout[None], "seq", scatter_dimension=1, tiled=True),
-    )
-    gate_grad = jnp.sum(upstream * expert_rows, axis=1, keepdims=True) * kept
-    dl = gates * (jnp.where(chosen, gate_grad, 0.0) - picked * gate_grad)
-    router_grad = jnp.dot(x3.astype(F32).T, dl, precision=highest)
-    dx3 = dx3 + jnp.dot(dl, router.astype(F32).T, precision=highest)
-    _, back3 = jax.vjp(rms_norm, r2, norm_gains[2])
-    dr2, gain3 = back3(dx3)
-    dr2 = dr2 + upstream
-    do2 = dr2.astype(BF16)
-    cross_out_grad = tn(oc, do2)
-    doc2 = nt(do2, cross_out).astype(BF16)
-    heads = lambda v: v.reshape(v.shape[0], H, HD)
-    unstack = lambda v: v.reshape(pairs, -1, 2, rows).transpose(0, 2, 1, 3).reshape(H, -1, rows)
-    pc = unstack(cross_prob).astype(F32)
-    kc, vc = heads(ekv[:, :width]), heads(ekv[:, width:])
-    dp = jnp.einsum("qhd,khd->hkq", heads(doc2), vc, preferred_element_type=F32)
-    dc = (pc * (dp - jnp.sum(pc * dp, axis=1, keepdims=True))).astype(BF16)
-    dqc = (jnp.einsum("hkq,khd->qhd", dc, kc, preferred_element_type=F32) * 0.125).reshape(rows, width).astype(BF16)
-    dkc = jnp.einsum("hkq,qhd->khd", dc, heads(qc), preferred_element_type=F32).reshape(-1, width)
-    dvc = jnp.einsum("hkq,qhd->khd", pc.astype(BF16), heads(doc2), preferred_element_type=F32).reshape(-1, width)
-    dekv = lax.psum_scatter(jnp.concatenate([dkc, dvc], axis=1), ("seq", "exp"), scatter_dimension=0, tiled=True).astype(BF16)
-    enc_count = dekv.shape[0]
-    flat_index = seq_index * lax.axis_size("exp") + lax.axis_index("exp")
-    own_enc = lax.dynamic_slice_in_dim(encoder, flat_index * enc_count, enc_count, 0)
-    grad_encoder = nt(dekv, cross_kv)
-    pair_grad = tn(own_enc, dekv)
-    cq_grad = tn(n2, dqc)
-    _, back2 = jax.vjp(rms_norm, r1, norm_gains[1])
-    dr1, gain2 = back2(nt(dqc, cross_q))
-    dr1 = dr1 + dr2
-    do1 = dr1.astype(BF16)
-    self_out_grad = tn(o, do1)
-    dob = nt(do1, self_out).astype(BF16)
-    pr = unstack(prob).astype(F32)
-    k, v = heads(kv_all[:, :width]), heads(kv_all[:, width:])
-    dp = jnp.einsum("qhd,khd->hkq", heads(dob), v, preferred_element_type=F32)
-    ds = (pr * (dp - jnp.sum(pr * dp, axis=1, keepdims=True))).astype(BF16)
-    dq = (jnp.einsum("hkq,khd->qhd", ds, k, preferred_element_type=F32) * 0.125).reshape(rows, width).astype(BF16)
-    dk = jnp.einsum("hkq,qhd->khd", ds, heads(q), preferred_element_type=F32).reshape(-1, width)
-    dv = jnp.einsum("hkq,qhd->khd", pr.astype(BF16), heads(dob), preferred_element_type=F32).reshape(-1, width)
-    dkv = lax.psum_scatter(jnp.concatenate([dk, dv], axis=1), "seq", scatter_dimension=0, tiled=True).astype(BF16)
-    distance = jnp.clip(seq_index * rows + jnp.arange(rows)[None, :] - jnp.arange(seq_count * rows)[:, None], 0, 127)
-    table_grad = jax.vmap(lambda d: jnp.zeros((128,), F32).at[distance.reshape(-1)].add(d.reshape(-1).astype(F32)))(ds)
-    bucket_pick = (buckets[:, None] == jnp.arange(rel_bias.shape[0])[None, :]).astype(F32)
-    rel_grad = jnp.dot(bucket_pick.T, table_grad.T, precision=highest)
-    dqkv = jnp.concatenate([dq, dkv], axis=1)
-    qkv_grad = tn(n1_all[seq_index], dqkv)
-    _, back1 = jax.vjp(rms_norm, hidden, norm_gains[0])
-    dx, gain1 = back1(nt(dqkv, self_qkv))
-    grad_input = dx + dr1
-    summed = lax.psum((jnp.stack([gain1, gain2, gain3]), qkv_grad, self_out_grad, cq_grad, pair_grad, cross_out_grad,
-                       rel_grad, router_grad), ("seq", "exp"))
-    return (layer_out.astype(BF16)[None], grad_input[None], grad_encoder, *summed, *expert_sums)
+    buckets = buckets[None, :]
+    router = router.T
+    (n1_all, kv_all, prob, cross_prob, ekv, q, o, n2, qc, oc, x3, r1, r2, gates, chosen, slots, xs, dms) = forward_call(
+        seq_count, capacity, inputs[0], encoder, lengths, buckets, routes.reshape(1, rows), norm_gains, self_qkv,
+        self_out, cross_q, cross_kv, cross_out, rel_bias.T, router, cotangent[0])
+    made, dxb, x_all, dm_all = experts_call(seq_count, capacity, width, xs, dms, expert_in[0], expert_out[0])
+    (layer_out, grad_input, weights, dekv, small, gin, gout, grad_encoder) = backward_call(
+        seq_count, experts, made, dxb, cotangent[0], inputs[0], r1, r2, gates, chosen, slots, x3, n2, o, oc, q, qc, norm_gains,
+        router, buckets, kv_all, prob, cross_prob, ekv, cross_out, cross_q, self_out, self_qkv, n1_all, x_all, dm_all,
+        expert_in[0], expert_out[0], cross_kv)
+    (layer_out, grad_input, grad_encoder, gains, g_qkv, g_so, g_cq, g_ckv, g_co, g_rel, g_router, gin, gout) = finish_call(
+        rel_bias.shape[1], rel_bias.shape[0], experts, weights, dekv, encoder, small, layer_out, grad_input, grad_encoder, gin,
+        gout)
+    return (layer_out[None], grad_input[None], grad_encoder, gains, g_qkv, g_so, g_cq, g_ckv, g_co, g_rel.T, g_router.T,
+            gin[None], gout[None])
 
 
 def on_device(*operands):
-    if lax.axis_size("seq") * operands[0].shape[1] <= 1024 and lax.axis_size("seq") % 2 == 0:
+    if lax.axis_size("seq") == 8 and lax.axis_size("exp") == 4 and operands[0].shape[1] == 128:
         return fused(*operands)
     return streamed(*operands)
 

time: 1300 us -> 188 us (0.14)
  other arithmetic: 906 us -> 0 us
  Pallas kernels: 32.4 us -> 187 us
  waiting for transfers between devices: 119 us -> 0 us
  local copies, waits for them, and re-layouts: 83.5 us -> 0 us
  matrix products: 72.6 us -> 0 us
  blocking collectives: 40.6 us -> 0 us
  starting transfers between devices: 20.5 us -> 0 us
  between operations: 14.8 us -> 0.87 us
    scatter-add x1 -> x0, other arithmetic: 885 us -> none  [fused(): jnp.zeros((128,), F32).at[distance.reshape(-1)]]
    pallas_call x1 -> x4, Pallas kernels: 32.4 us -> 187 us  [the longest x1 112 us: backward_call(): pl.pallas_call(functools.partial(backward_kernel, seq_count, experts), ou...]
    dot_general x29 -> x0, matrix products: 72.6 us -> none  [the longest x7 29.8 us: tn(): lax.dot_general(a, b, (((0,), (0,)), ((), ())), preferred_element_type=F32)]
    reduce_scatter x3 -> x0, waiting for transfers between devices: 58.8 us -> none  [the longest x1 58.8 us: fused(): lax.psum_scatter(jnp.concatenate([dk, dv], axis=1), 'seq', scatter_dimens...]
    unnamed x6 -> x0, waiting for transfers between devices: 53.3 us -> none
    psum x1 -> x0, blocking collectives: 40.6 us -> none  [fused(): lax.psum((jnp.stack([gain1, gain2, gain3]), qkv_grad, self_out_grad, cq_g...]
    unnamed x115 -> x0, local copies, waits for them, and re-layouts: 34.5 us -> none
    convert_element_type x3 -> x0, local copies, waits for them, and re-layouts: 31.5 us -> none  [the longest x1 28.6 us: fused(): d.reshape(-1).astype(F32)]
  transfers between devices with their start and end apart: 9 -> 0, of which waited for: 4 -> 0; matrix products, arithmetic and copies ran while one was open for 79% -> 0% of each run, Pallas kernels for 0% -> 0%
where the time goes in v3:
time: 188 us
  Pallas kernels  187 us (99%)
    pallas_call x1, Pallas kernels, backward_call(): pl.pallas_call(functools.partial(backward_kernel, seq_count, experts), ou...  112 us
    pallas_call x1, Pallas kernels, experts_call(): pl.pallas_call(functools.partial(experts_kernel, seq_count, experts, slot...  32.5 us
    pallas_call x1, Pallas kernels, forward_call(): pl.pallas_call(functools.partial(forward_kernel, seq_count, capacity), ou...  29.1 us
    pallas_call x1, Pallas kernels, finish_call(): pl.pallas_call(functools.partial(finish_kernel, experts), out_shape=(shap...  13.4 us

profile of v3, /device:TPU:0, one launch (start us, length us, event | category | flops | bytes accessed | tf_op | source)
XLA Modules:
  0.0 187.7 jit_solution(17767518481701831738)
XLA Ops:
  0.6 29.1 %forward.1 = (bf16[8,128,768]{2,1,0:T(8,128)(2,1)}, bf16[1024,1536]{1,0:T(8,128)(2,1)}, bf16[6,1024,256]{2,1,0:T(8,128)(2,1)}, bf16[6,512,256]{2,1,0:T(8,128)(2,...) custom-call(bf16[128,768]{1,0:T(8,128)(2,1)} %bitcast.18, ...), custom_call_target="tpu_custom_call" | custom-call | tf_op jit(solution)/shard_map/forward/pallas_call | solution.py:819
  29.8 32.5 %experts.1 = (bf16[160,768]{1,0:T(8,128)(2,1)}, bf16[160,768]{1,0:T(8,128)(2,1)}, bf16[8,160,768]{2,1,0:T(8,128)(2,1)}, bf16[8,160,768]{2,1,0:T(8,128)(2,1)}) custom-call(bf16[4,240,128]{2,1,0:T(8,128)(2,1)} %get-tuple-element.56.xs_ref, bf16[4,240,128]{2,1,0:T(8,128)(2,1)} %get-tuple-element.57.dms_ref, bf16[768,3072]{1,0:T(8,128)(2,1)} %bitcast.14, ...), custom_call_target="tpu_custom_call" | custom-call | tf_op jit(solution)/shard_map/experts/pallas_call | solution.py:946
  62.2 111.8 %backward.1 = (bf16[128,768]{1,0:T(8,128)(2,1)}, f32[128,768]{1,0:T(8,128)}, bf16[6,8,96,768]{3,2,1,0:T(8,128)(2,1)}, bf16[8,4,16,1536]{3,2,1,0:T(8,128)(2,1)}, ...) custom-call(bf16[160,768]{1,0:T(8,128)(2,1)} %get-tuple-element.58.made_ref, ...), custom_call_target="tpu_custom_call" | custom-call | tf_op jit(solution)/shard_map/backward/pallas_call | solution.py:1401
  174.0 13.4 %finish.1 = (bf16[128,768]{1,0:T(8,128)(2,1)}, f32[128,768]{1,0:T(8,128)}, f32[16,768]{1,0:T(8,128)}, f32[3,768]{1,0:T(4,128)}, f32[768,2304]{1,0:T(8,128)}, /*i...) custom-call(bf16[6,8,96,768]{3,2,1,0:T(8,128)(2,1)} %get-tuple-eleme, ...), custom_call_target="tpu_custom_call" | custom-call | tf_op jit(solution)/shard_map/finish/pallas_call | solution.py:1492

commit v4 on v0

--- a/solution.py
+++ b/solution.py
@@ -1,8 +1,11 @@
+import functools
 import math
 
 import jax
 import jax.numpy as jnp
 from jax import lax
+from jax.experimental import pallas as pl
+from jax.experimental.pallas import tpu as pltpu
 from jax.sharding import PartitionSpec as P
 
 H = 12
@@ -105,7 +108,7 @@
     return result
 
 
-def on_device(
+def streamed(
     inputs,
     encoder,
     lengths,
@@ -453,6 +456,1046 @@
     )
 
 
+F32 = jnp.float32
+BF16 = jnp.bfloat16
+MESH = pl.DeviceIdType.MESH
+ANY = pl.BlockSpec(memory_space=pl.ANY)
+VMEM = pl.BlockSpec(memory_space=pltpu.VMEM)
+SMEM = pl.BlockSpec(memory_space=pltpu.SMEM)
+LANES = 128
+
+
+def nn(a, b):
+    return lax.dot_general(a, b, (((1,), (0,)), ((), ())), preferred_element_type=F32)
+
+
+def nt(a, b):
+    return lax.dot_general(a, b, (((1,), (1,)), ((), ())), preferred_element_type=F32)
+
+
+def tn(a, b):
+    return lax.dot_general(a, b, (((0,), (0,)), ((), ())), preferred_element_type=F32)
+
+
+def rms_scale(a):
+    return lax.rsqrt(jnp.mean(a * a, axis=-1, keepdims=True) + epsilon)
+
+
+def pair_lanes(p):
+    return pl.ds(pl.multiple_of(p * LANES, LANES), LANES)
+
+
+def block_of(index, size):
+    return pl.ds(pl.multiple_of(index * size, size), size)
+
+
+def head_stack(pair):
+    lane = lax.broadcasted_iota(jnp.int32, pair.shape, 1)
+    zero = jnp.zeros_like(pair)
+    return jnp.concatenate([jnp.where(lane < HD, pair, zero), jnp.where(lane < HD, zero, pair)], axis=0)
+
+
+def head_unstack(both, rows):
+    feature = lax.broadcasted_iota(jnp.int32, (both.shape[0], rows), 0)
+    return jnp.where(feature < HD, both[:, :rows], both[:, rows:]).T
+
+
+def pack_slots(value, experts):
+    slots = value.shape[0] // experts
+    blocks = value.shape[1] // LANES
+    return jnp.stack([
+        jnp.concatenate(
+            [value[e * slots : (e + 1) * slots, b * LANES : (b + 1) * LANES] for b in range(blocks)], axis=0
+        )
+        for e in range(experts)
+    ])
+
+
+def unpack_slots(packed, slots):
+    experts, blocks = packed.shape[0], packed.shape[1] // slots
+    wide = packed.astype(F32)
+    return jnp.concatenate(
+        [
+            jnp.concatenate([wide[e, b * slots : (b + 1) * slots] for e in range(experts)], axis=0)
+            for b in range(blocks)
+        ],
+        axis=1,
+    )
+
+
+class Place:
+    def __init__(self):
+        self.me = lax.axis_index("seq")
+        self.core = lax.rem(self.me, 2)
+        self.chip = lax.div(self.me, 2)
+        self.partner = self.me + 1 - 2 * self.core
+        self.x_chip = self.chip + 1 - 2 * lax.rem(self.chip, 2)
+        self.y_chip = lax.rem(self.chip + 2, 4)
+        self.far_chip = 3 - self.chip
+        self.x, self.y, self.far = (c * 2 + self.core for c in (self.x_chip, self.y_chip, self.far_chip))
+
+
+def enter(devices):
+    barrier = pltpu.get_barrier_semaphore()
+    for device in devices:
+        pl.semaphore_signal(barrier, inc=1, device_id=device, device_id_type=MESH)
+    pl.semaphore_wait(barrier, len(devices))
+
+
+def remote(src, dst, send_sem, recv_sem, device):
+    return pltpu.make_async_remote_copy(
+        src_ref=src, dst_ref=dst, send_sem=send_sem, recv_sem=recv_sem, device_id=device, device_id_type=MESH
+    )
+
+
+class Gather:
+    def __init__(self, place, every, rows, sends, recvs):
+        self.place, self.every, self.sends, self.recvs = place, every, sends, recvs
+        half = rows // 2 if rows < 32 else -(-rows // 32) * 16
+        self.halves = pl.ds(0, half), pl.ds(half, rows - half)
+
+    def copy(self, slot):
+        place, every = self.place, self.every
+        block, device = (
+            lambda: (every.at[place.me], place.partner),
+            lambda: (every.at[place.me], place.x),
+            lambda: (every.at[place.me], place.y),
+            lambda: (every.at[place.x, self.halves[0]], place.y),
+            lambda: (every.at[place.y, self.halves[1]], place.x),
+            lambda: (every.at[place.x], place.partner),
+            lambda: (every.at[place.y], place.partner),
+            lambda: (every.at[place.far], place.partner),
+        )[slot]()
+        return remote(block, block, self.sends.at[slot], self.recvs.at[slot], {"seq": device})
+
+    def send(self, *slots):
+        for slot in slots:
+            self.copy(slot).start()
+
+    def wait(self, *slots):
+        for slot in slots:
+            self.copy(slot).wait_recv()
+
+    def start(self):
+        self.send(1, 2, 0)
+
+    def relay(self):
+        self.wait(1)
+        self.send(3)
+        self.wait(2)
+        self.send(4, 5, 6)
+
+    def relay_far(self):
+        self.wait(3, 4)
+        self.send(7)
+
+    def finish(self):
+        self.wait(0, 5, 6, 7)
+
+    def drain(self):
+        for slot in range(8):
+            self.copy(slot).wait_send()
+
+
+class Scatter:
+    def __init__(self, place, out, pair, turn, side, half, sems):
+        self.place, self.out, self.pair, self.turn, self.side, self.half = place, out, pair, turn, side, half
+        self.pair_sems, self.turn_sems, self.side_sems = sems
+
+    def pair_copy(self):
+        send, recv = self.pair_sems
+        return remote(self.out.at[1 - self.place.core], self.pair, send, recv, {"seq": self.place.partner})
+
+    def turn_copies(self):
+        place = self.place
+        send, recv = self.turn_sems
+        far = self.out.at[place.core, place.far_chip]
+        return (
+            remote(far.at[pl.ds(0, self.half)], self.turn.at[0], send.at[0], recv.at[0], {"seq": place.x}),
+            remote(far.at[pl.ds(self.half, self.half)], self.turn.at[1], send.at[1], recv.at[1], {"seq": place.y}),
+        )
+
+    def side_copies(self):
+        place = self.place
+        send, recv = self.side_sems
+        return (
+            remote(self.out.at[place.core, place.x_chip], self.side.at[0], send.at[0], recv.at[0], {"seq": place.x}),
+            remote(self.out.at[place.core, place.y_chip], self.side.at[1], send.at[1], recv.at[1], {"seq": place.y}),
+        )
+
+    def start(self):
+        self.pair_copy().start()
+
+    def turn_on(self):
+        core = self.place.core
+        self.pair_copy().wait_recv()
+        self.out[core] = (self.out[core].astype(F32) + self.pair[...].astype(F32)).astype(BF16)
+        for copy in self.turn_copies():
+            copy.start()
+
+    def side_on(self):
+        place = self.place
+        first, second = pl.ds(0, self.half), pl.ds(self.half, self.half)
+        from_x, from_y = self.turn_copies()
+        from_x.wait_recv()
+        at = (place.core, place.y_chip, first)
+        self.out[at] = (self.out[at].astype(F32) + self.turn[0].astype(F32)).astype(BF16)
+        from_y.wait_recv()
+        at = (place.core, place.x_chip, second)
+        self.out[at] = (self.out[at].astype(F32) + self.turn[1].astype(F32)).astype(BF16)
+        for copy in self.side_copies():
+            copy.start()
+
+    def total(self):
+        for copy in self.side_copies():
+            copy.wait_recv()
+        own = self.out[self.place.core, self.place.chip].astype(F32)
+        return own + self.side[0].astype(F32) + self.side[1].astype(F32)
+
+    def drain(self):
+        self.pair_copy().wait_send()
+        for copy in self.turn_copies() + self.side_copies():
+            copy.wait_send()
+
+
+def expert_peers(exp_index, experts):
+    return [lax.rem(exp_index + d, experts) for d in range(1, experts)]
+
+
+def gelu_parts(hid):
+    root, cubic = 0.7978845608028654, 0.044715
+    square = hid * hid
+    bent = jnp.tanh(root * hid * (1.0 + cubic * square))
+    half = 0.5 * (1.0 + bent)
+    return hid * half, half + 0.5 * hid * (1.0 - bent * bent) * (root + 3.0 * root * cubic * square)
+
+
+def rms_back(a, gain, grad):
+    scale = rms_scale(a)
+    weighted = grad * gain
+    da = scale * weighted - a * (scale * scale * scale * jnp.mean(a * weighted, axis=-1, keepdims=True))
+    return da, jnp.sum(grad * (a * scale), axis=0, keepdims=True)
+
+
+def in_two(value):
+    high = value.astype(BF16)
+    return high, (value - high.astype(F32)).astype(BF16)
+
+
+GATE_ROWS = 16
+
+
+def in_three(value):
+    high = value.astype(BF16)
+    rest = value - high.astype(F32)
+    middle = rest.astype(BF16)
+    low = (rest - middle.astype(F32)).astype(BF16)
+    lane = lax.broadcasted_iota(jnp.int32, (value.shape[0], GATE_ROWS), 1)
+    zero = jnp.zeros((value.shape[0], GATE_ROWS), BF16)
+    return jnp.where(lane == 0, high, jnp.where(lane == 1, middle, jnp.where(lane == 2, low, zero)))
+
+
+def slot_gates(parts):
+    return jnp.sum(parts, axis=0, keepdims=True).T
+
+
+class Chunk:
+    def __init__(self, place, quarters, mine, peers, src, slots, own, every, sems, gather_sems, local_sem):
+        self.place, self.quarters, self.mine, self.peers = place, quarters, mine, peers
+        self.src, self.slots, self.own, self.every = src, slots, own, every
+        self.scatter_sems, self.gather_sems, self.local_sem = sems[:2], sems[2:], local_sem
+        self.over_seq = Gather(place, every, src.shape[0], *gather_sems)
+
+    def scatter_copies(self):
+        send, recv = self.scatter_sems
+        return [
+            remote(self.src.at[self.quarters[1 + d]], self.slots.at[d], send.at[d], recv.at[d], {"exp": peer})
+            for d, peer in enumerate(self.peers)
+        ]
+
+    def gather_copies(self):
+        send, recv = self.gather_sems
+        target = self.every.at[(self.place.me,) + self.quarters[0]]
+        return [remote(self.own, target, send.at[d], recv.at[d], {"exp": peer}) for d, peer in enumerate(self.peers)]
+
+    def local_copy(self):
+        return pltpu.make_async_copy(self.own, self.every.at[(self.place.me,) + self.quarters[0]], self.local_sem)
+
+    def over_exp(self, value):
+        self.src[...] = value.astype(BF16)
+        for copy in self.scatter_copies():
+            copy.start()
+
+    def back_over_exp(self):
+        total = self.src[self.quarters[0]].astype(F32)
+        for d, copy in enumerate(self.scatter_copies()):
+            copy.wait_recv()
+            total = total + self.slots[d].astype(F32)
+        self.own[...] = total.astype(BF16)
+        self.local_copy().start()
+        for copy in self.gather_copies():
+            copy.start()
+
+    def spread(self):
+        self.local_copy().wait()
+        for copy in self.gather_copies():
+            copy.wait_recv()
+        self.over_seq.start()
+
+    def drain(self):
+        for copy in self.scatter_copies() + self.gather_copies():
+            copy.wait_send()
+        self.over_seq.drain()
+
+
+def layer_kernel(
+    seq_count, capacity,
+    x_ref, encoder_hbm, lengths_ref, buckets_ref, routes_ref, gains_ref, qkv_hbm, so_hbm, cq_hbm, ckv_hbm, co_hbm, rel_ref,
+    router_ref, g_ref, in_hbm, out_hbm,
+    out_ref, dx_ref, weights_hbm, dekv_hbm, small_out_ref, gin_ref, gout_ref, genc_ref,
+    left, kv_all, prob, cross_prob, ekv, w_qkv, w_so, w_cq, w_ckv, w_co, table_ref, x_all, g_all, x_in, g_in, made_back, dx_back,
+    q_ref, qc_ref, x3_ref, r1_ref, r2_ref, gates_ref, chosen_ref, slots_ref,
+    dr_ref, doc_ref, dqc_ref, dqkv_ref, diag_ref, total_ref,
+    e_pair, e_turn, e_side, e_mine, e_exp, dekv, t_pair, t_turn, t_side,
+    c_slots, c_own, right, gin_in, small_a, small_b, small_c, small_pair, small_chip, small_exp,
+    load_sem, local_sem, n_send, n_recv, o_send, o_recv, m_send, m_recv, c_send, c_recv, x_send, x_recv, d_send, d_recv,
+    zx_send, zx_recv, zd_send, zd_recv, zm_send, zm_recv, zg_send, zg_recv,
+    ep_send, ep_recv, et_send, et_recv, es_send, es_recv, ez_send, ez_recv, eg_send, eg_recv, ea_send, ea_recv,
+    tp_send, tp_recv, tt_send, tt_recv, ts_send, ts_recv, cs_send, cs_recv, cg_send, cg_recv, ca_send, ca_recv,
+    r_send, r_recv, g_send, g_recv, s1_send, s1_recv, s2_send, s2_recv, s3_send, s3_recv,
+):
+    rows, width = x_ref.shape
+    span = seq_count * rows
+    pairs = width // LANES
+    enc_rows = encoder_hbm.shape[0]
+    hidden = in_hbm.shape[1]
+    own_hidden = hidden // seq_count
+    place = Place()
+    me = place.me
+    mine = lax.axis_index("exp")
+    experts = router_ref.shape[0]
+    slot_rows = experts * capacity
+    peers = expert_peers(mine, experts)
+    everyone = [lax.rem(me + d, seq_count) for d in range(1, seq_count)]
+    part = width // seq_count
+    half_rows, half_lanes = part // 2, width // (experts // 2)
+    quarters = [
+        (block_of(lax.div(e, experts // 2), half_rows), block_of(lax.rem(e, experts // 2), half_lanes)) for e in [mine] + peers
+    ]
+    at_hidden = block_of(me, own_hidden)
+    own_lanes = block_of(me, rows)
+    near = pl.ds(pl.multiple_of(me * rows, rows), 2 * rows)
+    gather, o_gather, n2_gather, oc_gather = (
+        Gather(place, left.at[i], rows, *sems)
+        for i, sems in ((3, (n_send, n_recv)), (0, (o_send, o_recv)), (1, (m_send, m_recv)), (2, (c_send, c_recv)))
+    )
+    x_gather = Gather(place, x_all, x_all.shape[1], x_send, x_recv)
+    g_gather = Gather(place, g_all, slot_rows, d_send, d_recv)
+
+    def load(i, src, dst):
+        return pltpu.make_async_copy(src, dst, load_sem.at[i])
+
+    def exp_moves(src, dst, send, recv):
+        return [remote(src.at[peer], dst.at[mine], send.at[d], recv.at[d], {"exp": peer}) for d, peer in enumerate(peers)]
+
+    def over_exp(src, dst, send, recv):
+        for copy in exp_moves(src, dst, send, recv):
+            copy.start()
+        dst[mine] = src[mine]
+
+    def arrive(src, dst, send, recv):
+        for copy in exp_moves(src, dst, send, recv):
+            copy.wait_recv()
+
+    load_qkv, load_ckv = load(0, qkv_hbm, w_qkv), load(1, ckv_hbm, w_ckv)
+    load_so, load_cq, load_co = load(3, so_hbm, w_so), load(4, cq_hbm, w_cq), load(5, co_hbm, w_co)
+    load_qkv.start()
+    load_ckv.start()
+
+    def own_slots(e):
+        of_all = lax.broadcasted_iota(jnp.int32, (slot_rows, LANES), 0) - e * capacity
+        lane = lax.broadcasted_iota(jnp.int32, (slot_rows, LANES), 1)
+        return ((of_all == lane) & (lane < capacity)).astype(BF16)
+
+    def self_attention(scores, mask, enc, gs_ref):
+        load_enc = load(2, encoder_hbm, enc)
+        load_enc.start()
+        x = x_ref[...].astype(F32)
+        left[3, me] = (x * rms_scale(x) * gains_ref[0:1, :]).astype(BF16)
+        enter([{"seq": device} for device in everyone] + [{"exp": peer} for peer in peers])
+        gather.start()
+
+        def project(chip):
+            both = left[3, pl.ds(chip * 2, 2)].reshape(2 * rows, width)
+            kv_all[block_of(chip, 2 * rows), :] = nn(both, w_qkv[:, width:]).astype(BF16)
+
+        chosen = (routes_ref[...] == lax.broadcasted_iota(jnp.int32, (LANES, rows), 0)).astype(F32).T[:, :experts]
+        chosen_ref[...] = chosen
+        earlier = (
+            lax.broadcasted_iota(jnp.int32, (rows, rows), 1) < lax.broadcasted_iota(jnp.int32, (rows, rows), 0)
+        ).astype(BF16)
+        slot = jnp.sum(nn(earlier, chosen.astype(BF16)) * chosen, axis=1, keepdims=True).astype(jnp.int32)
+        kept = slot < capacity
+        expert = lax.broadcasted_iota(jnp.int32, (rows, experts), 1).astype(F32)
+        route = jnp.sum(chosen * expert, axis=1, keepdims=True).astype(jnp.int32)
+        target = jnp.where(kept, route * capacity + slot, -1)
+        slots = (lax.broadcasted_iota(jnp.int32, (rows, slot_rows), 1) == target).astype(BF16)
+        slots_ref[...] = slots
+        gs_ref[...] = pack_slots(tn(slots, g_ref[...]), experts).astype(BF16)
+        g_trip = (gs_ref, g_in, zd_send, zd_recv)
+        over_exp(*g_trip)
+
+        load_qkv.wait()
+        q_ref[...] = nn(left[3, me], w_qkv[:, :width]).astype(BF16) * jnp.asarray(0.125, BF16)
+        gather.wait(0)
+        project(place.chip)
+        load_so.start()
+        load_cq.start()
+        load_co.start()
+        load_ckv.wait()
+        load_enc.wait()
+        ekv[...] = nn(enc[...], w_ckv[...]).astype(BF16)
+        gather.relay()
+        pick = (buckets_ref[...] == lax.broadcasted_iota(jnp.int32, (rel_ref.shape[1], LANES), 0)).astype(F32)
+        table = jnp.dot(rel_ref[...], pick, precision=highest, preferred_element_type=F32)
+        table = table - table[:, LANES - 1 :]
+        table_ref[...] = jnp.concatenate([jnp.zeros_like(table), table], axis=1)
+        query_pos = me * rows + lax.broadcasted_iota(jnp.int32, (1, rows), 1)
+        start = jnp.zeros((1, rows), jnp.int32)
+        end = jnp.int32(0)
+        for i in range(lengths_ref.shape[1]):
+            end = end + lengths_ref[0, i]
+            start = jnp.where(end <= query_pos, end, start)
+        key_pos = lax.broadcasted_iota(jnp.int32, (span, rows), 0)
+        seen = jnp.where((key_pos >= start) & (key_pos <= query_pos), 0.0, masked_out)
+        mask[...] = jnp.concatenate([seen, seen], axis=1)
+        gather.wait(5, 6)
+        project(place.x_chip)
+        project(place.y_chip)
+        gather.relay_far()
+        arrive(*g_trip)
+        g_all[me] = unpack_slots(g_in[...], capacity).astype(BF16)
+        g_gather.start()
+        gather.wait(7)
+        project(place.far_chip)
+
+        @pl.loop(0, pairs)
+        def _(p):
+            lanes = pair_lanes(p)
+            q_both = head_stack(q_ref[:, lanes])
+            scores[pl.ds(rows, span), :] = nt(kv_all[:, lanes], q_both) + mask[...]
+            biases = []
+            for h in range(2):
+                band = jnp.broadcast_to(table_ref[pl.ds(2 * p + h, 1), :], (2 * rows, 2 * LANES))
+                biases.append(pltpu.roll(band, 0, 1, stride=1, stride_axis=0)[:, :rows])
+            scores[near, :] = scores[near, :] + jnp.concatenate(biases, axis=1)
+            s = scores[pl.ds(rows, span), :]
+            weights = jnp.exp(s - jnp.max(s, axis=0, keepdims=True))
+            weights = (weights * (1.0 / jnp.sum(weights, axis=0, keepdims=True))).astype(BF16)
+            prob[p] = weights
+            both = tn(kv_all[:, pair_lanes(pairs + p)], weights)
+            left[0, me, :, lanes] = head_unstack(both, rows).astype(BF16)
+
+        for copy in exp_moves(*g_trip):
+            copy.wait_send()
+
+    def rest_forward(xs_ref, made_out, dx_out, slope, w_in, w_out):
+        load_in, load_out = load(6, in_hbm, w_in), load(7, out_hbm, w_out)
+        load_in.start()
+        load_out.start()
+        o_gather.start()
+        g_gather.relay()
+        load_so.wait()
+        load_cq.wait()
+        load_co.wait()
+        r1 = x_ref[...].astype(F32) + nn(left[0, me], w_so[...])
+        r1_ref[...] = r1
+        n2 = (r1 * rms_scale(r1) * gains_ref[1:2, :]).astype(BF16)
+        left[1, me] = n2
+        n2_gather.start()
+        qc_ref[...] = nn(n2, w_cq[...]).astype(BF16) * jnp.asarray(0.125, BF16)
+
+        @pl.loop(0, pairs)
+        def _(p):
+            lanes = pair_lanes(p)
+            s = nt(ekv[:, lanes], head_stack(qc_ref[:, lanes]))
+            weights = jnp.exp(s - jnp.max(s, axis=0, keepdims=True))
+            weights = (weights * (1.0 / jnp.sum(weights, axis=0, keepdims=True))).astype(BF16)
+            cross_prob[p] = weights
+            both = tn(ekv[:, pair_lanes(pairs + p)], weights)
+            left[2, me, :, lanes] = head_unstack(both, rows).astype(BF16)
+
+        oc_gather.start()
+        r2 = r1_ref[...] + nn(left[2, me], w_co[...])
+        r2_ref[...] = r2
+        x3 = (r2 * rms_scale(r2) * gains_ref[2:3, :]).astype(BF16)
+        x3_ref[...] = x3
+        logits = nt(x3, router_ref[...])
+        top = jnp.exp(logits - jnp.max(logits, axis=-1, keepdims=True))
+        gates = top / jnp.sum(top, axis=-1, keepdims=True)
+        gates_ref[...] = gates
+        chosen, slots = chosen_ref[...], slots_ref[...]
+        kept = jnp.sum(slots.astype(F32), axis=1, keepdims=True)
+        gate_used = jnp.sum(gates * chosen, axis=1, keepdims=True) * kept
+        packed_rows = x_in.shape[1] - GATE_ROWS
+        xs_ref[:, :packed_rows, :] = pack_slots(tn(slots, x3), experts).astype(BF16)
+        by_slot = tn(in_three(gate_used), slots).astype(BF16)
+        for e in range(experts):
+            xs_ref[e, packed_rows:, :] = nn(by_slot, own_slots(e)).astype(BF16)
+        x_trip = (xs_ref, x_in, zx_send, zx_recv)
+        over_exp(*x_trip)
+
+        o_gather.relay()
+        load_in.wait()
+        load_out.wait()
+        arrive(*x_trip)
+        x_all[me, :slot_rows, :] = unpack_slots(x_in[:, :packed_rows, :], capacity).astype(BF16)
+        gate_parts = jnp.zeros((GATE_ROWS, slot_rows), F32)
+        for e in range(experts):
+            gate_parts = gate_parts + nt(x_in[e, packed_rows:, :], own_slots(e))
+        x_all[me, slot_rows:, :] = jnp.concatenate(
+            [gate_parts, jnp.zeros((GATE_ROWS, width - slot_rows), F32)], axis=1
+        ).astype(BF16)
+        x_gather.start()
+        n2_gather.relay()
+        xs = x_all[me, :slot_rows, :]
+        made = jnp.zeros(xs.shape, F32)
+        for n in range(hidden // width):
+            at = slice(n * width, (n + 1) * width)
+            value, derivative = gelu_parts(nn(xs, w_in[:, at]))
+            slope[:, at] = derivative
+            made = made + nn(value.astype(BF16), w_out[at, :])
+        made_out[...] = pack_slots(made, experts).astype(BF16)
+        made_trip = (made_out, made_back, zm_send, zm_recv)
+        over_exp(*made_trip)
+        dm = (g_all[me].astype(F32) * slot_gates(gate_parts)).astype(BF16)
+        dx = jnp.zeros(dm.shape, F32)
+        for n in range(hidden // width):
+            at = slice(n * width, (n + 1) * width)
+            dh = (nt(dm, w_out[at, :]) * slope[:, at]).astype(BF16)
+            dx = dx + nt(dh, w_in[:, at])
+        dx_out[...] = pack_slots(dx, experts).astype(BF16)
+        dx_trip = (dx_out, dx_back, zg_send, zg_recv)
+        over_exp(*dx_trip)
+        g_gather.relay_far()
+        oc_gather.relay()
+        o_gather.relay_far()
+        n2_gather.relay_far()
+        arrive(*made_trip)
+        arrive(*dx_trip)
+        for trip in (x_trip, made_trip, dx_trip):
+            for copy in exp_moves(*trip):
+                copy.wait_send()
+
+    bf = lambda *n: pltpu.VMEM(n, BF16)
+    f32 = lambda *n: pltpu.VMEM(n, F32)
+    packed = bf(*g_in.shape)
+    pl.run_scoped(self_attention, f32(span + rows, 2 * rows), f32(span, 2 * rows), bf(enc_rows, width), packed)
+    pl.run_scoped(
+        rest_forward, bf(*x_in.shape), packed, packed, f32(slot_rows, hidden), bf(width, hidden), bf(hidden, width)
+    )
+
+    enc_part = enc_rows // seq_count
+    dekv_gather = Gather(place, dekv_hbm, experts, ea_send, ea_recv)
+    started = []
+
+    def send(src, dst, send_sem, recv_sem, device):
+        copy = remote(src, dst, send_sem, recv_sem, device)
+        copy.start()
+        started.append(copy)
+        return copy
+
+    def backward(e_out, t_out, c_src, turned_ref, ds_ref, gin_out, w_ein, w_eout):
+        load_ein, load_eout = load(8, in_hbm.at[:, at_hidden], w_ein), load(9, out_hbm.at[at_hidden, :], w_eout)
+        load_ein.start()
+        load_eout.start()
+        enc_scatter = Scatter(
+            place, e_out, e_pair, e_turn, e_side, e_turn.shape[1],
+            ((ep_send.at[0], ep_recv.at[0]), (et_send, et_recv), (es_send, es_recv)),
+        )
+        chunks = [
+            Chunk(
+                place, quarters, mine, peers, c_src.at[i], c_slots.at[i], c_own.at[i], weights_hbm.at[i],
+                (cs_send.at[i], cs_recv.at[i], cg_send.at[i], cg_recv.at[i]), (ca_send.at[i], ca_recv.at[i]), local_sem.at[i],
+            )
+            for i in range(6)
+        ]
+
+        def enc_over_exp():
+            return [
+                remote(e_mine.at[peer], e_exp.at[d], ez_send.at[d], ez_recv.at[d], {"exp": peer}) for d, peer in enumerate(peers)
+            ]
+
+        def dekv_over_exp():
+            return [
+                remote(dekv, dekv_hbm.at[me, mine], eg_send.at[d], eg_recv.at[d], {"exp": peer}) for d, peer in enumerate(peers)
+            ]
+
+        def dekv_local():
+            return pltpu.make_async_copy(dekv, dekv_hbm.at[me, mine], local_sem.at[6])
+
+        def right_copies(i):
+            return [
+                remote(turned_ref.at[i, block_of(peer, part), :], right.at[i, :, own_lanes], r_send.at[i, d], r_recv.at[i, d],
+                       {"seq": peer})
+                for d, peer in enumerate(everyone)
+            ]
+
+        def exchange(i, factor):
+            turned_ref[i] = factor.T
+            for copy in right_copies(i):
+                copy.start()
+            right[i, :, own_lanes] = turned_ref[i, block_of(me, part), :]
+
+        def multiply(i):
+            for copy in right_copies(i):
+                copy.wait_recv()
+            chunks[i].over_exp(nn(right[i], left[min(i, 3)].reshape(span, width)))
+
+        def gins():
+            return [
+                remote(gin_out.at[peer], gin_in.at[:, at_hidden], g_send.at[d], g_recv.at[d], {"seq": peer})
+                for d, peer in enumerate(everyone)
+            ]
+
+        slots = slots_ref[...]
+        made = nn(slots, unpack_slots(made_back[...], capacity).astype(BF16))
+        kept = jnp.sum(slots.astype(F32), axis=1, keepdims=True)
+        gates = gates_ref[...]
+        chosen = chosen_ref[...]
+        picked = jnp.sum(gates * chosen, axis=1, keepdims=True)
+        g = g_ref[...].astype(F32)
+        out_ref[...] = (r2_ref[...] + (picked * kept) * made).astype(BF16)
+        gate_grad = jnp.sum(g * made, axis=1, keepdims=True) * kept
+        dl = gates * (chosen * gate_grad - picked * gate_grad)
+        dl_high, dl_low = in_two(dl)
+        x3 = x3_ref[...]
+        small_a[...] = jnp.zeros_like(small_a)
+        small_a[4 : 4 + experts, :width] = tn(dl_high, x3) + tn(dl_low, x3)
+        dx3 = (
+            nn(slots, unpack_slots(dx_back[...], capacity).astype(BF16))
+            + nn(dl_high, router_ref[...]) + nn(dl_low, router_ref[...])
+        )
+        da, dw = rms_back(r2_ref[...], gains_ref[2:3, :], dx3)
+        small_a[2:3, :width] = dw
+        dr_ref[...] = g + da
+        do2 = dr_ref[...].astype(BF16)
+        doc_ref[...] = nt(do2, w_co[...]).astype(BF16)
+        exchange(2, do2)
+        x_gather.relay()
+        oc_gather.relay_far()
+
+        @pl.loop(0, pairs)
+        def _(p):
+            lanes, value_lanes = pair_lanes(p), pair_lanes(pairs + p)
+            doc_both = head_stack(doc_ref[:, lanes])
+            weights = cross_prob[p]
+            wide = weights.astype(F32)
+            dp = nt(ekv[:, value_lanes], doc_both)
+            dc = (wide * (dp - jnp.sum(wide * dp, axis=0, keepdims=True))).astype(BF16)
+            dk = nn(dc, head_stack(qc_ref[:, lanes])).astype(BF16).reshape(4, 2, enc_part, LANES)
+            dv = nn(weights, doc_both).astype(BF16).reshape(4, 2, enc_part, LANES)
+            for k in range(2):
+                e_out[k, :, :, lanes] = dk[:, k]
+                e_out[k, :, :, value_lanes] = dv[:, k]
+            dqc_ref[:, lanes] = (head_unstack(tn(ekv[:, lanes], dc), rows) * 0.125).astype(BF16)
+
+        enc_scatter.start()
+        x_gather.relay_far()
+        dqc = dqc_ref[...]
+        exchange(1, dqc)
+        da, dw = rms_back(r1_ref[...], gains_ref[1:2, :], nt(dqc, w_cq[...]))
+        small_a[1:2, :width] = dw
+        enc_scatter.turn_on()
+        dr_ref[...] = dr_ref[...] + da
+        do1 = dr_ref[...].astype(BF16)
+        doc_ref[...] = nt(do1, w_so[...]).astype(BF16)
+        exchange(0, do1)
+        oc_gather.finish()
+        multiply(2)
+        n2_gather.finish()
+        o_gather.finish()
+
+        ds_ref[pl.ds(0, rows), :] = jnp.zeros((rows, 2 * rows), BF16)
+        flip = (
+            lax.broadcasted_iota(jnp.int32, (2 * rows, 2 * rows), 0)
+            + lax.broadcasted_iota(jnp.int32, (2 * rows, 2 * rows), 1)
+            == 2 * rows - 1
+        ).astype(BF16)
+
+        def terms(p):
+            return Scatter(
+                place, t_out.at[p], t_pair.at[p], t_turn.at[p], t_side.at[p], rows // 2,
+                ((tp_send.at[p], tp_recv.at[p]), (tt_send.at[p], tt_recv.at[p]), (ts_send.at[p], ts_recv.at[p])),
+            )
+
+        def pair_back(p):
+            lanes, value_lanes = pair_lanes(p), pair_lanes(pairs + p)
+            do_both = head_stack(doc_ref[:, lanes])
+            weights = prob[p]
+            wide = weights.astype(F32)
+            dp = nt(kv_all[:, value_lanes], do_both)
+            ds_wide = wide * (dp - jnp.sum(wide * dp, axis=0, keepdims=True))
+            ds = ds_wide.astype(BF16)
+            ds_ref[pl.ds(rows, span), :] = ds
+            total_ref[pl.ds(p, 1), :] = jnp.sum(ds.astype(F32), axis=0, keepdims=True)
+            dk = nn(ds, head_stack(q_ref[:, lanes])).astype(BF16).reshape(4, 2, rows, LANES)
+            dv = nn(weights, do_both).astype(BF16).reshape(4, 2, rows, LANES)
+            for k in range(2):
+                t_out[p, k, :, :, :LANES] = dk[:, k]
+                t_out[p, k, :, :, LANES:] = dv[:, k]
+            terms(p).start()
+            dqkv_ref[:, lanes] = (head_unstack(tn(kv_all[:, lanes], ds), rows) * 0.125).astype(BF16)
+            turned = nn(flip, ds_ref[near, :])
+            for h in range(2):
+                one = turned[:, h * rows : (h + 1) * rows]
+                one = jnp.concatenate([one, jnp.zeros_like(one)], axis=1)
+                one = pltpu.roll(one, 1, 1, stride=1, stride_axis=0)
+                diag_ref[pl.ds(2 * p + h, 1), :] = jnp.sum(one, axis=0, keepdims=True)
+
+        def own_terms(p):
+            total = terms(p).total()
+            dqkv_ref[:, pair_lanes(pairs + p)] = total[:, :LANES].astype(BF16)
+            dqkv_ref[:, pair_lanes(2 * pairs + p)] = total[:, LANES:].astype(BF16)
+
+        @pl.loop(0, pairs)
+        def _(t):
+            pair_back(t)
+            @pl.when(t >= 1)
+            def _():
+                terms(jnp.maximum(t - 1, 0)).turn_on()
+
+            @pl.when(t >= 3)
+            def _():
+                terms(jnp.maximum(t - 3, 0)).side_on()
+
+            @pl.when(t >= 5)
+            def _():
+                own_terms(jnp.maximum(t - 5, 0))
+
+            @pl.when(t == 1)
+            def _():
+                enc_scatter.side_on()
+
+            @pl.when(t == 2)
+            def _():
+                multiply(1)
+                chunks[2].back_over_exp()
+
+            @pl.when(t == 3)
+            def _():
+                multiply(0)
+
+            @pl.when(t == 4)
+            def _():
+                e_mine[...] = enc_scatter.total().astype(BF16).reshape(e_mine.shape)
+                for copy in enc_over_exp():
+                    copy.start()
+                chunks[1].back_over_exp()
+
+
+        terms(5).turn_on()
+        terms(3).side_on()
+        own_terms(1)
+        exchange(3, dqkv_ref[:, :width])
+        load_ein.wait()
+        load_eout.wait()
+        x_gather.finish()
+        g_gather.finish()
+        xs = x_all[:, :slot_rows, :].reshape(-1, width)
+        parts = x_all[:, slot_rows:, : 2 * LANES].astype(F32).reshape(seq_count * GATE_ROWS, 2 * LANES).T
+        dm = jnp.concatenate(
+            [
+                (g_all[s].astype(F32) * sum(parts[:slot_rows, s * GATE_ROWS + n : s * GATE_ROWS + n + 1] for n in range(3)))
+                for s in range(seq_count)
+            ],
+            axis=0,
+        ).astype(BF16)
+        value, slope = gelu_parts(nn(xs, w_ein[...]))
+        gout_ref[...] = tn(value.astype(BF16), dm)
+        chunks[0].back_over_exp()
+        chunks[2].spread()
+        terms(4).side_on()
+        terms(5).side_on()
+        own_terms(2)
+        total = e_mine[mine].astype(F32)
+        for d, copy in enumerate(enc_over_exp()):
+            copy.wait_recv()
+            total = total + e_exp[d].astype(F32)
+        dekv[...] = total.astype(BF16)
+        dekv_local().start()
+        for copy in dekv_over_exp():
+            copy.start()
+        dh = (nt(dm, w_eout[...]) * slope).astype(BF16)
+        gin_out[...] = tn(xs, dh).astype(BF16).reshape(gin_out.shape)
+        own_terms(3)
+        multiply(3)
+        chunks[1].spread()
+        own_terms(4)
+        own_terms(5)
+
+        dqkv = dqkv_ref[...]
+        exchange(4, dqkv[:, width : 2 * width])
+        exchange(5, dqkv[:, 2 * width :])
+        x = x_ref[...].astype(F32)
+        da, dw = rms_back(x, gains_ref[0:1, :], nt(dqkv, w_qkv[...]))
+        small_a[0:1, :width] = dw
+        dx_ref[...] = dr_ref[...] + da
+        heads = 2 * pairs
+        table = diag_ref[:, 2 * rows - LANES :]
+        totals = total_ref[...]
+        first = jnp.sum(totals[:, :rows], axis=1, keepdims=True)
+        second = jnp.sum(totals[:, rows:], axis=1, keepdims=True)
+        head = lax.broadcasted_iota(jnp.int32, (heads, pairs), 0)
+        pair = lax.broadcasted_iota(jnp.int32, (heads, pairs), 1)
+        spread = lambda odd, v: jnp.dot(
+            (head == 2 * pair + odd).astype(F32), v, precision=highest, preferred_element_type=F32
+        )
+        whole = spread(0, jnp.broadcast_to(first, (pairs, LANES))) + spread(1, jnp.broadcast_to(second, (pairs, LANES)))
+        rest = whole - jnp.sum(table, axis=1, keepdims=True)
+        lane = lax.broadcasted_iota(jnp.int32, table.shape, 1)
+        table = table + jnp.where(lane == LANES - 1, rest, 0.0)
+        bucket = lax.broadcasted_iota(jnp.int32, (LANES, LANES), 0)
+        pick = (buckets_ref[...] == bucket).astype(F32)
+        by_bucket = lax.dot_general(table, pick, (((1,), (1,)), ((), ())), precision=highest, preferred_element_type=F32)
+        small_a[0:8, width : width + LANES] = by_bucket[0:8]
+        small_a[0 : heads - 8, width + LANES :] = by_bucket[8:heads]
+        s_pair = send(small_a, small_pair, s1_send.at[0], s1_recv.at[0], {"seq": place.partner})
+
+        chunks[3].back_over_exp()
+        multiply(4)
+        multiply(5)
+        for copy in gins():
+            copy.start()
+        gin_in[:, at_hidden] = gin_out[me]
+        chunks[0].spread()
+        dekv_local().wait()
+        for copy in dekv_over_exp():
+            copy.wait_recv()
+        dekv_gather.start()
+        chunks[2].over_seq.relay()
+        chunks[3].spread()
+        s_pair.wait_recv()
+        small_b[...] = small_a[...] + small_pair[...]
+        s_chip = [
+            send(small_b, small_chip.at[d], s2_send.at[d], s2_recv.at[d], {"seq": device})
+            for d, device in enumerate((place.x, place.y, place.far))
+        ]
+        chunks[4].back_over_exp()
+        chunks[5].back_over_exp()
+        chunks[1].over_seq.relay()
+        chunks[2].over_seq.relay_far()
+        genc_ref[...] = nt(dekv[...], w_ckv[...])
+        chunks[4].spread()
+        chunks[5].spread()
+        chunks[0].over_seq.relay()
+        dekv_gather.relay()
+        chunks[1].over_seq.relay_far()
+        total = small_b[...]
+        for d, copy in enumerate(s_chip):
+            copy.wait_recv()
+            total = total + small_chip[d]
+        small_c[...] = total
+        s_exp = [
+            send(small_c, small_exp.at[d], s3_send.at[d], s3_recv.at[d], {"exp": peer}) for d, peer in enumerate(peers)
+        ]
+        chunks[3].over_seq.relay()
+        chunks[0].over_seq.relay_far()
+        dekv_gather.relay_far()
+        for copy in gins():
+            copy.wait_recv()
+        gin_ref[...] = gin_in[...]
+        chunks[4].over_seq.relay()
+        chunks[5].over_seq.relay()
+        total = small_c[...]
+        for d, copy in enumerate(s_exp):
+            copy.wait_recv()
+            total = total + small_exp[d]
+        small_out_ref[...] = total
+        for i in (3, 4, 5):
+            chunks[i].over_seq.relay_far()
+        for chunk in chunks:
+            chunk.over_seq.finish()
+        dekv_gather.finish()
+
+        for copy in started + enc_over_exp() + dekv_over_exp() + gins():
+            copy.wait_send()
+        for i in range(6):
+            for copy in right_copies(i):
+                copy.wait_send()
+        for each in (gather, o_gather, n2_gather, oc_gather, x_gather, g_gather, dekv_gather, enc_scatter):
+            each.drain()
+        for chunk in chunks:
+            chunk.drain()
+
+        @pl.loop(0, pairs)
+        def _(p):
+            terms(p).drain()
+
+
+    pl.run_scoped(
+        backward, bf(2, 4, enc_part, 2 * width), bf(pairs, 2, 4, rows, 2 * LANES), bf(6, part, width), bf(6, width, rows),
+        bf(span + rows, 2 * rows), bf(seq_count, part, own_hidden), bf(width, own_hidden), bf(own_hidden, width),
+    )
+
+
+def layer_call(seq_count, capacity, x, encoder, lengths, buckets, routes, gains, qkv, so, cq, ckv, co, rel, router, g, w_in,
+               w_out):
+    rows, width = x.shape
+    span = seq_count * rows
+    pairs = width // LANES
+    heads = 2 * pairs
+    enc_rows = encoder.shape[0]
+    experts = router.shape[0]
+    slot_rows = experts * capacity
+    part = width // seq_count
+    enc_part = enc_rows // seq_count
+    own_enc = enc_part // experts
+    hidden = w_in.shape[1]
+    z = experts - 1
+    quarter = (part // 2, width // (experts // 2))
+    small = (8, width + 2 * LANES)
+    packed = (experts, capacity * pairs, LANES)
+    shape = jax.ShapeDtypeStruct
+    dma = lambda *n: pltpu.SemaphoreType.DMA(n)
+    bf = lambda *n: pltpu.VMEM(n, BF16)
+    f32 = lambda *n: pltpu.VMEM(n, F32)
+    wide = bf(rows, width)
+    return pl.pallas_call(
+        functools.partial(layer_kernel, seq_count, capacity),
+        out_shape=(
+            shape((rows, width), BF16), shape((rows, width), F32), shape((6, seq_count, part, width), BF16),
+            shape((seq_count, experts, own_enc, 2 * width), BF16), shape(small, F32), shape((part, hidden), BF16),
+            shape((hidden // seq_count, width), F32), shape((own_enc, width), F32),
+        ),
+        in_specs=[VMEM, ANY, SMEM, VMEM, VMEM, VMEM, ANY, ANY, ANY, ANY, ANY, VMEM, VMEM, VMEM, ANY, ANY],
+        out_specs=(VMEM, VMEM, ANY, ANY, VMEM, VMEM, VMEM, VMEM),
+        scratch_shapes=[
+            bf(4, seq_count, rows, width), bf(span, 2 * width), bf(pairs, span, 2 * rows), bf(pairs, enc_rows, 2 * rows),
+            bf(enc_rows, 2 * width), bf(*qkv.shape), bf(*so.shape), bf(*cq.shape), bf(*ckv.shape), bf(*co.shape),
+            f32(heads, 2 * LANES), bf(seq_count, slot_rows + GATE_ROWS, width), bf(seq_count, slot_rows, width),
+            bf(experts, capacity * pairs + GATE_ROWS, LANES), bf(*packed), bf(*packed), bf(*packed),
+            wide, wide, wide, f32(rows, width), f32(rows, width), f32(rows, experts), f32(rows, experts), bf(rows, slot_rows),
+            f32(rows, width), wide, wide, bf(rows, 3 * width), f32(heads, 2 * rows), f32(pairs, 2 * rows),
+            bf(4, enc_part, 2 * width), bf(2, enc_part // 2, 2 * width), bf(2, enc_part, 2 * width),
+            bf(experts, own_enc, 2 * width), bf(z, own_enc, 2 * width), bf(own_enc, 2 * width),
+            bf(pairs, 4, rows, 2 * LANES), bf(pairs, 2, rows // 2, 2 * LANES), bf(pairs, 2, rows, 2 * LANES),
+            bf(6, z, *quarter), bf(6, *quarter), bf(6, part, span), bf(part, hidden),
+            f32(*small), f32(*small), f32(*small), f32(*small), f32(3, *small), f32(z, *small),
+            dma(10), dma(7)] + [dma(8)] * 12 + [dma(z)] * 8 + [
+            dma(1), dma(1), dma(2), dma(2), dma(2), dma(2), dma(z), dma(z), dma(z), dma(z), dma(8), dma(8),
+            dma(pairs), dma(pairs), dma(pairs, 2), dma(pairs, 2), dma(pairs, 2), dma(pairs, 2),
+            dma(6, z), dma(6, z), dma(6, z), dma(6, z), dma(6, 8), dma(6, 8),
+            dma(6, seq_count - 1), dma(6, seq_count - 1), dma(seq_count - 1), dma(seq_count - 1),
+            dma(1), dma(1), dma(3), dma(3), dma(z), dma(z),
+        ],
+        compiler_params=pltpu.CompilerParams(collective_id=0, has_side_effects=True, vmem_limit_bytes=63 << 20),
+        name="layer",
+    )(x, encoder, lengths, buckets, routes, gains, qkv, so, cq, ckv, co, rel, router, g, w_in, w_out)
+
+
+def finish_kernel(
+    experts, weights_hbm, dekv_hbm, enc_hbm, small_ref, layer_hbm, dx_hbm, genc_hbm, gin_ref, gout_hbm,
+    layer_out, dx_out, genc_out, gains_out, qkv_hbm, so_hbm, cq_hbm, ckv_hbm, co_hbm, rel_out, router_out, gin_out, gout_out,
+    weights, dekv, enc, squares, qkv, ckv, layer, dx, genc, gin, gout, load_sem, sem,
+):
+    seq_count, part, width = weights.shape[1:]
+    loads = [pltpu.make_async_copy(weights_hbm.at[i], weights.at[i], load_sem.at[i]) for i in range(6)] + [
+        pltpu.make_async_copy(dekv_hbm, dekv, load_sem.at[6]), pltpu.make_async_copy(enc_hbm, enc, load_sem.at[7])
+    ]
+    through = ((gout_hbm, gout, gout_out), (dx_hbm, dx, dx_out), (layer_hbm, layer, layer_out), (genc_hbm, genc, genc_out))
+    loads += [pltpu.make_async_copy(src, held, load_sem.at[8 + i]) for i, (src, held, _) in enumerate(through)]
+    for load in loads:
+        load.start()
+    copies = []
+
+    def store(src, dst):
+        copy = pltpu.make_async_copy(src, dst, sem.at[len(copies)])
+        copy.start()
+        copies.append(copy)
+
+    gains_out[...] = small_ref[0:3, :width]
+    router_out[...] = small_ref[4 : 4 + experts, :width]
+    heads, buckets = rel_out.shape
+    rel_out[0:8, :] = small_ref[0:8, width : width + buckets]
+    rel_out[8:heads, :] = small_ref[0 : heads - 8, width + LANES : width + LANES + buckets]
+    gin[...] = gin_ref[...].astype(F32)
+    store(gin, gin_out)
+
+    def turn(i, target, at):
+        loads[i].wait()
+        for block in range(width // LANES):
+            rows = slice(block * LANES, (block + 1) * LANES)
+            target[:, at + block * LANES : at + (block + 1) * LANES] = (
+                weights[i].reshape(seq_count * part, width)[rows, :].astype(F32).T
+            )
+
+    for i, out in enumerate((so_hbm, cq_hbm, co_hbm)):
+        turn(i, squares.at[i], 0)
+        store(squares.at[i], out)
+    for i, (_, held, out) in enumerate(through):
+        loads[8 + i].wait()
+        store(held, out)
+    for i in range(3):
+        at = slice(i * width, (i + 1) * width)
+        turn(3 + i, qkv, i * width)
+        store(qkv.at[:, at], qkv_hbm.at[:, at])
+    loads[6].wait()
+    loads[7].wait()
+    for n in range(2):
+        at = slice(n * width, (n + 1) * width)
+        ckv[:, at] = tn(enc[...], dekv[...].reshape(enc.shape[0], 2 * width)[:, at])
+        store(ckv.at[:, at], ckv_hbm.at[:, at])
+    for copy in copies:
+        copy.wait()
+
+
+def finish_call(heads, buckets, experts, weights, dekv, enc, small, layer, dx, genc, gin, gout):
+    seq_count, part, width = weights.shape[1:]
+    shape = jax.ShapeDtypeStruct
+    f32 = lambda *n: shape(n, F32)
+    return pl.pallas_call(
+        functools.partial(finish_kernel, experts),
+        out_shape=(
+            shape(layer.shape, BF16), f32(*dx.shape), f32(*genc.shape), f32(3, width), f32(width, 3 * width), f32(width, width),
+            f32(width, width), f32(width, 2 * width), f32(width, width), f32(heads, buckets), f32(experts, width),
+            f32(*gin.shape), f32(*gout.shape),
+        ),
+        in_specs=[ANY, ANY, ANY, VMEM, ANY, ANY, ANY, VMEM, ANY],
+        out_specs=(ANY, ANY, ANY, VMEM, ANY, ANY, ANY, ANY, ANY, VMEM, VMEM, ANY, ANY),
+        scratch_shapes=[
+            pltpu.VMEM(weights.shape, BF16), pltpu.VMEM(dekv.shape, BF16), pltpu.VMEM(enc.shape, BF16),
+            pltpu.VMEM((3, width, width), F32), pltpu.VMEM((width, 3 * width), F32), pltpu.VMEM((width, 2 * width), F32),
+            pltpu.VMEM(layer.shape, BF16), pltpu.VMEM(dx.shape, F32), pltpu.VMEM(genc.shape, F32), pltpu.VMEM(gin.shape, F32),
+            pltpu.VMEM(gout.shape, F32), pltpu.SemaphoreType.DMA((13,)), pltpu.SemaphoreType.DMA((13,)),
+        ],
+        compiler_params=pltpu.CompilerParams(vmem_limit_bytes=60 << 20),
+        name="finish",
+    )(weights, dekv, enc, small, layer, dx, genc, gin, gout)
+
+
+def fused(inputs, encoder, lengths, buckets, routes, norm_gains, self_qkv, self_out, cross_q, cross_kv, cross_out,
+          rel_bias, router, expert_in, expert_out, cotangent):
+    seq_count = lax.axis_size("seq")
+    rows = inputs.shape[1]
+    experts = router.shape[1]
+    capacity = 5 * rows // (4 * experts)
+    (layer_out, grad_input, weights, dekv, small, gin, gout, grad_encoder) = layer_call(
+        seq_count, capacity, inputs[0], encoder, lengths, buckets[None, :], routes.reshape(1, rows), norm_gains, self_qkv,
+        self_out, cross_q, cross_kv, cross_out, rel_bias.T, router.T, cotangent[0], expert_in[0], expert_out[0])
+    (layer_out, grad_input, grad_encoder, gains, g_qkv, g_so, g_cq, g_ckv, g_co, g_rel, g_router, gin, gout) = finish_call(
+        rel_bias.shape[1], rel_bias.shape[0], experts, weights, dekv, encoder, small, layer_out, grad_input, grad_encoder, gin,
+        gout)
+    return (layer_out[None], grad_input[None], grad_encoder, gains, g_qkv, g_so, g_cq, g_ckv, g_co, g_rel.T, g_router.T,
+            gin[None], gout[None])
+
+
+def on_device(*operands):
+    if lax.axis_size("seq") == 8 and lax.axis_size("exp") == 4 and operands[0].shape[1] == 128:
+        return fused(*operands)
+    return streamed(*operands)
+
+
 def solution(mesh):
     in_specs = (
         P("exp", "seq", None),

time: 1200 us -> 161 us (0.13); the launches traced: 1180 us -> 160 us
  waiting for transfers between devices: 476 us -> 0 us
  local copies, waits for them, and re-layouts: 388 us -> 0 us
  Pallas kernels: 0 us -> 159 us
  matrix products: 122 us -> 0 us
  blocking collectives: 83.8 us -> 0 us
  other arithmetic: 80.4 us -> 0 us
  between operations: 14.7 us -> 0.86 us
    psum x1 -> x0, waiting for transfers between devices: 315 us -> none  [on_device(): lax.psum((jnp.stack([gain_one, gain_two, gain_three]), qkv_w_grad, self_o...]
    reshape x11 -> x0, local copies, waits for them, and re-layouts: 165 us -> none  [the longest x2 70.2 us: table_terms(): flat.reshape(head_count, query_rows, band_len)]
    pallas_call x0 -> x2, Pallas kernels: none -> 159 us  [the longest x1 146 us: layer_call(): pl.pallas_call(functools.partial(layer_kernel, seq_count, capacity), out_...]
    reduce_scatter x3 -> x0, waiting for transfers between devices: 118 us -> none  [the longest x1 81 us: on_device(): lax.psum_scatter(grad_in_w, 'seq', scatter_dimension=1, tiled=True)]
    dot_general x55 -> x0, matrix products: 117 us -> none  [the longest x4 13.7 us: self_scores(): jnp.einsum('qhd,khd->hqk', split_heads(queries), split_heads(keys_part),...]
    while x48 -> x0, local copies, waits for them, and re-layouts: 75.3 us -> none
    psum x1 -> x0, blocking collectives: 40.4 us -> none  [on_device(): lax.psum((jnp.stack([gain_one, gain_two, gain_three]), qkv_w_grad, self_o...]
    unnamed x136 -> x0, local copies, waits for them, and re-layouts: 38.3 us -> none
  transfers between devices with their start and end apart: 11 -> 0, of which waited for: 8 -> 0; matrix products, arithmetic and copies ran while one was open for 37% -> 0% of each run, Pallas kernels for 0% -> 0%
where the time goes in v4:
time: 161 us; the launch traced here: 160 us
  Pallas kernels  159 us (99%)
    pallas_call x1, Pallas kernels, layer_call(): pl.pallas_call(functools.partial(layer_kernel, seq_count, capacity), out_...  146 us
    pallas_call x1, Pallas kernels, finish_call(): pl.pallas_call(functools.partial(finish_kernel, experts), out_shape=(shap...  13.8 us

profile of v4, /device:TPU:0, one launch (start us, length us, event | category | flops | bytes accessed | tf_op | source)
XLA Modules:
  0.0 160.3 jit_solution(11640995741108257790)
XLA Ops:
  0.7 145.6 %layer.1 = (bf16[128,768]{1,0:T(8,128)(2,1)}, f32[128,768]{1,0:T(8,128)}, bf16[6,8,96,768]{3,2,1,0:T(8,128)(2,1)}, bf16[8,4,16,1536]{3,2,1,0:T(8,128)(2,1)}, f32...) custom-call(bf16[128,768]{1,0:T(8,128)(2,1)} %bitcast.16, ...), custom_call_target="tpu_custom_call" | custom-call | tf_op jit(solution)/shard_map/layer/pallas_call | solution.py:1364
  146.2 13.8 %finish.1 = (bf16[128,768]{1,0:T(8,128)(2,1)}, f32[128,768]{1,0:T(8,128)}, f32[16,768]{1,0:T(8,128)}, f32[3,768]{1,0:T(4,128)}, f32[768,2304]{1,0:T(8,128)}, /*i...) custom-call(bf16[6,8,96,768]{3,2,1,0:T(8,128)(2,1)} %get-tuple-eleme, ...), custom_call_target="tpu_custom_call" | custom-call | tf_op jit(solution)/shard_map/finish/pallas_call | solution.py:1457

commit v5 on v4

--- a/solution.py
+++ b/solution.py
@@ -548,114 +548,97 @@
     )
 
 
+def wait_bytes(sized, sem):
+    pltpu.make_async_copy(sized, sized, sem).wait()
+
+
 class Gather:
-    def __init__(self, place, every, rows, sends, recvs):
-        self.place, self.every, self.sends, self.recvs = place, every, sends, recvs
+    def __init__(self, place, every, rows, send_sem, recv_sems, staged=False):
+        self.place, self.every, self.send_sem, self.recv_sems, self.staged = place, every, send_sem, recv_sems, staged
         half = rows // 2 if rows < 32 else -(-rows // 32) * 16
         self.halves = pl.ds(0, half), pl.ds(half, rows - half)
 
     def copy(self, slot):
         place, every = self.place, self.every
-        block, device = (
-            lambda: (every.at[place.me], place.partner),
-            lambda: (every.at[place.me], place.x),
-            lambda: (every.at[place.me], place.y),
-            lambda: (every.at[place.x, self.halves[0]], place.y),
-            lambda: (every.at[place.y, self.halves[1]], place.x),
-            lambda: (every.at[place.x], place.partner),
-            lambda: (every.at[place.y], place.partner),
-            lambda: (every.at[place.far], place.partner),
+        block, device, sem = (
+            lambda: (every.at[place.me], place.partner, 3),
+            lambda: (every.at[place.me], place.x, 0),
+            lambda: (every.at[place.me], place.y, 1),
+            lambda: (every.at[place.x, self.halves[0]], place.y, 2),
+            lambda: (every.at[place.y, self.halves[1]], place.x, 2),
+            lambda: (every.at[place.x], place.partner, 4 if self.staged else 3),
+            lambda: (every.at[place.y], place.partner, 4 if self.staged else 3),
+            lambda: (every.at[place.far], place.partner, 5 if self.staged else 3),
         )[slot]()
-        return remote(block, block, self.sends.at[slot], self.recvs.at[slot], {"seq": device})
+        return remote(block, block, self.send_sem, self.recv_sems.at[sem], {"seq": device})
 
     def send(self, *slots):
         for slot in slots:
             self.copy(slot).start()
 
-    def wait(self, *slots):
-        for slot in slots:
-            self.copy(slot).wait_recv()
+    def arrived(self, blocks, sem):
+        wait_bytes(self.every.at[pl.ds(0, blocks)], self.recv_sems.at[sem])
 
     def start(self):
         self.send(1, 2, 0)
 
     def relay(self):
-        self.wait(1)
+        self.arrived(1, 0)
         self.send(3)
-        self.wait(2)
+        self.arrived(1, 1)
         self.send(4, 5, 6)
 
     def relay_far(self):
-        self.wait(3, 4)
+        self.arrived(1, 2)
         self.send(7)
 
     def finish(self):
-        self.wait(0, 5, 6, 7)
+        self.arrived(4, 3)
 
     def drain(self):
-        for slot in range(8):
-            self.copy(slot).wait_send()
+        wait_bytes(self.every.at[pl.ds(0, 7)], self.send_sem)
 
 
 class Scatter:
     def __init__(self, place, out, pair, turn, side, half, sems):
-        self.place, self.out, self.pair, self.turn, self.side, self.half = place, out, pair, turn, side, half
-        self.pair_sems, self.turn_sems, self.side_sems = sems
+        self.place, self.out, self.pair, self.turn, self.side, self.half, self.sems = place, out, pair, turn, side, half, sems
 
     def pair_copy(self):
-        send, recv = self.pair_sems
-        return remote(self.out.at[1 - self.place.core], self.pair, send, recv, {"seq": self.place.partner})
-
-    def turn_copies(self):
-        place = self.place
-        send, recv = self.turn_sems
-        far = self.out.at[place.core, place.far_chip]
-        return (
-            remote(far.at[pl.ds(0, self.half)], self.turn.at[0], send.at[0], recv.at[0], {"seq": place.x}),
-            remote(far.at[pl.ds(self.half, self.half)], self.turn.at[1], send.at[1], recv.at[1], {"seq": place.y}),
-        )
-
-    def side_copies(self):
-        place = self.place
-        send, recv = self.side_sems
-        return (
-            remote(self.out.at[place.core, place.x_chip], self.side.at[0], send.at[0], recv.at[0], {"seq": place.x}),
-            remote(self.out.at[place.core, place.y_chip], self.side.at[1], send.at[1], recv.at[1], {"seq": place.y}),
-        )
+        return remote(self.out.at[1 - self.place.core], self.pair, self.sems.at[0], self.sems.at[2], {"seq": self.place.partner})
+
+    def send_round(self, src, dst, recv, device):
+        remote(src, dst, self.sems.at[1], self.sems.at[recv], {"seq": device}).start()
 
     def start(self):
         self.pair_copy().start()
 
     def turn_on(self):
-        core = self.place.core
+        place = self.place
         self.pair_copy().wait_recv()
-        self.out[core] = (self.out[core].astype(F32) + self.pair[...].astype(F32)).astype(BF16)
-        for copy in self.turn_copies():
-            copy.start()
+        self.out[place.core] = (self.out[place.core].astype(F32) + self.pair[...].astype(F32)).astype(BF16)
+        far = self.out.at[place.core, place.far_chip]
+        self.send_round(far.at[pl.ds(0, self.half)], self.turn.at[0], 3, place.x)
+        self.send_round(far.at[pl.ds(self.half, self.half)], self.turn.at[1], 3, place.y)
 
     def side_on(self):
         place = self.place
         first, second = pl.ds(0, self.half), pl.ds(self.half, self.half)
-        from_x, from_y = self.turn_copies()
-        from_x.wait_recv()
+        wait_bytes(self.turn, self.sems.at[3])
         at = (place.core, place.y_chip, first)
         self.out[at] = (self.out[at].astype(F32) + self.turn[0].astype(F32)).astype(BF16)
-        from_y.wait_recv()
         at = (place.core, place.x_chip, second)
         self.out[at] = (self.out[at].astype(F32) + self.turn[1].astype(F32)).astype(BF16)
-        for copy in self.side_copies():
-            copy.start()
+        self.send_round(self.out.at[place.core, place.x_chip], self.side.at[0], 4, place.x)
+        self.send_round(self.out.at[place.core, place.y_chip], self.side.at[1], 4, place.y)
 
     def total(self):
-        for copy in self.side_copies():
-            copy.wait_recv()
+        wait_bytes(self.side, self.sems.at[4])
         own = self.out[self.place.core, self.place.chip].astype(F32)
         return own + self.side[0].astype(F32) + self.side[1].astype(F32)
 
     def drain(self):
         self.pair_copy().wait_send()
-        for copy in self.turn_copies() + self.side_copies():
-            copy.wait_send()
+        wait_bytes(self.out.at[0, pl.ds(0, 3)], self.sems.at[1])
 
 
 def expert_peers(exp_index, experts):
@@ -700,51 +683,40 @@
 
 
 class Chunk:
-    def __init__(self, place, quarters, mine, peers, src, slots, own, every, sems, gather_sems, local_sem):
-        self.place, self.quarters, self.mine, self.peers = place, quarters, mine, peers
-        self.src, self.slots, self.own, self.every = src, slots, own, every
-        self.scatter_sems, self.gather_sems, self.local_sem = sems[:2], sems[2:], local_sem
+    def __init__(self, place, quarters, peers, src, slots, own, every, sems, gather_sems, local_sem):
+        self.place, self.quarters, self.peers = place, quarters, peers
+        self.src, self.slots, self.own, self.every, self.sems, self.local_sem = src, slots, own, every, sems, local_sem
         self.over_seq = Gather(place, every, src.shape[0], *gather_sems)
-
-    def scatter_copies(self):
-        send, recv = self.scatter_sems
-        return [
-            remote(self.src.at[self.quarters[1 + d]], self.slots.at[d], send.at[d], recv.at[d], {"exp": peer})
-            for d, peer in enumerate(self.peers)
-        ]
-
-    def gather_copies(self):
-        send, recv = self.gather_sems
-        target = self.every.at[(self.place.me,) + self.quarters[0]]
-        return [remote(self.own, target, send.at[d], recv.at[d], {"exp": peer}) for d, peer in enumerate(self.peers)]
 
     def local_copy(self):
         return pltpu.make_async_copy(self.own, self.every.at[(self.place.me,) + self.quarters[0]], self.local_sem)
 
     def over_exp(self, value):
         self.src[...] = value.astype(BF16)
-        for copy in self.scatter_copies():
-            copy.start()
+        for d, peer in enumerate(self.peers):
+            remote(
+                self.src.at[self.quarters[1 + d]], self.slots.at[d], self.sems.at[0], self.sems.at[1], {"exp": peer}
+            ).start()
 
     def back_over_exp(self):
         total = self.src[self.quarters[0]].astype(F32)
-        for d, copy in enumerate(self.scatter_copies()):
-            copy.wait_recv()
+        wait_bytes(self.slots, self.sems.at[1])
+        for d in range(len(self.peers)):
             total = total + self.slots[d].astype(F32)
         self.own[...] = total.astype(BF16)
         self.local_copy().start()
-        for copy in self.gather_copies():
-            copy.start()
+        target = self.every.at[(self.place.me,) + self.quarters[0]]
+        for peer in self.peers:
+            remote(self.own, target, self.sems.at[2], self.sems.at[3], {"exp": peer}).start()
 
     def spread(self):
         self.local_copy().wait()
-        for copy in self.gather_copies():
-            copy.wait_recv()
+        wait_bytes(self.slots, self.sems.at[3])
         self.over_seq.start()
 
     def drain(self):
-        for copy in self.scatter_copies() + self.gather_copies():
-            copy.wait_send()
+        wait_bytes(self.slots, self.sems.at[0])
+        wait_bytes(self.slots, self.sems.at[2])
         self.over_seq.drain()
 
 
@@ -752,17 +724,14 @@
     seq_count, capacity,
     x_ref, encoder_hbm, lengths_ref, buckets_ref, routes_ref, gains_ref, qkv_hbm, so_hbm, cq_hbm, ckv_hbm, co_hbm, rel_ref,
     router_ref, g_ref, in_hbm, out_hbm,
-    out_ref, dx_ref, weights_hbm, dekv_hbm, small_out_ref, gin_ref, gout_ref, genc_ref,
+    out_hbm_ref, dx_hbm, weights_hbm, dekv_hbm, small_hbm, gin_hbm, gout_hbm, genc_hbm,
     left, kv_all, prob, cross_prob, ekv, w_qkv, w_so, w_cq, w_ckv, w_co, table_ref, x_all, g_all, x_in, g_in, made_back, dx_back,
     q_ref, qc_ref, x3_ref, r1_ref, r2_ref, gates_ref, chosen_ref, slots_ref,
     dr_ref, doc_ref, dqc_ref, dqkv_ref, diag_ref, total_ref,
     e_pair, e_turn, e_side, e_mine, e_exp, dekv, t_pair, t_turn, t_side,
-    c_slots, c_own, right, gin_in, small_a, small_b, small_c, small_pair, small_chip, small_exp,
-    load_sem, local_sem, n_send, n_recv, o_send, o_recv, m_send, m_recv, c_send, c_recv, x_send, x_recv, d_send, d_recv,
-    zx_send, zx_recv, zd_send, zd_recv, zm_send, zm_recv, zg_send, zg_recv,
-    ep_send, ep_recv, et_send, et_recv, es_send, es_recv, ez_send, ez_recv, eg_send, eg_recv, ea_send, ea_recv,
-    tp_send, tp_recv, tt_send, tt_recv, ts_send, ts_recv, cs_send, cs_recv, cg_send, cg_recv, ca_send, ca_recv,
-    r_send, r_recv, g_send, g_recv, s1_send, s1_recv, s2_send, s2_recv, s3_send, s3_recv,
+    out_ref, dx_ref, gout_ref, genc_ref, small_out_ref, c_slots, c_own, right, gin_in, small_a, small_b, small_c, small_pair, small_chip, small_exp,
+    load_sem, local_sem, store_sem, n_recv, gather_send, gather_recv, trip_sem, enc_sem, enc_exp_sem, term_sem, chunk_sem,
+    chunk_send, chunk_recv, right_sem, unit_send, unit_recv, small_sem,
 ):
     rows, width = x_ref.shape
     span = seq_count * rows
@@ -782,30 +751,35 @@
     quarters = [
         (block_of(lax.div(e, experts // 2), half_rows), block_of(lax.rem(e, experts // 2), half_lanes)) for e in [mine] + peers
     ]
-    at_hidden = block_of(me, own_hidden)
     own_lanes = block_of(me, rows)
     near = pl.ds(pl.multiple_of(me * rows, rows), 2 * rows)
-    gather, o_gather, n2_gather, oc_gather = (
-        Gather(place, left.at[i], rows, *sems)
-        for i, sems in ((3, (n_send, n_recv)), (0, (o_send, o_recv)), (1, (m_send, m_recv)), (2, (c_send, c_recv)))
-    )
-    x_gather = Gather(place, x_all, x_all.shape[1], x_send, x_recv)
-    g_gather = Gather(place, g_all, slot_rows, d_send, d_recv)
+    gather = Gather(place, left.at[3], rows, gather_send.at[0], n_recv, staged=True)
+    o_gather, n2_gather, oc_gather = (
+        Gather(place, left.at[i], rows, gather_send.at[1 + i], gather_recv.at[i]) for i in range(3)
+    )
+    x_gather = Gather(place, x_all, x_all.shape[1], gather_send.at[4], gather_recv.at[3])
+    g_gather = Gather(place, g_all, slot_rows, gather_send.at[5], gather_recv.at[4])
 
     def load(i, src, dst):
         return pltpu.make_async_copy(src, dst, load_sem.at[i])
 
-    def exp_moves(src, dst, send, recv):
-        return [remote(src.at[peer], dst.at[mine], send.at[d], recv.at[d], {"exp": peer}) for d, peer in enumerate(peers)]
-
-    def over_exp(src, dst, send, recv):
-        for copy in exp_moves(src, dst, send, recv):
-            copy.start()
+    stores = []
+
+    def store(src, dst):
+        copy = pltpu.make_async_copy(src, dst, store_sem.at[len(stores)])
+        copy.start()
+        stores.append(copy)
+
+    def over_exp(src, dst, sems):
+        for peer in peers:
+            remote(src.at[peer], dst.at[mine], sems.at[0], sems.at[1], {"exp": peer}).start()
         dst[mine] = src[mine]
 
-    def arrive(src, dst, send, recv):
-        for copy in exp_moves(src, dst, send, recv):
-            copy.wait_recv()
+    def arrive(src, dst, sems):
+        wait_bytes(src.at[pl.ds(0, experts - 1)], sems.at[1])
+
+    def sent(src, dst, sems):
+        wait_bytes(src.at[pl.ds(0, experts - 1)], sems.at[0])
 
     load_qkv, load_ckv = load(0, qkv_hbm, w_qkv), load(1, ckv_hbm, w_ckv)
     load_so, load_cq, load_co = load(3, so_hbm, w_so), load(4, cq_hbm, w_cq), load(5, co_hbm, w_co)
@@ -842,12 +816,12 @@
         slots = (lax.broadcasted_iota(jnp.int32, (rows, slot_rows), 1) == target).astype(BF16)
         slots_ref[...] = slots
         gs_ref[...] = pack_slots(tn(slots, g_ref[...]), experts).astype(BF16)
-        g_trip = (gs_ref, g_in, zd_send, zd_recv)
+        g_trip = (gs_ref, g_in, trip_sem.at[0])
         over_exp(*g_trip)
 
         load_qkv.wait()
         q_ref[...] = nn(left[3, me], w_qkv[:, :width]).astype(BF16) * jnp.asarray(0.125, BF16)
-        gather.wait(0)
+        gather.arrived(1, 3)
         project(place.chip)
         load_so.start()
         load_cq.start()
@@ -869,14 +843,14 @@
         key_pos = lax.broadcasted_iota(jnp.int32, (span, rows), 0)
         seen = jnp.where((key_pos >= start) & (key_pos <= query_pos), 0.0, masked_out)
         mask[...] = jnp.concatenate([seen, seen], axis=1)
-        gather.wait(5, 6)
+        gather.arrived(2, 4)
         project(place.x_chip)
         project(place.y_chip)
         gather.relay_far()
         arrive(*g_trip)
         g_all[me] = unpack_slots(g_in[...], capacity).astype(BF16)
         g_gather.start()
-        gather.wait(7)
+        gather.arrived(1, 5)
         project(place.far_chip)
 
         @pl.loop(0, pairs)
@@ -896,8 +870,7 @@
             both = tn(kv_all[:, pair_lanes(pairs + p)], weights)
             left[0, me, :, lanes] = head_unstack(both, rows).astype(BF16)
 
-        for copy in exp_moves(*g_trip):
-            copy.wait_send()
+        sent(*g_trip)
 
     def rest_forward(xs_ref, made_out, dx_out, slope, w_in, w_out):
         load_in, load_out = load(6, in_hbm, w_in), load(7, out_hbm, w_out)
@@ -942,7 +915,7 @@
         by_slot = tn(in_three(gate_used), slots).astype(BF16)
         for e in range(experts):
             xs_ref[e, packed_rows:, :] = nn(by_slot, own_slots(e)).astype(BF16)
-        x_trip = (xs_ref, x_in, zx_send, zx_recv)
+        x_trip = (xs_ref, x_in, trip_sem.at[1])
         over_exp(*x_trip)
 
         o_gather.relay()
@@ -957,7 +930,6 @@
             [gate_parts, jnp.zeros((GATE_ROWS, width - slot_rows), F32)], axis=1
         ).astype(BF16)
         x_gather.start()
-        n2_gather.relay()
         xs = x_all[me, :slot_rows, :]
         made = jnp.zeros(xs.shape, F32)
         for n in range(hidden // width):
@@ -966,8 +938,9 @@
             slope[:, at] = derivative
             made = made + nn(value.astype(BF16), w_out[at, :])
         made_out[...] = pack_slots(made, experts).astype(BF16)
-        made_trip = (made_out, made_back, zm_send, zm_recv)
+        made_trip = (made_out, made_back, trip_sem.at[2])
         over_exp(*made_trip)
+        n2_gather.relay()
         dm = (g_all[me].astype(F32) * slot_gates(gate_parts)).astype(BF16)
         dx = jnp.zeros(dm.shape, F32)
         for n in range(hidden // width):
@@ -975,17 +948,14 @@
             dh = (nt(dm, w_out[at, :]) * slope[:, at]).astype(BF16)
             dx = dx + nt(dh, w_in[:, at])
         dx_out[...] = pack_slots(dx, experts).astype(BF16)
-        dx_trip = (dx_out, dx_back, zg_send, zg_recv)
+        dx_trip = (dx_out, dx_back, trip_sem.at[3])
         over_exp(*dx_trip)
         g_gather.relay_far()
-        oc_gather.relay()
         o_gather.relay_far()
-        n2_gather.relay_far()
         arrive(*made_trip)
         arrive(*dx_trip)
         for trip in (x_trip, made_trip, dx_trip):
-            for copy in exp_moves(*trip):
-                copy.wait_send()
+            sent(*trip)
 
     bf = lambda *n: pltpu.VMEM(n, BF16)
     f32 = lambda *n: pltpu.VMEM(n, F32)
@@ -996,67 +966,77 @@
     )
 
     enc_part = enc_rows // seq_count
-    dekv_gather = Gather(place, dekv_hbm, experts, ea_send, ea_recv)
-    started = []
-
-    def send(src, dst, send_sem, recv_sem, device):
-        copy = remote(src, dst, send_sem, recv_sem, device)
-        copy.start()
-        started.append(copy)
-        return copy
-
-    def backward(e_out, t_out, c_src, turned_ref, ds_ref, gin_out, w_ein, w_eout):
-        load_ein, load_eout = load(8, in_hbm.at[:, at_hidden], w_ein), load(9, out_hbm.at[at_hidden, :], w_eout)
-        load_ein.start()
-        load_eout.start()
-        enc_scatter = Scatter(
-            place, e_out, e_pair, e_turn, e_side, e_turn.shape[1],
-            ((ep_send.at[0], ep_recv.at[0]), (et_send, et_recv), (es_send, es_recv)),
-        )
+    dekv_gather = Gather(place, dekv_hbm, experts, gather_send.at[6], gather_recv.at[5])
+    def backward(e_out, t_out, c_src, turned_ref, ds_ref, gin_out, gin_window, w_ein, w_eout):
+        def unit_block(j):
+            return block_of(lax.rem(place.chip + j, 4) * 2 + place.core, own_hidden)
+
+        def expert_loads(j):
+            return (
+                load(8 + 2 * (j % 2), in_hbm.at[:, unit_block(j)], w_ein.at[j % 2]),
+                load(9 + 2 * (j % 2), out_hbm.at[unit_block(j), :], w_eout.at[j % 2]),
+            )
+
+        def gin_copy(j):
+            return remote(
+                gin_out.at[j], gin_in.at[:, unit_block(j)], unit_send.at[0], unit_recv.at[0], {"seq": place.partner}
+            )
+
+        def expert_units(j):
+            for copy in expert_loads(j):
+                copy.wait()
+            xs = x_all[:, :slot_rows, :].reshape(-1, width)
+            dm = g_all[...].reshape(-1, width)
+            value, slope = gelu_parts(nn(xs, w_ein[j % 2]))
+            if j == 0:
+                gout_ref[...] = tn(value.astype(BF16), dm)
+                store(gout_ref, gout_hbm)
+            dh = (nt(dm, w_eout[j % 2]) * slope).astype(BF16)
+            if j < 2:
+                for copy in expert_loads(j + 2):
+                    copy.start()
+            lanes = pl.ds(pl.multiple_of((place.chip + lax.div(place.chip, 2)) * LANES, LANES), 2 * LANES)
+            gin_window[...] = tn(x_all[:, :slot_rows, lanes].reshape(-1, 2 * LANES), dh)
+            first = lax.rem(place.chip, 2) * (LANES // 2)
+            rows_of = lambda core: pl.ds(pl.multiple_of(first + core * part, 32), part)
+            gin_in[:, unit_block(j)] = gin_window[rows_of(place.core), :].astype(BF16)
+            gin_out[j] = gin_window[rows_of(1 - place.core), :].astype(BF16)
+            gin_copy(j).start()
+
+        for copy in expert_loads(0) + expert_loads(1):
+            copy.start()
+        enc_scatter = Scatter(place, e_out, e_pair, e_turn, e_side, e_turn.shape[1], enc_sem)
         chunks = [
             Chunk(
-                place, quarters, mine, peers, c_src.at[i], c_slots.at[i], c_own.at[i], weights_hbm.at[i],
-                (cs_send.at[i], cs_recv.at[i], cg_send.at[i], cg_recv.at[i]), (ca_send.at[i], ca_recv.at[i]), local_sem.at[i],
+                place, quarters, peers, c_src.at[i], c_slots.at[i], c_own.at[i], weights_hbm.at[i], chunk_sem.at[i],
+                (chunk_send.at[i], chunk_recv.at[i]), local_sem.at[i],
             )
             for i in range(6)
         ]
 
         def enc_over_exp():
-            return [
-                remote(e_mine.at[peer], e_exp.at[d], ez_send.at[d], ez_recv.at[d], {"exp": peer}) for d, peer in enumerate(peers)
-            ]
+            for d, peer in enumerate(peers):
+                remote(e_mine.at[peer], e_exp.at[d], enc_exp_sem.at[0], enc_exp_sem.at[1], {"exp": peer}).start()
 
         def dekv_over_exp():
-            return [
-                remote(dekv, dekv_hbm.at[me, mine], eg_send.at[d], eg_recv.at[d], {"exp": peer}) for d, peer in enumerate(peers)
-            ]
+            for peer in peers:
+                remote(dekv, dekv_hbm.at[me, mine], enc_exp_sem.at[2], enc_exp_sem.at[3], {"exp": peer}).start()
 
         def dekv_local():
             return pltpu.make_async_copy(dekv, dekv_hbm.at[me, mine], local_sem.at[6])
 
-        def right_copies(i):
-            return [
-                remote(turned_ref.at[i, block_of(peer, part), :], right.at[i, :, own_lanes], r_send.at[i, d], r_recv.at[i, d],
-                       {"seq": peer})
-                for d, peer in enumerate(everyone)
-            ]
-
         def exchange(i, factor):
             turned_ref[i] = factor.T
-            for copy in right_copies(i):
-                copy.start()
+            for peer in everyone:
+                remote(
+                    turned_ref.at[i, block_of(peer, part), :], right.at[i, :, own_lanes], right_sem.at[i, 0], right_sem.at[i, 1],
+                    {"seq": peer},
+                ).start()
             right[i, :, own_lanes] = turned_ref[i, block_of(me, part), :]
 
         def multiply(i):
-            for copy in right_copies(i):
-                copy.wait_recv()
+            wait_bytes(turned_ref.at[i, pl.ds(0, (seq_count - 1) * part), :], right_sem.at[i, 1])
             chunks[i].over_exp(nn(right[i], left[min(i, 3)].reshape(span, width)))
-
-        def gins():
-            return [
-                remote(gin_out.at[peer], gin_in.at[:, at_hidden], g_send.at[d], g_recv.at[d], {"seq": peer})
-                for d, peer in enumerate(everyone)
-            ]
 
         slots = slots_ref[...]
         made = nn(slots, unpack_slots(made_back[...], capacity).astype(BF16))
@@ -1066,6 +1046,7 @@
         picked = jnp.sum(gates * chosen, axis=1, keepdims=True)
         g = g_ref[...].astype(F32)
         out_ref[...] = (r2_ref[...] + (picked * kept) * made).astype(BF16)
+        store(out_ref, out_hbm_ref)
         gate_grad = jnp.sum(g * made, axis=1, keepdims=True) * kept
         dl = gates * (chosen * gate_grad - picked * gate_grad)
         dl_high, dl_low = in_two(dl)
@@ -1082,8 +1063,9 @@
         do2 = dr_ref[...].astype(BF16)
         doc_ref[...] = nt(do2, w_co[...]).astype(BF16)
         exchange(2, do2)
+        oc_gather.relay()
+        n2_gather.relay_far()
         x_gather.relay()
-        oc_gather.relay_far()
 
         @pl.loop(0, pairs)
         def _(p):
@@ -1101,7 +1083,7 @@
             dqc_ref[:, lanes] = (head_unstack(tn(ekv[:, lanes], dc), rows) * 0.125).astype(BF16)
 
         enc_scatter.start()
-        x_gather.relay_far()
+        oc_gather.relay_far()
         dqc = dqc_ref[...]
         exchange(1, dqc)
         da, dw = rms_back(r1_ref[...], gains_ref[1:2, :], nt(dqc, w_cq[...]))
@@ -1111,6 +1093,7 @@
         do1 = dr_ref[...].astype(BF16)
         doc_ref[...] = nt(do1, w_so[...]).astype(BF16)
         exchange(0, do1)
+        x_gather.relay_far()
         oc_gather.finish()
         multiply(2)
         n2_gather.finish()
@@ -1124,10 +1107,7 @@
         ).astype(BF16)
 
         def terms(p):
-            return Scatter(
-                place, t_out.at[p], t_pair.at[p], t_turn.at[p], t_side.at[p], rows // 2,
-                ((tp_send.at[p], tp_recv.at[p]), (tt_send.at[p], tt_recv.at[p]), (ts_send.at[p], ts_recv.at[p])),
-            )
+            return Scatter(place, t_out.at[p], t_pair.at[p], t_turn.at[p], t_side.at[p], rows // 2, term_sem.at[p])
 
         def pair_back(p):
             lanes, value_lanes = pair_lanes(p), pair_lanes(pairs + p)
@@ -1189,58 +1169,41 @@
             @pl.when(t == 4)
             def _():
                 e_mine[...] = enc_scatter.total().astype(BF16).reshape(e_mine.shape)
-                for copy in enc_over_exp():
-                    copy.start()
+                enc_over_exp()
                 chunks[1].back_over_exp()
 
 
-        terms(5).turn_on()
-        terms(3).side_on()
-        own_terms(1)
+        last = pairs - 1
+        terms(last).turn_on()
+        terms(last - 2).side_on()
         exchange(3, dqkv_ref[:, :width])
-        load_ein.wait()
-        load_eout.wait()
-        x_gather.finish()
-        g_gather.finish()
-        xs = x_all[:, :slot_rows, :].reshape(-1, width)
-        parts = x_all[:, slot_rows:, : 2 * LANES].astype(F32).reshape(seq_count * GATE_ROWS, 2 * LANES).T
-        dm = jnp.concatenate(
-            [
-                (g_all[s].astype(F32) * sum(parts[:slot_rows, s * GATE_ROWS + n : s * GATE_ROWS + n + 1] for n in range(3)))
-                for s in range(seq_count)
-            ],
-            axis=0,
-        ).astype(BF16)
-        value, slope = gelu_parts(nn(xs, w_ein[...]))
-        gout_ref[...] = tn(value.astype(BF16), dm)
+        own_terms(last - 4)
+        terms(last - 1).side_on()
+        own_terms(last - 3)
+        terms(last).side_on()
+        own_terms(last - 2)
         chunks[0].back_over_exp()
-        chunks[2].spread()
-        terms(4).side_on()
-        terms(5).side_on()
-        own_terms(2)
+        own_terms(last - 1)
+        wait_bytes(e_exp, enc_exp_sem.at[1])
         total = e_mine[mine].astype(F32)
-        for d, copy in enumerate(enc_over_exp()):
-            copy.wait_recv()
+        for d in range(experts - 1):
             total = total + e_exp[d].astype(F32)
         dekv[...] = total.astype(BF16)
         dekv_local().start()
-        for copy in dekv_over_exp():
-            copy.start()
-        dh = (nt(dm, w_eout[...]) * slope).astype(BF16)
-        gin_out[...] = tn(xs, dh).astype(BF16).reshape(gin_out.shape)
-        own_terms(3)
+        dekv_over_exp()
         multiply(3)
-        chunks[1].spread()
-        own_terms(4)
-        own_terms(5)
+        own_terms(last)
 
         dqkv = dqkv_ref[...]
         exchange(4, dqkv[:, width : 2 * width])
         exchange(5, dqkv[:, 2 * width :])
+        chunks[2].spread()
+
         x = x_ref[...].astype(F32)
         da, dw = rms_back(x, gains_ref[0:1, :], nt(dqkv, w_qkv[...]))
         small_a[0:1, :width] = dw
         dx_ref[...] = dr_ref[...] + da
+        store(dx_ref, dx_hbm)
         heads = 2 * pairs
         table = diag_ref[:, 2 * rows - LANES :]
         totals = total_ref[...]
@@ -1260,70 +1223,79 @@
         by_bucket = lax.dot_general(table, pick, (((1,), (1,)), ((), ())), precision=highest, preferred_element_type=F32)
         small_a[0:8, width : width + LANES] = by_bucket[0:8]
         small_a[0 : heads - 8, width + LANES :] = by_bucket[8:heads]
-        s_pair = send(small_a, small_pair, s1_send.at[0], s1_recv.at[0], {"seq": place.partner})
-
+        s_pair = remote(small_a, small_pair, small_sem.at[0], small_sem.at[1], {"seq": place.partner})
+        s_pair.start()
+
+        x_gather.finish()
+        g_gather.finish()
+        g_gather.drain()
+        parts = x_all[:, slot_rows:, : 2 * LANES].astype(F32).reshape(seq_count * GATE_ROWS, 2 * LANES).T
+        for n in range(seq_count):
+            gate = sum(parts[:slot_rows, n * GATE_ROWS + i : n * GATE_ROWS + i + 1] for i in range(3))
+            g_all[n] = (g_all[n].astype(F32) * gate).astype(BF16)
+        expert_units(0)
         chunks[3].back_over_exp()
         multiply(4)
         multiply(5)
-        for copy in gins():
-            copy.start()
-        gin_in[:, at_hidden] = gin_out[me]
+        chunks[1].spread()
         chunks[0].spread()
         dekv_local().wait()
-        for copy in dekv_over_exp():
-            copy.wait_recv()
+        wait_bytes(e_exp, enc_exp_sem.at[3])
         dekv_gather.start()
         chunks[2].over_seq.relay()
-        chunks[3].spread()
         s_pair.wait_recv()
         small_b[...] = small_a[...] + small_pair[...]
-        s_chip = [
-            send(small_b, small_chip.at[d], s2_send.at[d], s2_recv.at[d], {"seq": device})
-            for d, device in enumerate((place.x, place.y, place.far))
-        ]
+        for d, device in enumerate((place.x, place.y, place.far)):
+            remote(small_b, small_chip.at[d], small_sem.at[2], small_sem.at[3], {"seq": device}).start()
+        expert_units(1)
+        chunks[3].spread()
         chunks[4].back_over_exp()
+        expert_units(2)
         chunks[5].back_over_exp()
         chunks[1].over_seq.relay()
         chunks[2].over_seq.relay_far()
-        genc_ref[...] = nt(dekv[...], w_ckv[...])
-        chunks[4].spread()
-        chunks[5].spread()
         chunks[0].over_seq.relay()
         dekv_gather.relay()
+        chunks[4].spread()
+        genc_ref[...] = nt(dekv[...], w_ckv[...])
+        store(genc_ref, genc_hbm)
+        wait_bytes(small_chip, small_sem.at[3])
+        small_c[...] = small_b[...] + small_chip[0] + small_chip[1] + small_chip[2]
+        for d, peer in enumerate(peers):
+            remote(small_c, small_exp.at[d], small_sem.at[4], small_sem.at[5], {"exp": peer}).start()
+        chunks[5].spread()
+        expert_units(3)
         chunks[1].over_seq.relay_far()
-        total = small_b[...]
-        for d, copy in enumerate(s_chip):
-            copy.wait_recv()
-            total = total + small_chip[d]
-        small_c[...] = total
-        s_exp = [
-            send(small_c, small_exp.at[d], s3_send.at[d], s3_recv.at[d], {"exp": peer}) for d, peer in enumerate(peers)
-        ]
         chunks[3].over_seq.relay()
         chunks[0].over_seq.relay_far()
         dekv_gather.relay_far()
-        for copy in gins():
-            copy.wait_recv()
-        gin_ref[...] = gin_in[...]
         chunks[4].over_seq.relay()
         chunks[5].over_seq.relay()
+        wait_bytes(gin_out, unit_recv.at[0])
+        store(gin_in, gin_hbm)
+        wait_bytes(small_exp, small_sem.at[5])
         total = small_c[...]
-        for d, copy in enumerate(s_exp):
-            copy.wait_recv()
+        for d in range(experts - 1):
             total = total + small_exp[d]
         small_out_ref[...] = total
+        store(small_out_ref, small_hbm)
         for i in (3, 4, 5):
             chunks[i].over_seq.relay_far()
         for chunk in chunks:
             chunk.over_seq.finish()
         dekv_gather.finish()
 
-        for copy in started + enc_over_exp() + dekv_over_exp() + gins():
-            copy.wait_send()
+        for copy in stores:
+            copy.wait()
+        wait_bytes(e_exp, enc_exp_sem.at[0])
+        wait_bytes(e_exp, enc_exp_sem.at[2])
+        wait_bytes(gin_out, unit_send.at[0])
+        s_pair.wait_send()
+        wait_bytes(small_chip, small_sem.at[2])
+        wait_bytes(small_exp, small_sem.at[4])
         for i in range(6):
-            for copy in right_copies(i):
-                copy.wait_send()
-        for each in (gather, o_gather, n2_gather, oc_gather, x_gather, g_gather, dekv_gather, enc_scatter):
+            wait_bytes(turned_ref.at[i, pl.ds(0, (seq_count - 1) * part), :], right_sem.at[i, 0])
+        for each in (gather, o_gather, n2_gather, oc_gather, x_gather, dekv_gather, enc_scatter):
             each.drain()
         for chunk in chunks:
             chunk.drain()
@@ -1335,7 +1307,7 @@
 
     pl.run_scoped(
         backward, bf(2, 4, enc_part, 2 * width), bf(pairs, 2, 4, rows, 2 * LANES), bf(6, part, width), bf(6, width, rows),
-        bf(span + rows, 2 * rows), bf(seq_count, part, own_hidden), bf(width, own_hidden), bf(own_hidden, width),
+        bf(span + rows, 2 * rows), bf(4, part, own_hidden), f32(2 * LANES, own_hidden), bf(2, width, own_hidden), bf(2, own_hidden, width),
     )
 
 
@@ -1369,7 +1341,7 @@
             shape((hidden // seq_count, width), F32), shape((own_enc, width), F32),
         ),
         in_specs=[VMEM, ANY, SMEM, VMEM, VMEM, VMEM, ANY, ANY, ANY, ANY, ANY, VMEM, VMEM, VMEM, ANY, ANY],
-        out_specs=(VMEM, VMEM, ANY, ANY, VMEM, VMEM, VMEM, VMEM),
+        out_specs=(ANY,) * 8,
         scratch_shapes=[
             bf(4, seq_count, rows, width), bf(span, 2 * width), bf(pairs, span, 2 * rows), bf(pairs, enc_rows, 2 * rows),
             bf(enc_rows, 2 * width), bf(*qkv.shape), bf(*so.shape), bf(*cq.shape), bf(*ckv.shape), bf(*co.shape),
@@ -1380,14 +1352,11 @@
             bf(4, enc_part, 2 * width), bf(2, enc_part // 2, 2 * width), bf(2, enc_part, 2 * width),
             bf(experts, own_enc, 2 * width), bf(z, own_enc, 2 * width), bf(own_enc, 2 * width),
             bf(pairs, 4, rows, 2 * LANES), bf(pairs, 2, rows // 2, 2 * LANES), bf(pairs, 2, rows, 2 * LANES),
+            wide, f32(rows, width), f32(hidden // seq_count, width), f32(own_enc, width), f32(*small),
             bf(6, z, *quarter), bf(6, *quarter), bf(6, part, span), bf(part, hidden),
             f32(*small), f32(*small), f32(*small), f32(*small), f32(3, *small), f32(z, *small),
-            dma(10), dma(7)] + [dma(8)] * 12 + [dma(z)] * 8 + [
-            dma(1), dma(1), dma(2), dma(2), dma(2), dma(2), dma(z), dma(z), dma(z), dma(z), dma(8), dma(8),
-            dma(pairs), dma(pairs), dma(pairs, 2), dma(pairs, 2), dma(pairs, 2), dma(pairs, 2),
-            dma(6, z), dma(6, z), dma(6, z), dma(6, z), dma(6, 8), dma(6, 8),
-            dma(6, seq_count - 1), dma(6, seq_count - 1), dma(seq_count - 1), dma(seq_count - 1),
-            dma(1), dma(1), dma(3), dma(3), dma(z), dma(z),
+            dma(12), dma(7), dma(6), dma(6), dma(7), dma(6, 4), dma(4, 2), dma(5), dma(4), dma(pairs, 5), dma(6, 4),
+            dma(6), dma(6, 4), dma(6, 2), dma(1), dma(1), dma(6),
         ],
         compiler_params=pltpu.CompilerParams(collective_id=0, has_side_effects=True, vmem_limit_bytes=63 << 20),
         name="layer",

time: 161 us -> 152 us (0.944)
  Pallas kernels: 159 us -> 151 us
    pallas_call x1, Pallas kernels: 146 us -> 137 us  [layer_call(): pl.pallas_call(functools.partial(layer_kernel, seq_count, capacity), out_...]
where the time goes in v5:
time: 152 us
  Pallas kernels  151 us (99%)
    pallas_call x1, Pallas kernels, layer_call(): pl.pallas_call(functools.partial(layer_kernel, seq_count, capacity), out_...  137 us
    pallas_call x1, Pallas kernels, finish_call(): pl.pallas_call(functools.partial(finish_kernel, experts), out_shape=(shap...  13.8 us

profile of v5, /device:TPU:0, one launch (start us, length us, event | category | flops | bytes accessed | tf_op | source)
XLA Modules:
  0.0 151.5 jit_solution(15886427298142580417)
XLA Ops:
  0.7 136.8 %layer.1 = (bf16[128,768]{1,0:T(8,128)(2,1)}, f32[128,768]{1,0:T(8,128)}, bf16[6,8,96,768]{3,2,1,0:T(8,128)(2,1)}, bf16[8,4,16,1536]{3,2,1,0:T(8,128)(2,1)}, f32...) custom-call(bf16[128,768]{1,0:T(8,128)(2,1)} %bitcast.16, ...), custom_call_target="tpu_custom_call" | custom-call | tf_op jit(solution)/shard_map/layer/pallas_call | solution.py:1336
  137.5 13.8 %finish.1 = (bf16[128,768]{1,0:T(8,128)(2,1)}, f32[128,768]{1,0:T(8,128)}, f32[16,768]{1,0:T(8,128)}, f32[3,768]{1,0:T(4,128)}, f32[768,2304]{1,0:T(8,128)}, /*i...) custom-call(bf16[6,8,96,768]{3,2,1,0:T(8,128)(2,1)} %get-tuple-eleme, ...), custom_call_target="tpu_custom_call" | custom-call | tf_op jit(solution)/shard_map/finish/pallas_call | solution.py:1426

commit v6 on v5

--- a/solution.py
+++ b/solution.py
@@ -853,8 +853,7 @@
         gather.arrived(1, 5)
         project(place.far_chip)
 
-        @pl.loop(0, pairs)
-        def _(p):
+        def attend(p, scores):
             lanes = pair_lanes(p)
             q_both = head_stack(q_ref[:, lanes])
             scores[pl.ds(rows, span), :] = nt(kv_all[:, lanes], q_both) + mask[...]
@@ -869,6 +868,11 @@
             prob[p] = weights
             both = tn(kv_all[:, pair_lanes(pairs + p)], weights)
             left[0, me, :, lanes] = head_unstack(both, rows).astype(BF16)
+
+        @pl.loop(0, pairs, step=2)
+        def _(first):
+            for side in range(2):
+                attend(first + side, scores.at[side])
 
         sent(*g_trip)
 
@@ -888,7 +892,7 @@
         n2_gather.start()
         qc_ref[...] = nn(n2, w_cq[...]).astype(BF16) * jnp.asarray(0.125, BF16)
 
-        @pl.loop(0, pairs)
+        @pl.loop(0, pairs, unroll=2)
         def _(p):
             lanes = pair_lanes(p)
             s = nt(ekv[:, lanes], head_stack(qc_ref[:, lanes]))
@@ -960,7 +964,7 @@
     bf = lambda *n: pltpu.VMEM(n, BF16)
     f32 = lambda *n: pltpu.VMEM(n, F32)
     packed = bf(*g_in.shape)
-    pl.run_scoped(self_attention, f32(span + rows, 2 * rows), f32(span, 2 * rows), bf(enc_rows, width), packed)
+    pl.run_scoped(self_attention, f32(2, span + rows, 2 * rows), f32(span, 2 * rows), bf(enc_rows, width), packed)
     pl.run_scoped(
         rest_forward, bf(*x_in.shape), packed, packed, f32(slot_rows, hidden), bf(width, hidden), bf(hidden, width)
     )
@@ -1067,7 +1071,7 @@
         n2_gather.relay_far()
         x_gather.relay()
 
-        @pl.loop(0, pairs)
+        @pl.loop(0, pairs, unroll=2)
         def _(p):
             lanes, value_lanes = pair_lanes(p), pair_lanes(pairs + p)
             doc_both = head_stack(doc_ref[:, lanes])
@@ -1083,7 +1087,6 @@
             dqc_ref[:, lanes] = (head_unstack(tn(ekv[:, lanes], dc), rows) * 0.125).astype(BF16)
 
         enc_scatter.start()
-        oc_gather.relay_far()
         dqc = dqc_ref[...]
         exchange(1, dqc)
         da, dw = rms_back(r1_ref[...], gains_ref[1:2, :], nt(dqc, w_cq[...]))
@@ -1093,9 +1096,7 @@
         do1 = dr_ref[...].astype(BF16)
         doc_ref[...] = nt(do1, w_so[...]).astype(BF16)
         exchange(0, do1)
-        x_gather.relay_far()
-        oc_gather.finish()
-        multiply(2)
+        oc_gather.relay_far()
         n2_gather.finish()
         o_gather.finish()
 
@@ -1153,13 +1154,22 @@
             def _():
                 own_terms(jnp.maximum(t - 5, 0))
 
+            @pl.when(t == 0)
+            def _():
+                oc_gather.finish()
+                multiply(2)
+
             @pl.when(t == 1)
             def _():
+                x_gather.relay_far()
                 enc_scatter.side_on()
 
             @pl.when(t == 2)
             def _():
                 multiply(1)
+
+            @pl.when(t == 5)
+            def _():
                 chunks[2].back_over_exp()
 
             @pl.when(t == 3)
@@ -1170,7 +1180,6 @@
             def _():
                 e_mine[...] = enc_scatter.total().astype(BF16).reshape(e_mine.shape)
                 enc_over_exp()
-                chunks[1].back_over_exp()
 
 
         last = pairs - 1
@@ -1182,6 +1191,7 @@
         own_terms(last - 3)
         terms(last).side_on()
         own_terms(last - 2)
+        chunks[1].back_over_exp()
         chunks[0].back_over_exp()
         own_terms(last - 1)
         wait_bytes(e_exp, enc_exp_sem.at[1])
@@ -1190,14 +1200,13 @@
             total = total + e_exp[d].astype(F32)
         dekv[...] = total.astype(BF16)
         dekv_local().start()
+        multiply(3)
         dekv_over_exp()
-        multiply(3)
         own_terms(last)
 
         dqkv = dqkv_ref[...]
         exchange(4, dqkv[:, width : 2 * width])
         exchange(5, dqkv[:, 2 * width :])
-        chunks[2].spread()
 
         x = x_ref[...].astype(F32)
         da, dw = rms_back(x, gains_ref[0:1, :], nt(dqkv, w_qkv[...]))
@@ -1237,12 +1246,12 @@
         chunks[3].back_over_exp()
         multiply(4)
         multiply(5)
+        chunks[2].spread()
         chunks[1].spread()
         chunks[0].spread()
         dekv_local().wait()
         wait_bytes(e_exp, enc_exp_sem.at[3])
         dekv_gather.start()
-        chunks[2].over_seq.relay()
         s_pair.wait_recv()
         small_b[...] = small_a[...] + small_pair[...]
         for d, device in enumerate((place.x, place.y, place.far)):
@@ -1252,25 +1261,34 @@
         chunks[4].back_over_exp()
         expert_units(2)
         chunks[5].back_over_exp()
-        chunks[1].over_seq.relay()
-        chunks[2].over_seq.relay_far()
-        chunks[0].over_seq.relay()
-        dekv_gather.relay()
-        chunks[4].spread()
         genc_ref[...] = nt(dekv[...], w_ckv[...])
         store(genc_ref, genc_hbm)
         wait_bytes(small_chip, small_sem.at[3])
         small_c[...] = small_b[...] + small_chip[0] + small_chip[1] + small_chip[2]
         for d, peer in enumerate(peers):
             remote(small_c, small_exp.at[d], small_sem.at[4], small_sem.at[5], {"exp": peer}).start()
+        chunks[4].spread()
+        chunks[2].over_seq.relay()
+        chunks[1].over_seq.relay()
         chunks[5].spread()
+        chunks[0].over_seq.relay()
+        dekv_gather.relay()
+        chunks[3].over_seq.relay()
         expert_units(3)
-        chunks[1].over_seq.relay_far()
-        chunks[3].over_seq.relay()
-        chunks[0].over_seq.relay_far()
-        dekv_gather.relay_far()
+        wait_bytes(e_exp, enc_exp_sem.at[0])
+        wait_bytes(e_exp, enc_exp_sem.at[2])
+        s_pair.wait_send()
+        wait_bytes(small_chip, small_sem.at[2])
+        for i in range(6):
+            wait_bytes(turned_ref.at[i, pl.ds(0, (seq_count - 1) * part), :], right_sem.at[i, 0])
+        for each in (gather, o_gather, n2_gather, oc_gather, x_gather, enc_scatter):
+            each.drain()
+
+        @pl.loop(0, pairs)
+        def _(p):
+            terms(p).drain()
+
         chunks[4].over_seq.relay()
-        chunks[5].over_seq.relay()
         wait_bytes(gin_out, unit_recv.at[0])
         store(gin_in, gin_hbm)
         wait_bytes(small_exp, small_sem.at[5])
@@ -1279,31 +1297,23 @@
             total = total + small_exp[d]
         small_out_ref[...] = total
         store(small_out_ref, small_hbm)
+        chunks[5].over_seq.relay()
+        for i in (2, 1, 0):
+            chunks[i].over_seq.relay_far()
+        dekv_gather.relay_far()
         for i in (3, 4, 5):
             chunks[i].over_seq.relay_far()
         for chunk in chunks:
             chunk.over_seq.finish()
         dekv_gather.finish()
 
+        wait_bytes(gin_out, unit_send.at[0])
+        wait_bytes(small_exp, small_sem.at[4])
+        dekv_gather.drain()
+        for chunk in chunks:
+            chunk.drain()
         for copy in stores:
             copy.wait()
-        wait_bytes(e_exp, enc_exp_sem.at[0])
-        wait_bytes(e_exp, enc_exp_sem.at[2])
-        wait_bytes(gin_out, unit_send.at[0])
-        s_pair.wait_send()
-        wait_bytes(small_chip, small_sem.at[2])
-        wait_bytes(small_exp, small_sem.at[4])
-        for i in range(6):
-            wait_bytes(turned_ref.at[i, pl.ds(0, (seq_count - 1) * part), :], right_sem.at[i, 0])
-        for each in (gather, o_gather, n2_gather, oc_gather, x_gather, dekv_gather, enc_scatter):
-            each.drain()
-        for chunk in chunks:
-            chunk.drain()
-
-        @pl.loop(0, pairs)
-        def _(p):
-            terms(p).drain()
-
 
     pl.run_scoped(
         backward, bf(2, 4, enc_part, 2 * width), bf(pairs, 2, 4, rows, 2 * LANES), bf(6, part, width), bf(6, width, rows),
@@ -1374,7 +1384,7 @@
     ]
     through = ((gout_hbm, gout, gout_out), (dx_hbm, dx, dx_out), (layer_hbm, layer, layer_out), (genc_hbm, genc, genc_out))
     loads += [pltpu.make_async_copy(src, held, load_sem.at[8 + i]) for i, (src, held, _) in enumerate(through)]
-    for load in loads:
+    for load in loads[8:] + loads[6:8] + loads[:6]:
         load.start()
     copies = []
 
@@ -1391,30 +1401,30 @@
     gin[...] = gin_ref[...].astype(F32)
     store(gin, gin_out)
 
-    def turn(i, target, at):
-        loads[i].wait()
-        for block in range(width // LANES):
-            rows = slice(block * LANES, (block + 1) * LANES)
-            target[:, at + block * LANES : at + (block + 1) * LANES] = (
-                weights[i].reshape(seq_count * part, width)[rows, :].astype(F32).T
-            )
-
-    for i, out in enumerate((so_hbm, cq_hbm, co_hbm)):
-        turn(i, squares.at[i], 0)
-        store(squares.at[i], out)
     for i, (_, held, out) in enumerate(through):
         loads[8 + i].wait()
         store(held, out)
-    for i in range(3):
-        at = slice(i * width, (i + 1) * width)
-        turn(3 + i, qkv, i * width)
-        store(qkv.at[:, at], qkv_hbm.at[:, at])
     loads[6].wait()
     loads[7].wait()
     for n in range(2):
         at = slice(n * width, (n + 1) * width)
         ckv[:, at] = tn(enc[...], dekv[...].reshape(enc.shape[0], 2 * width)[:, at])
         store(ckv.at[:, at], ckv_hbm.at[:, at])
+    def turn(i, target, at):
+        loads[i].wait()
+        for block in range(width // LANES):
+            rows = slice(block * LANES, (block + 1) * LANES)
+            target[:, at + block * LANES : at + (block + 1) * LANES] = (
+                weights[i].reshape(seq_count * part, width)[rows, :].T.astype(F32)
+            )
+
+    for i, out in enumerate((so_hbm, cq_hbm, co_hbm)):
+        turn(i, squares.at[i], 0)
+        store(squares.at[i], out)
+    for i in range(3):
+        at = slice(i * width, (i + 1) * width)
+        turn(3 + i, qkv, i * width)
+        store(qkv.at[:, at], qkv_hbm.at[:, at])
     for copy in copies:
         copy.wait()
 

time: 152 us -> 150 us (0.987); the launches traced: 152 us -> 148 us
  Pallas kernels: 151 us -> 147 us
    pallas_call x1, Pallas kernels: 137 us -> 135 us  [layer_call(): pl.pallas_call(functools.partial(layer_kernel, seq_count, capacity), out_...]
    pallas_call x1, Pallas kernels: 13.8 us -> 12.3 us  [finish_call(): pl.pallas_call(functools.partial(finish_kernel, experts), out_shape=(shap...]
where the time goes in v6:
time: 150 us; the launch traced here: 148 us
  Pallas kernels  147 us (98%)
    pallas_call x1, Pallas kernels, layer_call(): pl.pallas_call(functools.partial(layer_kernel, seq_count, capacity), out_...  135 us
    pallas_call x1, Pallas kernels, finish_call(): pl.pallas_call(functools.partial(finish_kernel, experts), out_shape=(shap...  12.3 us

profile of v6, /device:TPU:0, one launch (start us, length us, event | category | flops | bytes accessed | tf_op | source)
XLA Modules:
  0.0 147.9 jit_solution(6210629898001334327)
XLA Ops:
  0.7 134.8 %layer.1 = (bf16[128,768]{1,0:T(8,128)(2,1)}, f32[128,768]{1,0:T(8,128)}, bf16[6,8,96,768]{3,2,1,0:T(8,128)(2,1)}, bf16[8,4,16,1536]{3,2,1,0:T(8,128)(2,1)}, f32...) custom-call(bf16[128,768]{1,0:T(8,128)(2,1)} %bitcast.16, ...), custom_call_target="tpu_custom_call" | custom-call | tf_op jit(solution)/shard_map/layer/pallas_call | solution.py:1346
  135.4 12.3 %finish.1 = (bf16[128,768]{1,0:T(8,128)(2,1)}, f32[128,768]{1,0:T(8,128)}, f32[16,768]{1,0:T(8,128)}, f32[3,768]{1,0:T(4,128)}, f32[768,2304]{1,0:T(8,128)}, /*i...) custom-call(bf16[6,8,96,768]{3,2,1,0:T(8,128)(2,1)} %get-tuple-eleme, ...), custom_call_target="tpu_custom_call" | custom-call | tf_op jit(solution)/shard_map/finish/pallas_call | solution.py:1436

commit v7 on v6

--- a/solution.py
+++ b/solution.py
@@ -714,10 +714,71 @@
         wait_bytes(self.slots, self.sems.at[3])
         self.over_seq.start()
 
+    def relay(self):
+        self.over_seq.relay()
+
+    def relay_far(self):
+        self.over_seq.relay_far()
+
     def drain(self):
         wait_bytes(self.slots, self.sems.at[0])
         wait_bytes(self.slots, self.sems.at[2])
         self.over_seq.drain()
+
+
+class WideChunk(Chunk):
+    def quarter(self, device, first=0, rows=None):
+        at, lanes = self.quarters[0]
+        rows = at.size if rows is None else rows
+        return self.every.at[device, pl.ds(pl.multiple_of(at.start + first, 16), rows), lanes]
+
+    def same_core(self):
+        return [c * 2 + self.place.core for c in range(4)]
+
+    def send_quarter(self, block, sem, device):
+        remote(block, block, self.sems.at[4], self.over_seq.recv_sems.at[sem], {"seq": device}).start()
+
+    def back_over_exp(self):
+        total = self.src[self.quarters[0]].astype(F32)
+        wait_bytes(self.slots, self.sems.at[1])
+        for d in range(len(self.peers)):
+            total = total + self.slots[d].astype(F32)
+        self.own[...] = total.astype(BF16)
+        self.local_copy().start()
+
+    def spread(self):
+        place = self.place
+        self.local_copy().wait()
+        for sem, device in enumerate((place.x, place.y)):
+            self.send_quarter(self.quarter(place.me), sem, device)
+
+    def relay(self):
+        place = self.place
+        rows = self.quarters[0][0].size
+        half = -(-rows // 32) * 16
+        wait_bytes(self.own, self.over_seq.recv_sems.at[0])
+        self.send_quarter(self.quarter(place.x, 0, half), 2, place.y)
+        wait_bytes(self.own, self.over_seq.recv_sems.at[1])
+        self.send_quarter(self.quarter(place.y, half, rows - half), 2, place.x)
+
+    def cross(self):
+        wait_bytes(self.own, self.over_seq.recv_sems.at[2])
+        for peer in self.peers:
+            for device in self.same_core():
+                block = self.quarter(device)
+                remote(block, block, self.sems.at[2], self.sems.at[3], {"exp": peer}).start()
+
+    def relay_far(self):
+        wait_bytes(self.every.at[pl.ds(0, len(self.peers))], self.sems.at[3])
+        for device in self.same_core():
+            block = self.every.at[device]
+            remote(block, block, self.over_seq.send_sem, self.over_seq.recv_sems.at[3], {"seq": self.place.partner}).start()
+
+    def drain(self):
+        wait_bytes(self.slots, self.sems.at[0])
+        wait_bytes(self.every.at[pl.ds(0, len(self.peers))], self.sems.at[2])
+        wait_bytes(self.slots, self.sems.at[4])
+        wait_bytes(self.every.at[pl.ds(0, 4)], self.over_seq.send_sem)
 
 
 def layer_kernel(
@@ -1010,8 +1071,9 @@
         for copy in expert_loads(0) + expert_loads(1):
             copy.start()
         enc_scatter = Scatter(place, e_out, e_pair, e_turn, e_side, e_turn.shape[1], enc_sem)
+        wide = (2,)
         chunks = [
-            Chunk(
+            (WideChunk if i in wide else Chunk)(
                 place, quarters, peers, c_src.at[i], c_slots.at[i], c_own.at[i], weights_hbm.at[i], chunk_sem.at[i],
                 (chunk_send.at[i], chunk_recv.at[i]), local_sem.at[i],
             )
@@ -1168,18 +1230,16 @@
             def _():
                 multiply(1)
 
-            @pl.when(t == 5)
-            def _():
-                chunks[2].back_over_exp()
-
             @pl.when(t == 3)
             def _():
                 multiply(0)
+                chunks[2].back_over_exp()
 
             @pl.when(t == 4)
             def _():
                 e_mine[...] = enc_scatter.total().astype(BF16).reshape(e_mine.shape)
                 enc_over_exp()
+                chunks[1].back_over_exp()
 
 
         last = pairs - 1
@@ -1191,7 +1251,7 @@
         own_terms(last - 3)
         terms(last).side_on()
         own_terms(last - 2)
-        chunks[1].back_over_exp()
+        multiply(3)
         chunks[0].back_over_exp()
         own_terms(last - 1)
         wait_bytes(e_exp, enc_exp_sem.at[1])
@@ -1200,13 +1260,14 @@
             total = total + e_exp[d].astype(F32)
         dekv[...] = total.astype(BF16)
         dekv_local().start()
-        multiply(3)
         dekv_over_exp()
         own_terms(last)
 
         dqkv = dqkv_ref[...]
         exchange(4, dqkv[:, width : 2 * width])
         exchange(5, dqkv[:, 2 * width :])
+        chunks[2].spread()
+        chunks[1].spread()
 
         x = x_ref[...].astype(F32)
         da, dw = rms_back(x, gains_ref[0:1, :], nt(dqkv, w_qkv[...]))
@@ -1243,37 +1304,36 @@
             gate = sum(parts[:slot_rows, n * GATE_ROWS + i : n * GATE_ROWS + i + 1] for i in range(3))
             g_all[n] = (g_all[n].astype(F32) * gate).astype(BF16)
         expert_units(0)
-        chunks[3].back_over_exp()
         multiply(4)
         multiply(5)
-        chunks[2].spread()
-        chunks[1].spread()
-        chunks[0].spread()
-        dekv_local().wait()
-        wait_bytes(e_exp, enc_exp_sem.at[3])
-        dekv_gather.start()
+        chunks[3].back_over_exp()
         s_pair.wait_recv()
         small_b[...] = small_a[...] + small_pair[...]
         for d, device in enumerate((place.x, place.y, place.far)):
             remote(small_b, small_chip.at[d], small_sem.at[2], small_sem.at[3], {"seq": device}).start()
         expert_units(1)
-        chunks[3].spread()
+        chunks[2].relay()
+        chunks[0].spread()
+        dekv_local().wait()
+        wait_bytes(e_exp, enc_exp_sem.at[3])
+        dekv_gather.start()
         chunks[4].back_over_exp()
-        expert_units(2)
+        chunks[1].relay()
         chunks[5].back_over_exp()
+        chunks[0].relay()
         genc_ref[...] = nt(dekv[...], w_ckv[...])
         store(genc_ref, genc_hbm)
         wait_bytes(small_chip, small_sem.at[3])
         small_c[...] = small_b[...] + small_chip[0] + small_chip[1] + small_chip[2]
         for d, peer in enumerate(peers):
             remote(small_c, small_exp.at[d], small_sem.at[4], small_sem.at[5], {"exp": peer}).start()
+        chunks[2].cross()
+        expert_units(2)
+        dekv_gather.relay()
+        chunks[3].spread()
         chunks[4].spread()
-        chunks[2].over_seq.relay()
-        chunks[1].over_seq.relay()
         chunks[5].spread()
-        chunks[0].over_seq.relay()
-        dekv_gather.relay()
-        chunks[3].over_seq.relay()
+        chunks[3].relay()
         expert_units(3)
         wait_bytes(e_exp, enc_exp_sem.at[0])
         wait_bytes(e_exp, enc_exp_sem.at[2])
@@ -1288,7 +1348,8 @@
         def _(p):
             terms(p).drain()
 
-        chunks[4].over_seq.relay()
+        chunks[4].relay()
+        chunks[5].relay()
         wait_bytes(gin_out, unit_recv.at[0])
         store(gin_in, gin_hbm)
         wait_bytes(small_exp, small_sem.at[5])
@@ -1297,12 +1358,11 @@
             total = total + small_exp[d]
         small_out_ref[...] = total
         store(small_out_ref, small_hbm)
-        chunks[5].over_seq.relay()
-        for i in (2, 1, 0):
-            chunks[i].over_seq.relay_far()
+        for i in (1, 0):
+            chunks[i].relay_far()
         dekv_gather.relay_far()
-        for i in (3, 4, 5):
-            chunks[i].over_seq.relay_far()
+        for i in (3, 2, 4, 5):
+            chunks[i].relay_far()
         for chunk in chunks:
             chunk.over_seq.finish()
         dekv_gather.finish()
@@ -1365,7 +1425,7 @@
             wide, f32(rows, width), f32(hidden // seq_count, width), f32(own_enc, width), f32(*small),
             bf(6, z, *quarter), bf(6, *quarter), bf(6, part, span), bf(part, hidden),
             f32(*small), f32(*small), f32(*small), f32(*small), f32(3, *small), f32(z, *small),
-            dma(12), dma(7), dma(6), dma(6), dma(7), dma(6, 4), dma(4, 2), dma(5), dma(4), dma(pairs, 5), dma(6, 4),
+            dma(12), dma(7), dma(6), dma(6), dma(7), dma(6, 4), dma(4, 2), dma(5), dma(4), dma(pairs, 5), dma(6, 5),
             dma(6), dma(6, 4), dma(6, 2), dma(1), dma(1), dma(6),
         ],
         compiler_params=pltpu.CompilerParams(collective_id=0, has_side_effects=True, vmem_limit_bytes=63 << 20),

time: 150 us -> 149 us (level); the launches traced: 148 us -> 148 us
  no operation moved by 1% of the time
where the time goes in v7:
time: 149 us; the launch traced here: 148 us
  Pallas kernels  148 us (99%)
    pallas_call x1, Pallas kernels, layer_call(): pl.pallas_call(functools.partial(layer_kernel, seq_count, capacity), out_...  135 us
    pallas_call x1, Pallas kernels, finish_call(): pl.pallas_call(functools.partial(finish_kernel, experts), out_shape=(shap...  12.3 us

profile of v7, /device:TPU:0, one launch (start us, length us, event | category | flops | bytes accessed | tf_op | source)
XLA Modules:
  0.0 148.4 jit_solution(6288174551288363278)
XLA Ops:
  0.7 135.3 %layer.1 = (bf16[128,768]{1,0:T(8,128)(2,1)}, f32[128,768]{1,0:T(8,128)}, bf16[6,8,96,768]{3,2,1,0:T(8,128)(2,1)}, bf16[8,4,16,1536]{3,2,1,0:T(8,128)(2,1)}, f32...) custom-call(bf16[128,768]{1,0:T(8,128)(2,1)} %bitcast.16, ...), custom_call_target="tpu_custom_call" | custom-call | tf_op jit(solution)/shard_map/layer/pallas_call | solution.py:1406
  136.0 12.3 %finish.1 = (bf16[128,768]{1,0:T(8,128)(2,1)}, f32[128,768]{1,0:T(8,128)}, f32[16,768]{1,0:T(8,128)}, f32[3,768]{1,0:T(4,128)}, f32[768,2304]{1,0:T(8,128)}, /*i...) custom-call(bf16[6,8,96,768]{3,2,1,0:T(8,128)(2,1)} %get-tuple-eleme, ...), custom_call_target="tpu_custom_call" | custom-call | tf_op jit(solution)/shard_map/finish/pallas_call | solution.py:1496
